TPU v7x, 32 devices: a whole 2x2x4 slice. The times are simulated.
32 devices in a mesh: rep: 16 (over z, x, core), fsdp: 2 (over y).
Axes of the slice: x: 2, y: 2, z: 4, core: 2. Of those that a mesh axis runs over, the one named last changes fastest.
Arguments:
- tokens: bfloat16 [16, 1024, 4096], P('rep', 'fsdp'), may hold values from -6 to 6
- cotangent: bfloat16 [16, 1024, 512], P('rep', 'fsdp'), may hold values from -6 to 6
- doc_ids: int32 [16, 1024], P('rep', 'fsdp'), may hold values from 0 to 7, never falling along the last dimension, each value on 1 to 256 neighbouring positions
- pseudo_grads: float32 [16, 4096, 512], P('rep', 'fsdp'), may hold values from -2 to 2
- master: float32 [2, 2048, 512], P('fsdp', 'rep'), may hold values from -0.09375 to 0.09375
- momentum: float32 [2, 2048, 512], P('fsdp', 'rep'), may hold values from -0.15625 to 0.15625
Outputs:
- new_master: float32 [2, 2048, 512], P('fsdp', 'rep')
- new_momentum: float32 [2, 2048, 512], P('fsdp', 'rep')
- keys: bfloat16 [16, 1024, 512], P('rep', 'fsdp')
- weight_grad: bfloat16 [16, 4096, 512], P('rep', 'fsdp')
Inputs may be any that keep to these rules, and one draw needn't show every extreme that they name: `doc_ids`: along each row the numbers never fall; each document has 1 to 256 tokens, and some document has exactly that many.
All inputs are finite; a program needn't handle non-finite values.
Results may differ from a plain program's by a relative error of at most 0.005.
Values may be sent and summed in bfloat16 or wider, within the bound.
No kernel may reach another device: no remote copies, remote signals or barrier semaphores. Data moves between devices by JAX's collectives and lax.ppermute only.
A program may use at most 64 MiB of HBM per device.

v0:
```python
import jax
import jax.numpy as jnp
from jax import lax
from jax.sharding import PartitionSpec as P

HEAD = 128


def passed_along(value, axis, steps):
    count = lax.axis_size(axis)
    leading, last = (max(0, -steps), min(count, count - steps))
    return lax.ppermute(value, axis, [(source, source + steps) for source in range(leading, last)])


def rotate(values, positions, sign):
    count = values.shape[0]
    heads = values.reshape(count, -1, HEAD)
    freqs = 500000.0 ** (-jnp.arange(HEAD // 2, dtype=jnp.float32) / (HEAD // 2))
    angles = positions.astype(jnp.float32)[:, None] * freqs[None, :]
    cosine = jnp.cos(angles)[:, None, :]
    sine = sign * jnp.sin(angles)[:, None, :]
    first = heads[..., : HEAD // 2]
    second = heads[..., HEAD // 2 :]
    turned = jnp.concatenate(
        [first * cosine - second * sine, second * cosine + first * sine], axis=-1
    )
    return turned.reshape(count, -1)


def local(tokens, cotangent, doc_ids, pseudo_grads, master, momentum):
    rep_count = lax.axis_size("rep")
    pair_count = lax.axis_size("fsdp")
    summed = lax.psum_scatter(pseudo_grads, "rep", scatter_dimension=1, tiled=True)
    outer_delta = summed / rep_count
    new_momentum = 0.9 * momentum + outer_delta
    new_master = master - 0.7 * (outer_delta + 0.9 * new_momentum)
    shard_weights = new_master.astype(jnp.bfloat16)
    features = tokens[0]
    width = features.shape[1]
    half_rows = width // pair_count
    key_cols = shard_weights.shape[2]
    halves = lax.all_gather(shard_weights, "rep", axis=1, tiled=True)
    piece = lax.all_gather(halves, "fsdp", axis=0, tiled=True)
    blocks = piece.shape[0]
    columns = features
    flat_piece = piece.reshape(blocks * half_rows, key_cols)
    projected = jnp.dot(columns, flat_piece, preferred_element_type=jnp.float32)
    documents = doc_ids[0]
    count = documents.shape[0]
    first_index = lax.axis_index("fsdp") * count
    places = first_index + jnp.arange(count, dtype=jnp.int32)
    changed = jnp.concatenate([jnp.ones((1,), dtype=bool), documents[1:] != documents[:-1]])
    local_start = lax.cummax(jnp.where(changed, places, 0), axis=0)
    boundary = passed_along(jnp.stack([documents[-1], local_start[-1]]), "fsdp", 1)
    carried = (local_start == first_index) & (documents[0] == boundary[0])
    starts = jnp.where(carried, boundary[1], local_start)
    positions = places - starts
    keys = rotate(projected, positions, 1.0).astype(jnp.bfloat16)
    rotated = rotate(cotangent[0].astype(jnp.float32), positions, -1.0).astype(jnp.bfloat16)
    columns = features
    grads = lax.psum_scatter(
        lax.dot_general(
            columns, rotated, (((0,), (0,)), ((), ())), preferred_element_type=jnp.float32
        ),
        "fsdp",
        scatter_dimension=0,
        tiled=True,
    )
    return (new_master, new_momentum, keys[None], grads.astype(jnp.bfloat16)[None])


def solution(mesh):
    return jax.shard_map(
        local,
        mesh=mesh,
        in_specs=(
            P("rep", "fsdp", None),
            P("rep", "fsdp", None),
            P("rep", "fsdp"),
            P("rep", "fsdp", None),
            P("fsdp", "rep", None),
            P("fsdp", "rep", None),
        ),
        out_specs=(
            P("fsdp", "rep", None),
            P("fsdp", "rep", None),
            P("rep", "fsdp", None),
            P("rep", "fsdp", None),
        ),
        check_vma=False,
    )
```

profile of v0, /device:TPU:0, one launch (start us, length us, event | category | flops | bytes accessed | tf_op | source)
XLA Modules:
  0.0 312.2 jit_solution(8749817201826092367)
XLA Ops:
  7.3 0.7 reduce-scatter.3.cloned.1.call-update
  7.9 0.0 all-gather.3.cloned.1.call-start
  8.0 79.0 %reduce-scatter.3.cloned.1.call-done = f32[1,128,512]{2,1,0:T(8,128)} async-done(((f32[1,2048,512]{2,1,0:T(8,128)}), f32[1,128,512]{2,1,0:T(8,128)}) %reduce-scatter.3.cloned.1.call-update) | async-done | bytes 262160 | tf_op jit(solution)/shard_map/reduce_scatter | solution.py:33
  87.0 1.9 fusion.3
  88.9 0.0 all-gather.5.cloned.1.call-start
  88.9 41.5 %all-gather.3.cloned.1.call-done = bf16[1,2048,512]{2,1,0:T(8,128)(2,1)} async-done(((bf16[1,128,512]{2,1,0:T(8,128)(2,1)}), bf16[1,2048,512]{2,1,0:T(8,128)(2,1)}) %all-gather.3.cloned.1.call-update) | async-done | bytes 2097168 | tf_op jit(solution)/shard_map/all_gather | solution.py:42
  130.5 0.0 reduce-scatter.5.cloned.1.call-start
  130.5 0.1 compare_reduce_fusion
  130.6 0.1 add_select_fusion
  130.7 0.3 reduce-window.9
  131.0 0.1 slice.49
  131.1 0.1 slice_reduce_fusion
  131.3 0.1 maximum_bitcast_fusion
  131.3 0.6 slice.54
  131.9 0.6 fusion.4
  132.5 1.4 pad_add_fusion
  133.9 3.4 %collective-permute-start = (s32[2]{0:T(128)S(1)}, s32[2]{0:T(128)S(1)}, u32[]{:S(2)}, u32[]{:S(2)}) collective-permute-start(s32[2]{0:T(128)S(1)} %pad_add_fusion), channel_id=1, source_target_pairs={{0,1},{2,3},{4,5},{6,7},{8,9},{10,11},{12,13},{14,15},{16,17},{18,... | collective-permute-start | bytes 32 | tf_op jit(solution)/shard_map/ppermute | solution.py:12
  137.3 0.2 copy.23
  137.5 1.0 collective-permute-done
  138.5 0.6 fusion.5
  140.4 0.6 subtract_convert_fusion.2
  141.1 0.5 broadcast_multiply_fusion
  141.6 46.0 %all-gather.5.cloned.1.call-done = bf16[2,2048,512]{2,1,0:T(8,128)(2,1)} async-done(((bf16[1,2048,512]{2,1,0:T(8,128)(2,1)}), bf16[2,2048,512]{2,1,0:T(8,128)(2,1)}) %all-gather.5.cloned.1.call-update) | async-done | bytes 4194320 | tf_op jit(solution)/shard_map/all_gather | solution.py:43
  187.6 5.8 %fusion.1 = f32[512,512]{1,0:T(8,128)S(1)} fusion(bf16[4096,512]{1,0:T(8,128)(2,1)} %bitcast.32, bf16[1,512,4096]{2,1,0:T(8,128)(2,1)} %param.6), kind=kOutput, calls=%fused_computation.2 | convolution fusion | flops 2147483648 | bytes 9437184 | tf_op jit(solution)/shard_map/dot_general | solution.py:47
  193.5 0.4 subtract_convert_fusion
  193.9 0.1 pad_maximum_fusion
  193.9 1.7 copy-done
  195.7 5.6 %convolution_bitcast_fusion = f32[4096,512]{0,1:T(8,128)} fusion(bf16[512,512]{0,1:T(8,128)(2,1)S(1)} %bitcast.29, bf16[1,512,4096]{2,1,0:T(8,128)(2,1)S(1)} %copy-done), kind=kOutput, calls=%fused_computation | convolution fusion | flops 2147483648 | bytes 13107200 | tf_op jit(solution)/shard_map/dot_general | solution.py:62
  201.3 1.0 copy.22
  202.3 98.4 %reduce-scatter.5.cloned.1.call-done = f32[2048,512]{0,1:T(8,128)} async-done(((f32[4096,512]{0,1:T(8,128)}), f32[2048,512]{0,1:T(8,128)}) %reduce-scatter.5.cloned.1.call-update) | async-done | bytes 4194320 | tf_op jit(solution)/shard_map/reduce_scatter | solution.py:61
  300.7 2.5 convert_bitcast_fusion
  303.2 2.5 copy.21
  (15 shorter events, 0.2 us)
Async XLA Ops:
  7.2 79.8 %copy-start.3 = (f32[1,128,512]{2,1,0:T(8,128)S(1)}, f32[1,128,512]{2,1,0:T(8,128)}, u32[]{:S(2)}) copy-start(f32[1,128,512]{2,1,0:T(8,128)} %param.11) | copy-start | bytes 786436
  7.2 79.8 %copy-start.2 = (f32[1,128,512]{2,1,0:T(8,128)S(1)}, f32[1,128,512]{2,1,0:T(8,128)}, u32[]{:S(2)}) copy-start(f32[1,128,512]{2,1,0:T(8,128)} %param.10) | copy-start | bytes 786436
  7.2 123.4 %copy-start.4 = (s32[1,512]{1,0:T(1,128)S(1)}, s32[1,512]{1,0:T(1,128)}, u32[]{:S(2)}) copy-start(s32[1,512]{1,0:T(1,128)} %param.8) | copy-start | bytes 6148
  7.2 130.1 %copy-start.1 = (bf16[1,512,512]{2,1,0:T(8,128)(2,1)S(1)}, bf16[1,512,512]{2,1,0:T(8,128)(2,1)}, u32[]{:S(2)}) copy-start(bf16[1,512,512]{2,1,0:T(8,128)(2,1)} %param.7) | copy-start | bytes 1572868
  7.2 79.8 %reduce-scatter.3.cloned.1.call-start = ((), (), s32[]{:S(2)}) async-start(), calls=%async_computation.2 | async-start | bytes 4456448 | tf_op jit(solution)/shard_map/reduce_scatter | solution.py:33
  7.9 122.5 %all-gather.3.cloned.1.call-start = ((), (), s32[]{:S(2)}) async-start(), calls=%async_computation.3 | async-start | bytes 2228224 | tf_op jit(solution)/shard_map/all_gather | solution.py:42
  88.9 98.8 %all-gather.5.cloned.1.call-start = ((), (), s32[]{:S(2)}) async-start(), calls=%async_computation.4 | async-start | bytes 6291456 | tf_op jit(solution)/shard_map/all_gather | solution.py:43
  130.5 170.2 %reduce-scatter.5.cloned.1.call-start = ((), (), s32[]{:S(2)}) async-start(), calls=%async_computation.5 | async-start | bytes 12582912 | tf_op jit(solution)/shard_map/reduce_scatter | solution.py:61
  133.9 4.7 %collective-permute-start = (s32[2]{0:T(128)S(1)}, s32[2]{0:T(128)S(1)}, u32[]{:S(2)}, u32[]{:S(2)}) collective-permute-start(s32[2]{0:T(128)S(1)} %pad_add_fusion), channel_id=1, source_target_pairs={{0,1},{2,3},{4,5},{6,7},{8,9},{10,11},{12,13},{14,15},{16,17},{18,... | collective-permute-start | bytes 32 | tf_op jit(solution)/shard_map/ppermute | solution.py:12
  193.5 2.2 copy-start
Sparse Core Ops, SparseCore 0:
  11.9 75.0 reduce-scatter.2
  89.9 40.4 all-gather.2
  132.1 55.5 all-gather.4
  201.4 99.2 reduce-scatter.4
where the time goes:
time: 312 us
  waiting for transfers between devices  267 us (86%)
  between operations  15.2 us (5%)
  matrix products  11.4 us (4%)
  other arithmetic  7.94 us (3%)
  local copies, waits for them, and re-layouts  7.45 us (2%)
  starting transfers between devices  3.52 us (1%)
    reduce_scatter x1, waiting for transfers between devices, local(): lax.psum_scatter(lax.dot_general(columns, rotated, (((0,), (0,)), ((), ()...  98.4 us
    reduce_scatter x1, waiting for transfers between devices, local(): lax.psum_scatter(pseudo_grads, 'rep', scatter_dimension=1, tiled=True)  79 us
    all_gather x1, waiting for transfers between devices, local(): piece = lax.all_gather(halves, 'fsdp', axis=0, tiled=True)  46 us
    all_gather x1, waiting for transfers between devices, local(): halves = lax.all_gather(shard_weights, 'rep', axis=1, tiled=True)  41.5 us
  transfers between devices with their start and end apart: 5, of which 5 were waited for; matrix products, arithmetic and copies ran while one was open for 2% of the time, Pallas kernels for 0%

commit v1 on v0

v1 whole, which is shorter than its diff:
```python
import math

import jax
import jax.numpy as jnp
from jax import lax
from jax.sharding import PartitionSpec as P

HEAD = 128
LINK = jnp.bfloat16


def factors_of(count):
    parts = []
    for size in (2, 2, 4):
        if count % size == 0 and count > 1:
            parts.append(size)
            count //= size
    if count > 1:
        parts.append(count)
    return parts


def shift_pairs(count, stride, size, step):
    pairs = []
    for source in range(count):
        part = source // stride % size
        pairs.append((source, source + ((part + step) % size - part) * stride))
    return pairs


def picked(value, index, axis):
    return lax.dynamic_index_in_dim(value, index, axis, keepdims=False)


def tables(positions):
    freqs = 500000.0 ** (-jnp.arange(HEAD // 2, dtype=jnp.float32) / (HEAD // 2))
    angles = positions.astype(jnp.float32)[:, None] * freqs[None, :]
    return jnp.cos(angles)[:, None, :], jnp.sin(angles)[:, None, :]


def rotate(values, cosine, sine):
    count = values.shape[0]
    heads = values.reshape(count, -1, HEAD)
    first = heads[..., : HEAD // 2]
    second = heads[..., HEAD // 2 :]
    turned = jnp.concatenate(
        [first * cosine - second * sine, second * cosine + first * sine], axis=-1
    )
    return turned.reshape(count, -1)


def local(tokens, cotangent, doc_ids, pseudo_grads, master, momentum):
    reps = lax.axis_size("rep")
    pair = lax.axis_size("fsdp")
    rep = lax.axis_index("rep")
    side = lax.axis_index("fsdp")
    parts = factors_of(reps)
    band, columns = master.shape[1:]
    features = tokens[0]
    count, width = features.shape
    depth = width // pair

    strides = [math.prod(parts[:i]) for i in range(len(parts))]
    places = [rep // stride % size for stride, size in zip(strides, parts)]
    terms = [pseudo_grads[0].reshape(tuple(reversed(parts)) + (band, columns))]
    for level, (stride, size, place) in enumerate(zip(strides, parts, places)):
        axis = len(parts) - 1 - level
        kind = jnp.float32 if level == 0 else LINK
        received = []
        for step in range(1, size):
            chosen = sum(picked(t, (place + step) % size, axis).astype(jnp.float32) for t in terms)
            received.append(
                lax.ppermute(chosen.astype(kind), "rep", shift_pairs(reps, stride, size, step))
            )
        terms = [picked(t, place, axis) for t in terms] + received

    documents = doc_ids[0]
    halves = {0: (picked(features.reshape(count, pair, depth), side, 1), cotangent[0], documents)}
    for step in range(1, pair):
        pairs = shift_pairs(pair, 1, pair, step)
        wanted = picked(features.reshape(count, pair, depth), (side + step) % pair, 1)
        halves[(pair - step) % pair] = (
            lax.ppermute(wanted, "fsdp", pairs),
            lax.ppermute(cotangent[0], "fsdp", pairs),
            lax.ppermute(documents, "fsdp", pairs),
        )

    outer_delta = sum(t.astype(jnp.float32) for t in terms) / reps
    new_momentum = 0.9 * momentum[0] + outer_delta
    new_master = master[0] - 0.7 * (outer_delta + 0.9 * new_momentum)

    held = new_master.astype(LINK)[None]
    for stride, size, place in reversed(list(zip(strides, parts, places))):
        pieces = [held] + [
            lax.ppermute(held, "rep", shift_pairs(reps, stride, size, size - step))
            for step in range(1, size)
        ]
        joined = jnp.stack(pieces, axis=1)
        rolled = jnp.concatenate([joined, joined[:, : size - 1]], axis=1)
        held = lax.dynamic_slice_in_dim(rolled, (size - place) % size, size, axis=1)
        held = held.reshape((-1, band, columns))
    weights = held.reshape(depth, columns)

    all_documents = jnp.concatenate([half[2] for half in halves.values()])
    grads = jnp.zeros((depth, columns), jnp.float32)
    turns = {}
    for step, (part, upstream, docs) in halves.items():
        at = (side + step) % pair * count + jnp.arange(count, dtype=jnp.int32)
        starts = jnp.sum((all_documents[None, :] < docs[:, None]).astype(jnp.int32), axis=1)
        turns[step] = tables(at - starts)
        cosine, sine = turns[step]
        rotated = rotate(upstream.astype(jnp.float32), cosine, -sine).astype(jnp.bfloat16)
        grads = grads + lax.dot_general(
            part, rotated, (((0,), (0,)), ((), ())), preferred_element_type=jnp.float32
        )

    projected = jnp.float32(0)
    for step in range(pair - 1, -1, -1):
        product = jnp.dot(halves[step][0], weights, preferred_element_type=jnp.float32)
        if step:
            product = lax.ppermute(
                product.astype(LINK), "fsdp", shift_pairs(pair, 1, pair, step)
            ).astype(jnp.float32)
        projected = projected + product
    keys = rotate(projected, *turns[0]).astype(jnp.bfloat16)
    return (
        new_master[None],
        new_momentum[None],
        keys[None],
        grads.astype(jnp.bfloat16)[None],
    )


def solution(mesh):
    return jax.shard_map(
        local,
        mesh=mesh,
        in_specs=(
            P("rep", "fsdp", None),
            P("rep", "fsdp", None),
            P("rep", "fsdp"),
            P("rep", "fsdp", None),
            P("fsdp", "rep", None),
            P("fsdp", "rep", None),
        ),
        out_specs=(
            P("fsdp", "rep", None),
            P("fsdp", "rep", None),
            P("rep", "fsdp", None),
            P("rep", "fsdp", None),
        ),
        check_vma=False,
    )
```

time: 312 us -> 129 us (0.41)
  waiting for transfers between devices: 267 us -> 56.9 us
  starting transfers between devices: 3.52 us -> 20.9 us
  between operations: 15.2 us -> 0.95 us
  other arithmetic: 7.94 us -> 20.2 us
  local copies, waits for them, and re-layouts: 7.45 us -> 17.2 us
    reduce_scatter x2 -> x0, waiting for transfers between devices: 177 us -> none  [the longest x1 98.4 us: local(): lax.psum_scatter(lax.dot_general(columns, rotated, (((0,), (0,)), ((), ()...]
    all_gather x2 -> x0, waiting for transfers between devices: 87.5 us -> none  [the longest x1 46 us: local(): piece = lax.all_gather(halves, 'fsdp', axis=0, tiled=True)]
    ppermute x1 -> x14, waiting for transfers between devices: 1.04 us -> 56.9 us  [the longest x5 23.2 us: local(): lax.ppermute(held, 'rep', shift_pairs(reps, stride, size, size - step))]
    ppermute x1 -> x14, starting transfers between devices: 3.37 us -> 20.9 us  [the longest x5 9.14 us: local(): lax.ppermute(chosen.astype(kind), 'rep', shift_pairs(reps, stride, size,...]
    dynamic_slice x0 -> x3, local copies, waits for them, and re-layouts: none -> 4.39 us  [the longest x2 4.21 us: picked(): return lax.dynamic_index_in_dim(value, index, axis, keepdims=False)]
    cos x0 -> x1, other arithmetic: none -> 3.19 us  [tables(): return (jnp.cos(angles)[:, None, :], jnp.sin(angles)[:, None, :])]
    unnamed x11 -> x31, local copies, waits for them, and re-layouts: 4.25 us -> 6.56 us
    dot_general x2 -> x4, matrix products: 11.4 us -> 12.8 us  [the longest x2 8.65 us: local(): lax.dot_general(part, rotated, (((0,), (0,)), ((), ())), preferred_elemen...]
  transfers between devices with their start and end apart: 5 -> 14, of which waited for: 5 -> 9; matrix products, arithmetic and copies ran while one was open for 2% -> 19% of each run, Pallas kernels for 0% -> 0%
where the time goes in v1:
time: 129 us
  waiting for transfers between devices  56.9 us (44%)
  starting transfers between devices  20.9 us (16%)
  other arithmetic  20.2 us (16%)
  local copies, waits for them, and re-layouts  17.2 us (13%)
  matrix products  12.8 us (10%)
    ppermute x5, waiting for transfers between devices, local(): lax.ppermute(held, 'rep', shift_pairs(reps, stride, size, size - step))  23.2 us
    ppermute x1, waiting for transfers between devices, local(): lax.ppermute(documents, 'fsdp', pairs)  11.1 us
    ppermute x5, waiting for transfers between devices, local(): lax.ppermute(chosen.astype(kind), 'rep', shift_pairs(reps, stride, size,...  11 us
    ppermute x5, starting transfers between devices, local(): lax.ppermute(chosen.astype(kind), 'rep', shift_pairs(reps, stride, size,...  9.14 us
    dot_general x2, matrix products, local(): lax.dot_general(part, rotated, (((0,), (0,)), ((), ())), preferred_elemen...  8.65 us
    ppermute x1, waiting for transfers between devices, local(): lax.ppermute(product.astype(LINK), 'fsdp', shift_pairs(pair, 1, pair, step))  6.71 us
    unnamed x31, local copies, waits for them, and re-layouts  6.56 us
    ppermute x5, starting transfers between devices, local(): lax.ppermute(held, 'rep', shift_pairs(reps, stride, size, size - step))  6.52 us
  transfers between devices with their start and end apart: 14, of which 9 were waited for; matrix products, arithmetic and copies ran while one was open for 19% of the time, Pallas kernels for 0%

profile of v1, /device:TPU:0, one launch (start us, length us, event | category | flops | bytes accessed | tf_op | source)
XLA Modules:
  0.0 128.9 jit_solution(11543918238695902053)
XLA Ops:
  0.7 3.1 %dynamic-slice_bitcast_fusion = f32[4,2,128,512]{3,2,1,0:T(8,128)} fusion(f32[4,2,2,128,512]{4,3,2,1,0:T(8,128)} %bitcast.117, s32[]{:T(128)S(6)} %select_n.159), kind=kLoop, calls=%fused_computation.13 | loop fusion | bytes 4194308 | tf_op jit(solution)/shard_map/jit(dynamic_index_in_dim)/squeeze | solution.py:32
  4.2 4.0 %collective-permute-done = f32[4,2,128,512]{3,2,1,0:T(8,128)S(1)} collective-permute-done((f32[4,2,128,512]{3,2,1,0:T(8,128)}, f32[4,2,128,512]{3,2,1,0:T(8,128)S(1)}, u32[]{:S(2)}, u32[]{:S(2)}) %collective-permute-start) | collective-permute-done | bytes 2097184 | tf_op jit(solution)/shard_map/ppermute | solution.py:73
  8.2 2.1 %fusion.11 = bf16[4,128,512]{2,1,0:T(8,128)(2,1)S(1)} fusion(f32[4,2,128,512]{3,2,1,0:T(8,128)S(1)} %collective-permute-done, s32[]{:T(128)S(6)} %select_n.161, f32[4,2,2,128,512]{4,3,2,1,0:T(8,128)} %bitcast.118, s32[]{:T(128)S(6)} %select_n.162, s32[]{:T(128)S(6)} %select_n.157), kind=kLoop, calls=%fused_computation.23 | loop fusion | flops 524288 | bytes 2621452 | tf_op jit(solution)/shard_map/convert_element_type | solution.py:73
  10.3 2.9 %collective-permute-start.1 = (bf16[4,128,512]{2,1,0:T(8,128)(2,1)S(1)}, bf16[4,128,512]{2,1,0:T(8,128)(2,1)S(1)}, u32[]{:S(2)}, u32[]{:S(2)}) collective-permute-start(bf16[4,128,512]{2,1,0:T(8,128)(2,1)S(1)} %fusion.11), channel_id=1, source_target_pairs={{0,4},{2,6},{4,0},{6,2},{8,12},{10,14},{12,8},{14,10},{16,20},{18,... | collective-permute-start | bytes 1572872 | tf_op jit(solution)/shard_map/ppermute | solution.py:73
  13.3 6.5 %copy.17 = bf16[1,512,4096]{1,2,0:T(8,128)(2,1)} copy(bf16[1,512,4096]{2,1,0:T(8,128)(2,1)} %param.6) | data formatting | bytes 8388608 | tf_op args[0]
  19.7 5.8 %collective-permute-done.1 = bf16[4,128,512]{2,1,0:T(8,128)(2,1)S(1)} collective-permute-done((bf16[4,128,512]{2,1,0:T(8,128)(2,1)S(1)}, bf16[4,128,512]{2,1,0:T(8,128)(2,1)S(1)}, u32[]{:S(2)}, u32[]{:S(2)}) %collective-permute-start.1) | collective-permute-done | bytes 524320 | tf_op jit(solution)/shard_map/ppermute | solution.py:73
  25.5 2.0 %fusion.19 = (bf16[128,512]{1,0:T(8,128)(2,1)}, bf16[128,512]{1,0:T(8,128)(2,1)S(1)}, bf16[128,512]{1,0:T(8,128)(2,1)}) fusion(f32[4,2,128,512]{3,2,1,0:T(8,128)S(1)} %collective-permute-done, s32[]{:T(128)S(6)} %select_n.165, s32[]{:T(128)S(6)} %select_n.154, f32[4,2,2,128,512]{4,3,2,1,0:T(8,128)} %bitcast.119, s32[]{:T(128)S(6)} %select_n.157, ...), kind=kLoop, calls=%fused_computation.50 | loop fusion | flops 786432 | bytes 2359328 | tf_op jit(solution)/shard_map/convert_element_type | solution.py:73
  27.5 1.8 %collective-permute-start.2 = (bf16[128,512]{1,0:T(8,128)(2,1)}, bf16[128,512]{1,0:T(8,128)(2,1)S(1)}, u32[]{:S(2)}, u32[]{:S(2)}) collective-permute-start(bf16[128,512]{1,0:T(8,128)(2,1)} %get-tuple-element.9), channel_id=1, source_target_pairs={{0,8},{2,10},{4,12},{6,14},{8,16},{10,18},{12,20},{14,22},{16,24},... | collective-permute-start | bytes 393224 | tf_op jit(solution)/shard_map/ppermute | solution.py:73
  29.3 2.6 %collective-permute-start.3 = (bf16[128,512]{1,0:T(8,128)(2,1)}, bf16[128,512]{1,0:T(8,128)(2,1)S(1)}, u32[]{:S(2)}, u32[]{:S(2)}) collective-permute-start(bf16[128,512]{1,0:T(8,128)(2,1)} %get-tuple-element.11), channel_id=1, source_target_pairs={{0,16},{2,18},{4,20},{6,22},{8,24},{10,26},{12,28},{14,30},{16,0},... | collective-permute-start | bytes 393224 | tf_op jit(solution)/shard_map/ppermute | solution.py:73
  31.9 1.3 %collective-permute-start.4 = (bf16[128,512]{1,0:T(8,128)(2,1)S(1)}, bf16[128,512]{1,0:T(8,128)(2,1)}, u32[]{:S(2)}, u32[]{:S(2)}) collective-permute-start(bf16[128,512]{1,0:T(8,128)(2,1)S(1)} %get-tuple-element.10), channel_id=1, source_target_pairs={{0,24},{2,26},{4,28},{6,30},{8,0},{10,2},{12,4},{14,6},{16,8},{18,... | collective-permute-start | bytes 393224 | tf_op jit(solution)/shard_map/ppermute | solution.py:73
  33.3 1.7 %constant_dynamic-slice_fusion = bf16[512,1,2048]{0,2,1:T(8,128)(2,1)S(1)} fusion(bf16[512,2,2048]{0,2,1:T(8,128)(2,1)} %bitcast.110, s32[]{:T(128)S(6)} %select_n.173), kind=kLoop, calls=%fused_computation.72 | loop fusion | bytes 4194308 | tf_op jit(solution)/shard_map/jit(dynamic_index_in_dim)/dynamic_slice | solution.py:32
  35.0 2.5 %copy.18 = bf16[512,1,2048]{2,0,1:T(8,128)(2,1)} copy(bf16[512,1,2048]{0,2,1:T(8,128)(2,1)S(1)} %constant_dynamic-slice_fusion) | data formatting | bytes 4194304 | tf_op jit(solution)/shard_map/jit(dynamic_index_in_dim)/dynamic_slice | solution.py:32
  37.5 1.5 %collective-permute-start.5 = (bf16[512,2048]{1,0:T(8,128)(2,1)}, bf16[512,2048]{1,0:T(8,128)(2,1)}, u32[]{:S(2)}, u32[]{:S(2)}) collective-permute-start(bf16[512,2048]{1,0:T(8,128)(2,1)} %bitcast.122), channel_id=1, source_target_pairs={{0,1},{1,0},{2,3},{3,2},{4,5},{5,4},{6,7},{7,6},{8,9},{9,8},{10,11... | collective-permute-start | bytes 6291464 | tf_op jit(solution)/shard_map/ppermute | solution.py:83
  40.3 2.0 %convert_bitcast_fusion = (bf16[1,128,512]{2,1,0:T(8,128)(2,1)S(1)}, f32[128,512]{1,0:T(8,128)S(1)}, f32[128,512]{1,0:T(8,128)}) fusion(f32[1,128,512]{2,1,0:T(8,128)S(1)} %copy-done.6, f32[1,128,512]{2,1,0:T(8,128)S(1)} %copy-done.11, bf16[128,512]{1,0:T(8,128)(2,1)} %collective-permute-done.4, bf16[128,512]{1,0:T(8,128)(2,1)S(1)} %collective-permute-done.3, ...), kind=kLoop, calls=%fused_computation.78 | loop fusion | flops 1114112 | bytes 2228240 | tf_op jit(solution)/shard_map/broadcast_in_dim | solution.py:92
  42.2 4.3 %collective-permute-start.6 = (bf16[1,128,512]{2,1,0:T(8,128)(2,1)S(1)}, bf16[1,128,512]{2,1,0:T(8,128)(2,1)S(1)}, u32[]{:S(2)}, u32[]{:S(2)}) collective-permute-start(bf16[1,128,512]{2,1,0:T(8,128)(2,1)S(1)} %get-tuple-element.6), channel_id=1, source_target_pairs={{0,24},{2,26},{4,28},{6,30},{8,0},{10,2},{12,4},{14,6},{16,8},{18,... | collective-permute-start | bytes 393224 | tf_op jit(solution)/shard_map/ppermute | solution.py:95
  47.2 3.3 %collective-permute-done.6 = bf16[1,128,512]{2,1,0:T(8,128)(2,1)S(1)} collective-permute-done((bf16[1,128,512]{2,1,0:T(8,128)(2,1)S(1)}, bf16[1,128,512]{2,1,0:T(8,128)(2,1)S(1)}, u32[]{:S(2)}, u32[]{:S(2)}) %collective-permute-start.6) | collective-permute-done | bytes 131104 | tf_op jit(solution)/shard_map/ppermute | solution.py:95
  50.5 8.4 %collective-permute-done.7 = bf16[1,128,512]{2,1,0:T(8,128)(2,1)S(1)} collective-permute-done((bf16[1,128,512]{2,1,0:T(8,128)(2,1)S(1)}, bf16[1,128,512]{2,1,0:T(8,128)(2,1)S(1)}, u32[]{:S(2)}, u32[]{:S(2)}) %collective-permute-start.7) | collective-permute-done | bytes 131104 | tf_op jit(solution)/shard_map/ppermute | solution.py:95
  59.1 1.5 %collective-permute-start.9 = (bf16[4,128,512]{2,1,0:T(8,128)(2,1)S(1)}, bf16[4,128,512]{2,1,0:T(8,128)(2,1)S(1)}, u32[]{:S(2)}, u32[]{:S(2)}) collective-permute-start(bf16[4,128,512]{2,1,0:T(8,128)(2,1)S(1)} %get-tuple-element.18), channel_id=1, source_target_pairs={{0,4},{2,6},{4,0},{6,2},{8,12},{10,14},{12,8},{14,10},{16,20},{18,... | collective-permute-start | bytes 1572872 | tf_op jit(solution)/shard_map/ppermute | solution.py:95
  60.7 11.5 %collective-permute-done.9 = bf16[4,128,512]{2,1,0:T(8,128)(2,1)S(1)} collective-permute-done((bf16[4,128,512]{2,1,0:T(8,128)(2,1)S(1)}, bf16[4,128,512]{2,1,0:T(8,128)(2,1)S(1)}, u32[]{:S(2)}, u32[]{:S(2)}) %collective-permute-start.9) | collective-permute-done | bytes 524320 | tf_op jit(solution)/shard_map/ppermute | solution.py:95
  72.8 1.6 %collective-permute-start.12 = (s32[512]{0:T(512)S(1)}, s32[512]{0:T(512)S(1)}, u32[]{:S(2)}, u32[]{:S(2)}) collective-permute-start(s32[512]{0:T(512)S(1)} %bitcast.127), channel_id=1, source_target_pairs={{0,1},{1,0},{2,3},{3,2},{4,5},{5,4},{6,7},{7,6},{8,9},{9,8},{10,11... | collective-permute-start | bytes 6152 | tf_op jit(solution)/shard_map/ppermute | solution.py:85
  75.3 11.1 %collective-permute-done.12 = s32[512]{0:T(512)S(1)} collective-permute-done((s32[512]{0:T(512)S(1)}, s32[512]{0:T(512)S(1)}, u32[]{:S(2)}, u32[]{:S(2)}) %collective-permute-start.12) | collective-permute-done | bytes 2080 | tf_op jit(solution)/shard_map/ppermute | solution.py:85
  87.0 3.2 %multiply_cosine_fusion = (f32[512,64]{1,0:T(8,128)}, f32[512,64]{1,0:T(8,128)}, f32[512,64]{1,0:T(8,128)S(1)}, f32[512,64]{1,0:T(8,128)}, f32[512,64]{1,0:T(8,128)}) fusion(f32[512]{0:T(512)S(1)} %get-tuple-element.30, f32[64]{0:T(128)S(1)} %multiply_power_fusion, f32[512]{0:T(512)S(1)} %get-tuple-element.31), kind=kLoop, calls=%fused_computation.41 | loop fusion | flops 131072 | bytes 659712 | tf_op jit(solution)/shard_map/cos | solution.py:38
  90.2 4.9 %collective-permute-done.13 = bf16[512,512]{1,0:T(8,128)(2,1)} collective-permute-done((bf16[512,512]{1,0:T(8,128)(2,1)S(1)}, bf16[512,512]{1,0:T(8,128)(2,1)}, u32[]{:S(2)}, u32[]{:S(2)}) %collective-permute-start.13) | collective-permute-done | bytes 524320 | tf_op jit(solution)/shard_map/ppermute | solution.py:84
  95.1 1.4 %reshape.235 = f32[512,4,128]{2,1,0:T(4,128)S(1)} reshape(bf16[512,512]{1,0:T(8,128)(2,1)} %collective-permute-done.13) | data formatting | bytes 1572864 | tf_op jit(solution)/shard_map/reshape | solution.py:43
  96.5 2.4 %fusion.2 = bf16[8,2,128,512]{3,2,0,1:T(8,128)(2,1)S(1)} fusion(s32[]{:T(128)S(6)} %select_n.179, bf16[8,1,128,512]{3,2,0,1:T(8,128)(2,1)S(1)} %bitcast.116, bf16[8,1,128,512]{3,2,0,1:T(8,128)(2,1)} %bitcast.32), kind=kLoop, calls=%fused_computation.6 | loop fusion | flops 2097152 | bytes 4194308 | tf_op jit(solution)/shard_map/concatenate | solution.py:99
  99.1 2.9 %convolution_convert_fusion = bf16[512,512]{1,0:T(8,128)(2,1)S(1)} fusion(bf16[512,2048]{1,0:T(8,128)(2,1)} %collective-permute-done.5, bf16[2048,512]{1,0:T(8,128)(2,1)S(1)} %bitcast.113), kind=kOutput, calls=%fused_computation.19 | convolution fusion | flops 1074003968 | bytes 4718592 | tf_op jit(solution)/shard_map/dot_general | solution.py:119
  102.0 1.6 %collective-permute-start.11 = (bf16[512,512]{1,0:T(8,128)(2,1)S(1)}, bf16[512,512]{1,0:T(8,128)(2,1)S(1)}, u32[]{:S(2)}, u32[]{:S(2)}) collective-permute-start(bf16[512,512]{1,0:T(8,128)(2,1)S(1)} %convolution_convert_fusion), channel_id=1, source_target_pairs={{0,1},{1,0},{2,3},{3,2},{4,5},{5,4},{6,7},{7,6},{8,9},{9,8},{10,11... | collective-permute-start | bytes 1572872 | tf_op jit(solution)/shard_map/ppermute | solution.py:121
  104.5 1.5 %pad_maximum_fusion.2 = bf16[512,4,128]{2,1,0:T(4,128)(2,1)} fusion(bf16[512,4,64]{2,1,0:T(4,128)(2,1)S(1)} %get-tuple-element.13, bf16[512,4,64]{2,1,0:T(4,128)(2,1)S(1)} %get-tuple-element.12), kind=kLoop, calls=%fused_computation.37 | loop fusion | flops 1048576 | bytes 1048576 | tf_op jit(solution)/shard_map/concatenate | solution.py:46
  106.7 6.7 %collective-permute-done.11 = bf16[512,512]{1,0:T(8,128)(2,1)S(1)} collective-permute-done((bf16[512,512]{1,0:T(8,128)(2,1)S(1)}, bf16[512,512]{1,0:T(8,128)(2,1)S(1)}, u32[]{:S(2)}, u32[]{:S(2)}) %collective-permute-start.11) | collective-permute-done | bytes 524320 | tf_op jit(solution)/shard_map/ppermute | solution.py:121
  115.1 2.7 %subtract_convert_fusion.1 = (bf16[512,4,64]{2,1,0:T(4,128)(2,1)S(1)}, bf16[512,4,64]{2,1,0:T(4,128)(2,1)S(1)}, bf16[512,4,64]{2,1,0:T(4,128)(2,1)S(1)}, bf16[512,4,64]{2,1,0:T(4,128)(2,1)S(1)}) fusion(f32[512,4,128]{2,1,0:T(4,128)S(1)} %reshape.233, f32[512,64]{1,0:T(8,128)} %get-tuple-element.29, f32[512,64]{1,0:T(8,128)S(1)} %get-tuple-element.27, ...), kind=kLoop, calls=%fused_computation.27 | loop fusion | flops 2097152 | bytes 3538944 | tf_op jit(solution)/shard_map/convert.8
  118.6 3.2 %fusion.3 = f32[2048,512]{1,0:T(8,128)} fusion(bf16[512,2,2048]{0,2,1:T(8,128)(2,1)S(1)} %bitcast.112, s32[]{:T(128)S(6)} %select_n.180, bf16[64,8,4,128]{3,2,1,0:T(4,128)(2,1)S(1)} %bitcast.126), kind=kOutput, calls=%fused_computation.7 | convolution fusion | flops 1073741824 | bytes 6815748 | tf_op jit(solution)/shard_map/dot_general | solution.py:113
  123.5 5.4 %fusion = bf16[1,2048,512]{2,1,0:T(8,128)(2,1)} fusion(f32[2048,512]{1,0:T(8,128)} %fusion.3, bf16[512,2048]{1,0:T(8,128)(2,1)} %collective-permute-done.5, bf16[64,8,4,128]{3,2,1,0:T(4,128)(2,1)S(1)} %bitcast.124), kind=kOutput, calls=%fused_computation.4 | convolution fusion | flops 1075838976 | bytes 8912896 | tf_op jit(solution)/shard_map/dot_general | solution.py:113
  (59 shorter events, 10.4 us)
Async XLA Ops:
  3.7 4.5 %collective-permute-start = (f32[4,2,128,512]{3,2,1,0:T(8,128)}, f32[4,2,128,512]{3,2,1,0:T(8,128)S(1)}, u32[]{:S(2)}, u32[]{:S(2)}) collective-permute-start(f32[4,2,128,512]{3,2,1,0:T(8,128)} %dynamic-slice_bitcast_fusion), channel_id=1, source_target_pairs={{0,2},{2,0},{4,6},{6,4},{8,10},{10,8},{12,14},{14,12},{16,18},{18,... | collective-permute-start | bytes 6291464 | tf_op jit(solution)/shard_map/ppermute | solution.py:73
  8.2 17.3 %copy-start.3 = (f32[4,2,128,512]{3,2,1,0:T(8,128)}, f32[4,2,128,512]{3,2,1,0:T(8,128)S(1)}, u32[]{:S(2)}) copy-start(f32[4,2,128,512]{3,2,1,0:T(8,128)S(1)} %collective-permute-done) | copy-start | bytes 6291460
  10.3 15.2 %collective-permute-start.1 = (bf16[4,128,512]{2,1,0:T(8,128)(2,1)S(1)}, bf16[4,128,512]{2,1,0:T(8,128)(2,1)S(1)}, u32[]{:S(2)}, u32[]{:S(2)}) collective-permute-start(bf16[4,128,512]{2,1,0:T(8,128)(2,1)S(1)} %fusion.11), channel_id=1, source_target_pairs={{0,4},{2,6},{4,0},{6,2},{8,12},{10,14},{12,8},{14,10},{16,20},{18,... | collective-permute-start | bytes 1572872 | tf_op jit(solution)/shard_map/ppermute | solution.py:73
  27.5 11.5 %collective-permute-start.2 = (bf16[128,512]{1,0:T(8,128)(2,1)}, bf16[128,512]{1,0:T(8,128)(2,1)S(1)}, u32[]{:S(2)}, u32[]{:S(2)}) collective-permute-start(bf16[128,512]{1,0:T(8,128)(2,1)} %get-tuple-element.9), channel_id=1, source_target_pairs={{0,8},{2,10},{4,12},{6,14},{8,16},{10,18},{12,20},{14,22},{16,24},... | collective-permute-start | bytes 393224 | tf_op jit(solution)/shard_map/ppermute | solution.py:73
  29.3 10.9 %collective-permute-start.3 = (bf16[128,512]{1,0:T(8,128)(2,1)}, bf16[128,512]{1,0:T(8,128)(2,1)S(1)}, u32[]{:S(2)}, u32[]{:S(2)}) collective-permute-start(bf16[128,512]{1,0:T(8,128)(2,1)} %get-tuple-element.11), channel_id=1, source_target_pairs={{0,16},{2,18},{4,20},{6,22},{8,24},{10,26},{12,28},{14,30},{16,0},... | collective-permute-start | bytes 393224 | tf_op jit(solution)/shard_map/ppermute | solution.py:73
  31.9 8.3 %collective-permute-start.4 = (bf16[128,512]{1,0:T(8,128)(2,1)S(1)}, bf16[128,512]{1,0:T(8,128)(2,1)}, u32[]{:S(2)}, u32[]{:S(2)}) collective-permute-start(bf16[128,512]{1,0:T(8,128)(2,1)S(1)} %get-tuple-element.10), channel_id=1, source_target_pairs={{0,24},{2,26},{4,28},{6,30},{8,0},{10,2},{12,4},{14,6},{16,8},{18,... | collective-permute-start | bytes 393224 | tf_op jit(solution)/shard_map/ppermute | solution.py:73
  35.0 5.3 %copy-start.6 = (f32[1,128,512]{2,1,0:T(8,128)S(1)}, f32[1,128,512]{2,1,0:T(8,128)}, u32[]{:S(2)}) copy-start(f32[1,128,512]{2,1,0:T(8,128)} %param.11) | copy-start | bytes 786436
  35.0 5.3 %copy-start.11 = (f32[1,128,512]{2,1,0:T(8,128)S(1)}, f32[1,128,512]{2,1,0:T(8,128)}, u32[]{:S(2)}) copy-start(f32[1,128,512]{2,1,0:T(8,128)} %param.10) | copy-start | bytes 786436
  37.5 61.6 %collective-permute-start.5 = (bf16[512,2048]{1,0:T(8,128)(2,1)}, bf16[512,2048]{1,0:T(8,128)(2,1)}, u32[]{:S(2)}, u32[]{:S(2)}) collective-permute-start(bf16[512,2048]{1,0:T(8,128)(2,1)} %bitcast.122), channel_id=1, source_target_pairs={{0,1},{1,0},{2,3},{3,2},{4,5},{5,4},{6,7},{7,6},{8,9},{9,8},{10,11... | collective-permute-start | bytes 6291464 | tf_op jit(solution)/shard_map/ppermute | solution.py:83
  42.2 30.5 %copy-start.2 = (f32[128,512]{1,0:T(8,128)}, f32[128,512]{1,0:T(8,128)S(1)}, u32[]{:S(2)}) copy-start(f32[128,512]{1,0:T(8,128)S(1)} %get-tuple-element.7) | copy-start | bytes 786436
  42.2 8.2 %collective-permute-start.6 = (bf16[1,128,512]{2,1,0:T(8,128)(2,1)S(1)}, bf16[1,128,512]{2,1,0:T(8,128)(2,1)S(1)}, u32[]{:S(2)}, u32[]{:S(2)}) collective-permute-start(bf16[1,128,512]{2,1,0:T(8,128)(2,1)S(1)} %get-tuple-element.6), channel_id=1, source_target_pairs={{0,24},{2,26},{4,28},{6,30},{8,0},{10,2},{12,4},{14,6},{16,8},{18,... | collective-permute-start | bytes 393224 | tf_op jit(solution)/shard_map/ppermute | solution.py:95
  46.6 12.3 %collective-permute-start.7 = (bf16[1,128,512]{2,1,0:T(8,128)(2,1)S(1)}, bf16[1,128,512]{2,1,0:T(8,128)(2,1)S(1)}, u32[]{:S(2)}, u32[]{:S(2)}) collective-permute-start(bf16[1,128,512]{2,1,0:T(8,128)(2,1)S(1)} %get-tuple-element.6), channel_id=1, source_target_pairs={{0,16},{2,18},{4,20},{6,22},{8,24},{10,26},{12,28},{14,30},{16,0},... | collective-permute-start | bytes 393224 | tf_op jit(solution)/shard_map/ppermute | solution.py:95
  47.1 11.8 %collective-permute-start.8 = (bf16[1,128,512]{2,1,0:T(8,128)(2,1)S(1)}, bf16[1,128,512]{2,1,0:T(8,128)(2,1)S(1)}, u32[]{:S(2)}, u32[]{:S(2)}) collective-permute-start(bf16[1,128,512]{2,1,0:T(8,128)(2,1)S(1)} %get-tuple-element.6), channel_id=1, source_target_pairs={{0,8},{2,10},{4,12},{6,14},{8,16},{10,18},{12,20},{14,22},{16,24},... | collective-permute-start | bytes 393224 | tf_op jit(solution)/shard_map/ppermute | solution.py:95
  59.0 13.9 %copy-start.12 = (s32[1,512]{1,0:T(1,128)S(1)}, s32[1,512]{1,0:T(1,128)}, u32[]{:S(2)}) copy-start(s32[1,512]{1,0:T(1,128)} %param.8) | copy-start | bytes 6148
  59.0 15.4 %copy-start.9 = (bf16[1,512,512]{2,1,0:T(8,128)(2,1)S(1)}, bf16[1,512,512]{2,1,0:T(8,128)(2,1)}, u32[]{:S(2)}) copy-start(bf16[1,512,512]{2,1,0:T(8,128)(2,1)} %param.7) | copy-start | bytes 1572868
  59.1 13.1 %collective-permute-start.9 = (bf16[4,128,512]{2,1,0:T(8,128)(2,1)S(1)}, bf16[4,128,512]{2,1,0:T(8,128)(2,1)S(1)}, u32[]{:S(2)}, u32[]{:S(2)}) collective-permute-start(bf16[4,128,512]{2,1,0:T(8,128)(2,1)S(1)} %get-tuple-element.18), channel_id=1, source_target_pairs={{0,4},{2,6},{4,0},{6,2},{8,12},{10,14},{12,8},{14,10},{16,20},{18,... | collective-permute-start | bytes 1572872 | tf_op jit(solution)/shard_map/ppermute | solution.py:95
  72.7 23.7 %collective-permute-start.10 = (bf16[8,128,512]{2,1,0:T(8,128)(2,1)S(1)}, bf16[8,128,512]{2,1,0:T(8,128)(2,1)}, u32[]{:S(2)}, u32[]{:S(2)}) collective-permute-start(bf16[8,128,512]{2,1,0:T(8,128)(2,1)S(1)} %bitcast.115), channel_id=1, source_target_pairs={{0,2},{2,0},{4,6},{6,4},{8,10},{10,8},{12,14},{14,12},{16,18},{18,... | collective-permute-start | bytes 3145736 | tf_op jit(solution)/shard_map/ppermute | solution.py:95
  72.8 13.6 %collective-permute-start.12 = (s32[512]{0:T(512)S(1)}, s32[512]{0:T(512)S(1)}, u32[]{:S(2)}, u32[]{:S(2)}) collective-permute-start(s32[512]{0:T(512)S(1)} %bitcast.127), channel_id=1, source_target_pairs={{0,1},{1,0},{2,3},{3,2},{4,5},{5,4},{6,7},{7,6},{8,9},{9,8},{10,11... | collective-permute-start | bytes 6152 | tf_op jit(solution)/shard_map/ppermute | solution.py:85
  74.4 20.7 %collective-permute-start.13 = (bf16[512,512]{1,0:T(8,128)(2,1)S(1)}, bf16[512,512]{1,0:T(8,128)(2,1)}, u32[]{:S(2)}, u32[]{:S(2)}) collective-permute-start(bf16[512,512]{1,0:T(8,128)(2,1)S(1)} %bitcast.123), channel_id=1, source_target_pairs={{0,1},{1,0},{2,3},{3,2},{4,5},{5,4},{6,7},{7,6},{8,9},{9,8},{10,11... | collective-permute-start | bytes 1572872 | tf_op jit(solution)/shard_map/ppermute | solution.py:84
  99.1 4.5 %copy-start.4 = (f32[512,64]{1,0:T(8,128)S(1)}, f32[512,64]{1,0:T(8,128)}, u32[]{:S(2)}) copy-start(f32[512,64]{1,0:T(8,128)} %get-tuple-element.22) | copy-start | bytes 393220
  99.1 4.5 %copy-start.5 = (f32[512,64]{1,0:T(8,128)S(1)}, f32[512,64]{1,0:T(8,128)}, u32[]{:S(2)}) copy-start(f32[512,64]{1,0:T(8,128)} %get-tuple-element.23) | copy-start | bytes 393220
  102.0 11.4 %collective-permute-start.11 = (bf16[512,512]{1,0:T(8,128)(2,1)S(1)}, bf16[512,512]{1,0:T(8,128)(2,1)S(1)}, u32[]{:S(2)}, u32[]{:S(2)}) collective-permute-start(bf16[512,512]{1,0:T(8,128)(2,1)S(1)} %convolution_convert_fusion), channel_id=1, source_target_pairs={{0,1},{1,0},{2,3},{3,2},{4,5},{5,4},{6,7},{7,6},{8,9},{9,8},{10,11... | collective-permute-start | bytes 1572872 | tf_op jit(solution)/shard_map/ppermute | solution.py:121
  103.6 2.4 %copy-start.7 = (f32[1,128,512]{2,1,0:T(8,128)S(1)}, f32[1,128,512]{2,1,0:T(8,128)}, u32[]{:S(2)}) copy-start(f32[1,128,512]{2,1,0:T(8,128)} %param.11) | copy-start | bytes 786436
  103.6 2.4 %copy-start.8 = (f32[128,512]{1,0:T(8,128)S(1)}, f32[128,512]{1,0:T(8,128)}, u32[]{:S(2)}) copy-start(f32[128,512]{1,0:T(8,128)} %get-tuple-element.8) | copy-start | bytes 786436
  103.6 9.8 %copy-start = (bf16[1,512,4096]{1,2,0:T(8,128)(2,1)S(1)}, bf16[1,512,4096]{1,2,0:T(8,128)(2,1)}, u32[]{:S(2)}) copy-start(bf16[1,512,4096]{1,2,0:T(8,128)(2,1)} %copy.17) | copy-start | bytes 12582916
  115.1 3.5 %copy-start.1 = (bf16[1,512,4096]{1,2,0:T(8,128)(2,1)S(1)}, bf16[1,512,4096]{1,2,0:T(8,128)(2,1)}, u32[]{:S(2)}) copy-start(bf16[1,512,4096]{1,2,0:T(8,128)(2,1)} %copy.17) | copy-start | bytes 12582916
  121.8 1.7 %copy-start.10 = (bf16[512,4,128]{2,1,0:T(4,128)(2,1)S(1)}, bf16[512,4,128]{2,1,0:T(4,128)(2,1)}, u32[]{:S(2)}) copy-start(bf16[512,4,128]{2,1,0:T(4,128)(2,1)} %pad_maximum_fusion.2) | copy-start | bytes 1572868

commit v2 on v1

v2 whole, which is shorter than its diff:
```python
import functools
import math

import jax
import jax.numpy as jnp
from jax import lax
from jax.experimental import pallas as pl
from jax.experimental.pallas import tpu as pltpu
from jax.sharding import PartitionSpec as P

HEAD = 128
LINK = jnp.bfloat16


def factors_of(count):
    parts = []
    for size in (2, 2, 4):
        size = math.gcd(size, count)
        parts.append(size)
        count //= size
    return parts + [count]


def shift_pairs(count, stride, size, step):
    pairs = []
    for source in range(count):
        part = source // stride % size
        pairs.append((source, source + ((part + step) % size - part) * stride))
    return pairs


def picked(value, index, axis):
    return lax.dynamic_index_in_dim(value, index, axis, keepdims=False)


def total(terms):
    return sum(t.astype(jnp.float32) for t in terms)


def tables(positions):
    freqs = 500000.0 ** (-jnp.arange(HEAD // 2, dtype=jnp.float32) / (HEAD // 2))
    angles = positions.astype(jnp.float32)[:, None] * freqs[None, :]
    cosine, sine = jnp.cos(angles), jnp.sin(angles)
    return jnp.concatenate([cosine, cosine], axis=1), jnp.concatenate([-sine, sine], axis=1)


def turned(block, cosine, sine):
    return block * cosine + pltpu.roll(block, HEAD // 2, 1) * sine


def turn_kernel(sign, value_ref, cosine_ref, sine_ref, out_ref):
    cosine, sine = cosine_ref[...], sine_ref[...] * sign
    for head in range(value_ref.shape[1] // HEAD):
        at = pl.ds(head * HEAD, HEAD)
        block = value_ref[:, at].astype(jnp.float32)
        out_ref[:, at] = turned(block, cosine, sine).astype(out_ref.dtype)


def turn(value, cosine, sine, sign):
    return pl.pallas_call(
        functools.partial(turn_kernel, sign),
        out_shape=jax.ShapeDtypeStruct(value.shape, jnp.bfloat16),
        name="turn",
    )(value, cosine, sine)


def finish_kernel(own_ref, other_ref, cosine_ref, sine_ref, out_ref):
    cosine, sine = cosine_ref[...], sine_ref[...]
    for head in range(own_ref.shape[1] // HEAD):
        at = pl.ds(head * HEAD, HEAD)
        block = own_ref[:, at] + other_ref[:, at].astype(jnp.float32)
        out_ref[:, at] = turned(block, cosine, sine).astype(out_ref.dtype)


def finish(own, other, cosine, sine):
    return pl.pallas_call(
        finish_kernel,
        out_shape=jax.ShapeDtypeStruct(own.shape, jnp.bfloat16),
        name="finish",
    )(own, other, cosine, sine)


def project_kernel(count, place_ref, part_ref, *refs):
    bands, (out_ref, weights_ref) = refs[:count], refs[count:]
    at = 0
    for ref in bands:
        for i in range(ref.shape[0]):
            rows = ref.shape[1]
            start = pl.multiple_of(place_ref[at] * rows, rows)
            weights_ref[pl.ds(start, rows), :] = ref[i]
            at += 1
    out_ref[...] = jnp.dot(
        part_ref[...], weights_ref[...], preferred_element_type=jnp.float32
    ).astype(out_ref.dtype)


def project(places, part, bands):
    rows = sum(b.shape[0] * b.shape[1] for b in bands)
    columns = bands[0].shape[2]
    vmem = pl.BlockSpec(memory_space=pltpu.VMEM)
    return pl.pallas_call(
        functools.partial(project_kernel, len(bands)),
        in_specs=[pl.BlockSpec(memory_space=pltpu.SMEM)] + [vmem] * (1 + len(bands)),
        out_specs=[vmem, vmem],
        out_shape=[
            jax.ShapeDtypeStruct((part.shape[0], columns), LINK),
            jax.ShapeDtypeStruct((rows, columns), LINK),
        ],
        compiler_params=pltpu.CompilerParams(vmem_limit_bytes=40 * 1024 * 1024),
        name="project",
    )(places, part, *bands)


def local(tokens, cotangent, doc_ids, pseudo_grads, master, momentum):
    reps = lax.axis_size("rep")
    pair = lax.axis_size("fsdp")
    rep = lax.axis_index("rep")
    side = lax.axis_index("fsdp")
    parts = factors_of(reps)
    strides = [math.prod(parts[:i]) for i in range(len(parts))]
    place = [rep // stride % size for stride, size in zip(strides, parts)]
    band, columns = master.shape[1:]
    features = tokens[0]
    count, width = features.shape
    depth = width // pair

    def moved(value, level, step):
        pairs = shift_pairs(reps, strides[level], parts[level], step)
        return lax.ppermute(value, "rep", pairs)

    def across(value, step):
        return lax.ppermute(value, "fsdp", shift_pairs(pair, 1, pair, step))

    def half_of(step):
        return lax.dynamic_slice_in_dim(features, (side + step) % pair * depth, depth, 1)

    fast, middle, slow, rest = parts
    mine = pseudo_grads[0].reshape(rest, slow, middle, fast, band, columns)
    sent = [picked(mine, (place[0] + k) % fast, 3).astype(LINK) for k in range(1, fast)]
    documents = doc_ids[0]
    wanted = [half_of(step) for step in range(1, pair)]
    sent, wanted = lax.optimization_barrier((sent, wanted))
    terms = [moved(t, 0, k + 1) for k, t in enumerate(sent)]

    halves = {0: (half_of(0), cotangent[0], documents)}
    for step in range(1, pair):
        halves[(pair - step) % pair] = (
            across(wanted[step - 1], step),
            across(cotangent[0], step),
            across(documents, step),
        )

    terms = [picked(mine, place[0], 3)] + terms
    received = []
    own = None
    for k in list(range(1, slow)) + [0]:
        slices = [picked(t, (place[2] + k) % slow, 1) for t in terms]
        piece = [picked(t, place[1], 1) for t in slices]
        for step in range(1, middle):
            chosen = total([picked(t, (place[1] + step) % middle, 1) for t in slices])
            piece.append(moved(chosen.astype(LINK), 1, step))
        if k:
            received.append(moved(total(piece).astype(LINK), 2, k))
        else:
            own = piece
    terms = own + received
    here = [picked(t, place[3], 0) for t in terms]
    for step in range(1, rest):
        chosen = total([picked(t, (place[3] + step) % rest, 0) for t in terms])
        here.append(moved(chosen.astype(LINK), 3, step))

    outer_delta = total(here) / reps
    new_momentum = 0.9 * momentum[0] + outer_delta
    new_master = master[0] - 0.7 * (outer_delta + 0.9 * new_momentum)

    held = new_master.astype(LINK)[None]
    pieces = [(held, [0])] + [(moved(held, 3, rest - k), [k]) for k in range(1, rest)]
    held = jnp.concatenate([piece for piece, _ in pieces])
    outer = [(place[3] + k) % rest * strides[3] for k in range(rest)]
    first = [(held if k == 0 else moved(held, 2, slow - k), k) for k in range(slow)]
    bands, places = [], []
    for shift in range(middle):
        group = [piece if shift == 0 else moved(piece, 1, middle - shift) for piece, _ in first]
        spots = [
            o + (place[2] + k) % slow * strides[2] + (place[1] + shift) % middle * strides[1]
            for _, k in first
            for o in outer
        ]
        bands += group
        places += [spot + place[0] for spot in spots]
        joined = jnp.concatenate(group)
        for step in range(1, fast):
            bands.append(moved(joined, 0, fast - step))
            places += [spot + (place[0] + step) % fast for spot in spots]
    places = jnp.stack(places)

    grads = jnp.zeros((depth, columns), jnp.float32)
    turns = {}
    for step, (part, upstream, docs) in halves.items():
        at = (side + step) % pair * count + jnp.arange(count, dtype=jnp.int32)
        for _, _, others in halves.values():
            at = at - jnp.sum((others[None, :] < docs[:, None]).astype(jnp.int32), axis=1)
        turns[step] = tables(at)
        rotated = turn(upstream, *turns[step], -1.0)
        grads = grads + lax.dot_general(
            part, rotated, (((0,), (0,)), ((), ())), preferred_element_type=jnp.float32
        )

    weights = None
    other = 0
    for step in range(1, pair):
        if weights is None:
            product, weights = project(places, halves[step][0], bands)
        else:
            product = jnp.dot(halves[step][0], weights, preferred_element_type=jnp.float32)
        other = other + across(product.astype(LINK), step)
    product = jnp.dot(halves[0][0], weights, preferred_element_type=jnp.float32)
    keys = finish(product, other, *turns[0])
    return (
        new_master[None],
        new_momentum[None],
        keys[None],
        grads.astype(jnp.bfloat16)[None],
    )


def solution(mesh):
    return jax.shard_map(
        local,
        mesh=mesh,
        in_specs=(
            P("rep", "fsdp", None),
            P("rep", "fsdp", None),
            P("rep", "fsdp"),
            P("rep", "fsdp", None),
            P("fsdp", "rep", None),
            P("fsdp", "rep", None),
        ),
        out_specs=(
            P("fsdp", "rep", None),
            P("fsdp", "rep", None),
            P("rep", "fsdp", None),
            P("rep", "fsdp", None),
        ),
        check_vma=False,
    )
```

time: 129 us -> 100 us (0.78)
  waiting for transfers between devices: 56.9 us -> 27.3 us
  Pallas kernels: 0 us -> 9.71 us
  local copies, waits for them, and re-layouts: 17.2 us -> 12.4 us
  other arithmetic: 20.2 us -> 16 us
  starting transfers between devices: 20.9 us -> 23.9 us
  matrix products: 12.8 us -> 9.94 us
    ppermute x14 -> x21, waiting for transfers between devices: 56.9 us -> 27.3 us  [the longest x17 19.5 us: moved(): return lax.ppermute(value, 'rep', pairs)]
    pallas_call x0 -> x4, Pallas kernels: none -> 9.71 us  [the longest x2 4.63 us: turn(): pl.pallas_call(functools.partial(turn_kernel, sign), out_shape=jax.ShapeD...]
    another operation x2 -> x0, other arithmetic: 3.58 us -> none
    cos x1 -> x0, other arithmetic: 3.19 us -> none  [tables(): return (jnp.cos(angles)[:, None, :], jnp.sin(angles)[:, None, :])]
    squeeze x1 -> x0, local copies, waits for them, and re-layouts: 3.09 us -> none  [picked(): return lax.dynamic_index_in_dim(value, index, axis, keepdims=False)]
    ppermute x14 -> x21, starting transfers between devices: 20.9 us -> 23.9 us  [the longest x17 18.6 us: moved(): return lax.ppermute(value, 'rep', pairs)]
    neg x0 -> x1, other arithmetic: none -> 2.73 us  [tables(): -sine]
    broadcast_in_dim x2 -> x0, other arithmetic: 2.72 us -> none  [the longest x1 1.97 us: local(): held = new_master.astype(LINK)[None]]
  transfers between devices with their start and end apart: 14 -> 21, of which waited for: 9 -> 9; matrix products, arithmetic and copies ran while one was open for 19% -> 26% of each run, Pallas kernels for 0% -> 5%
where the time goes in v2:
time: 100 us
  waiting for transfers between devices  27.3 us (27%)
  starting transfers between devices  23.9 us (24%)
  other arithmetic  16 us (16%)
  local copies, waits for them, and re-layouts  12.4 us (12%)
  matrix products  9.94 us (10%)
  Pallas kernels  9.71 us (10%)
    ppermute x17, waiting for transfers between devices, moved(): return lax.ppermute(value, 'rep', pairs)  19.5 us
    ppermute x17, starting transfers between devices, moved(): return lax.ppermute(value, 'rep', pairs)  18.6 us
    ppermute x4, waiting for transfers between devices, across(): return lax.ppermute(value, 'fsdp', shift_pairs(pair, 1, pair, step))  7.83 us
    dot_general x2, matrix products, local(): lax.dot_general(part, rotated, (((0,), (0,)), ((), ())), preferred_elemen...  7.66 us
    unnamed x30, local copies, waits for them, and re-layouts  6.37 us
    ppermute x4, starting transfers between devices, across(): return lax.ppermute(value, 'fsdp', shift_pairs(pair, 1, pair, step))  5.22 us
    pallas_call x2, Pallas kernels, turn(): pl.pallas_call(functools.partial(turn_kernel, sign), out_shape=jax.ShapeD...  4.63 us
    dynamic_slice x1, local copies, waits for them, and re-layouts, half_of(): lax.dynamic_slice_in_dim(features, (side + step) % pair * depth, depth, 1)  3.2 us
  transfers between devices with their start and end apart: 21, of which 9 were waited for; matrix products, arithmetic and copies ran while one was open for 26% of the time, Pallas kernels for 5%

profile of v2, /device:TPU:0, one launch (start us, length us, event | category | flops | bytes accessed | tf_op | source)
XLA Modules:
  0.0 100.0 jit_solution(10709729725439356928)
XLA Ops:
  0.7 2.7 %fusion.7 = bf16[1,4,2,128,512]{4,3,2,1,0:T(8,128)(2,1)} fusion(f32[1,4,2,2,128,512]{5,4,3,2,1,0:T(8,128)} %bitcast.79, s32[]{:T(128)S(6)} %select_n.224), kind=kLoop, calls=%fused_computation.10 | loop fusion | bytes 2097156 | tf_op jit(solution)/shard_map/convert_element_type | solution.py:139
  3.4 3.2 %dynamic-slice_bitcast_fusion = bf16[512,2048]{1,0:T(8,128)(2,1)} fusion(bf16[1,512,4096]{2,1,0:T(8,128)(2,1)} %param.6, s32[]{:T(128)S(6)} %select_n.226), kind=kLoop, calls=%fused_computation.7 | loop fusion | bytes 4194308 | tf_op jit(solution)/shard_map/dynamic_slice | solution.py:135
  7.1 2.5 %collective-permute-start.19 = (s32[512]{0:T(512)S(1)}, s32[512]{0:T(512)S(1)}, u32[]{:S(2)}, u32[]{:S(2)}) collective-permute-start(s32[512]{0:T(512)S(1)} %bitcast.86), channel_id=1, source_target_pairs={{0,1},{1,0},{2,3},{3,2},{4,5},{5,4},{6,7},{7,6},{8,9},{9,8},{10,11... | collective-permute-start | bytes 6152 | tf_op jit(solution)/shard_map/ppermute | solution.py:132
  9.8 1.4 %fusion.17 = (bf16[1,128,512]{2,1,0:T(8,128)(2,1)S(1)}, bf16[1,128,512]{2,1,0:T(8,128)(2,1)S(1)}, bf16[1,128,512]{2,1,0:T(8,128)(2,1)S(1)}, bf16[1,128,512]{2,1,0:T(8,128)(2,1)S(1)}) fusion(f32[1,4,2,2,128,512]{5,4,3,2,1,0:T(8,128)} %bitcast.80, s32[]{:T(128)S(6)} %select_n.215, s32[]{:T(128)S(6)} %select_n.229, s32[]{:T(128)S(6)} %select_n.222, ...), kind=kLoop, calls=%fused_computation.41 | loop fusion | flops 786432 | bytes 2097176 | tf_op jit(solution)/shard_map/convert_element_type | solution.py:161
  11.2 2.6 %collective-permute-start.6 = (bf16[1,128,512]{2,1,0:T(8,128)(2,1)S(1)}, bf16[1,128,512]{2,1,0:T(8,128)(2,1)S(1)}, u32[]{:S(2)}, u32[]{:S(2)}) collective-permute-start(bf16[1,128,512]{2,1,0:T(8,128)(2,1)S(1)} %get-tuple-element.20), channel_id=1, source_target_pairs={{0,4},{2,6},{4,0},{6,2},{8,12},{10,14},{12,8},{14,10},{16,20},{18,... | collective-permute-start | bytes 393224 | tf_op jit(solution)/shard_map/ppermute | solution.py:129
  13.9 1.9 %collective-permute-start.2 = (bf16[1,128,512]{2,1,0:T(8,128)(2,1)S(1)}, bf16[1,128,512]{2,1,0:T(8,128)(2,1)S(1)}, u32[]{:S(2)}, u32[]{:S(2)}) collective-permute-start(bf16[1,128,512]{2,1,0:T(8,128)(2,1)S(1)} %get-tuple-element.22), channel_id=1, source_target_pairs={{0,4},{2,6},{4,0},{6,2},{8,12},{10,14},{12,8},{14,10},{16,20},{18,... | collective-permute-start | bytes 393224 | tf_op jit(solution)/shard_map/ppermute | solution.py:129
  16.6 1.5 %collective-permute-done.6 = bf16[1,128,512]{2,1,0:T(8,128)(2,1)S(1)} collective-permute-done((bf16[1,128,512]{2,1,0:T(8,128)(2,1)S(1)}, bf16[1,128,512]{2,1,0:T(8,128)(2,1)S(1)}, u32[]{:S(2)}, u32[]{:S(2)}) %collective-permute-start.6) | collective-permute-done | bytes 131104 | tf_op jit(solution)/shard_map/ppermute | solution.py:129
  18.1 2.8 %collective-permute-done.4 = bf16[1,128,512]{2,1,0:T(8,128)(2,1)S(1)} collective-permute-done((bf16[1,128,512]{2,1,0:T(8,128)(2,1)S(1)}, bf16[1,128,512]{2,1,0:T(8,128)(2,1)S(1)}, u32[]{:S(2)}, u32[]{:S(2)}) %collective-permute-start.4) | collective-permute-done | bytes 131104 | tf_op jit(solution)/shard_map/ppermute | solution.py:129
  20.9 2.8 %collective-permute-done.2 = bf16[1,128,512]{2,1,0:T(8,128)(2,1)S(1)} collective-permute-done((bf16[1,128,512]{2,1,0:T(8,128)(2,1)S(1)}, bf16[1,128,512]{2,1,0:T(8,128)(2,1)S(1)}, u32[]{:S(2)}, u32[]{:S(2)}) %collective-permute-start.2) | collective-permute-done | bytes 131104 | tf_op jit(solution)/shard_map/ppermute | solution.py:129
  23.7 1.3 %fusion.16 = (bf16[1,128,512]{2,1,0:T(8,128)(2,1)S(1)}, bf16[1,128,512]{2,1,0:T(8,128)(2,1)S(1)}, bf16[1,128,512]{2,1,0:T(8,128)(2,1)S(1)}) fusion(bf16[1,128,512]{2,1,0:T(8,128)(2,1)S(1)} %collective-permute-done.2, f32[1,4,2,2,128,512]{5,4,3,2,1,0:T(8,128)} %bitcast.81, s32[]{:T(128)S(6)} %select_n.232, s32[]{:T(128)S(6)} %select_n.219, s32[]{:T(128)S(6)} %select_n.222, ...), kind=kLoop, calls=%fused_computation.39 | loop fusion | flops 983040 | bytes 1966100 | tf_op jit(solution)/shard_map/convert_element_type | solution.py:163
  25.0 2.2 %collective-permute-start.3 = (bf16[1,128,512]{2,1,0:T(8,128)(2,1)S(1)}, bf16[1,128,512]{2,1,0:T(8,128)(2,1)S(1)}, u32[]{:S(2)}, u32[]{:S(2)}) collective-permute-start(bf16[1,128,512]{2,1,0:T(8,128)(2,1)S(1)} %get-tuple-element.23), channel_id=1, source_target_pairs={{0,8},{2,10},{4,12},{6,14},{8,16},{10,18},{12,20},{14,22},{16,24},... | collective-permute-start | bytes 393224 | tf_op jit(solution)/shard_map/ppermute | solution.py:129
  27.2 2.1 %collective-permute-start.7 = (bf16[1,128,512]{2,1,0:T(8,128)(2,1)S(1)}, bf16[1,128,512]{2,1,0:T(8,128)(2,1)S(1)}, u32[]{:S(2)}, u32[]{:S(2)}) collective-permute-start(bf16[1,128,512]{2,1,0:T(8,128)(2,1)S(1)} %get-tuple-element.24), channel_id=1, source_target_pairs={{0,24},{2,26},{4,28},{6,30},{8,0},{10,2},{12,4},{14,6},{16,8},{18,... | collective-permute-start | bytes 393224 | tf_op jit(solution)/shard_map/ppermute | solution.py:129
  30.2 3.3 %collective-permute-done.3 = bf16[1,128,512]{2,1,0:T(8,128)(2,1)S(1)} collective-permute-done((bf16[1,128,512]{2,1,0:T(8,128)(2,1)S(1)}, bf16[1,128,512]{2,1,0:T(8,128)(2,1)S(1)}, u32[]{:S(2)}, u32[]{:S(2)}) %collective-permute-start.3) | collective-permute-done | bytes 131104 | tf_op jit(solution)/shard_map/ppermute | solution.py:129
  33.6 6.2 %collective-permute-done.5 = bf16[1,128,512]{2,1,0:T(8,128)(2,1)S(1)} collective-permute-done((bf16[1,128,512]{2,1,0:T(8,128)(2,1)S(1)}, bf16[1,128,512]{2,1,0:T(8,128)(2,1)S(1)}, u32[]{:S(2)}, u32[]{:S(2)}) %collective-permute-start.5) | collective-permute-done | bytes 131104 | tf_op jit(solution)/shard_map/ppermute | solution.py:129
  39.8 1.9 %fusion.27 = (bf16[1,128,512]{2,1,0:T(8,128)(2,1)S(1)}, f32[1,128,512]{2,1,0:T(8,128)}, f32[1,128,512]{2,1,0:T(8,128)}) fusion(f32[1,128,512]{2,1,0:T(8,128)S(1)} %copy-done.12, f32[1,128,512]{2,1,0:T(8,128)S(1)} %copy-done.13, bf16[1,128,512]{2,1,0:T(8,128)(2,1)S(1)} %collective-permute-done.7, bf16[1,128,512]{2,1,0:T(8,128)(2,1)S(1)} %collective-permute-done.5, ...), kind=kLoop, calls=%fused_computation.57 | loop fusion | flops 1179648 | bytes 2097164 | tf_op jit(solution)/shard_map/convert_element_type | solution.py:176
  41.7 2.9 %collective-permute-start.10 = (bf16[1,128,512]{2,1,0:T(8,128)(2,1)S(1)}, bf16[1,128,512]{2,1,0:T(8,128)(2,1)S(1)}, u32[]{:S(2)}, u32[]{:S(2)}) collective-permute-start(bf16[1,128,512]{2,1,0:T(8,128)(2,1)S(1)} %get-tuple-element.16.refs_0_), channel_id=1, source_target_pairs={{0,16},{2,18},{4,20},{6,22},{8,24},{10,26},{12,28},{14,30},{16,0},... | collective-permute-start | bytes 393224 | tf_op jit(solution)/shard_map/ppermute | solution.py:129
  45.6 2.7 %fusion.24 = (f32[512,64]{1,0:T(8,128)}, f32[512,64]{1,0:T(8,128)}, f32[512,64]{1,0:T(8,128)}, f32[512,64]{1,0:T(8,128)S(1)}, f32[512,64]{1,0:T(8,128)S(1)}, /*index=5*/f32[512,64]{1,0:T(8,128)S(1)}) fusion(f32[64]{0:T(128)S(1)} %multiply_power_fusion, f32[512]{0:T(512)S(1)} %get-tuple-element.35, f32[512]{0:T(512)S(1)} %get-tuple-element.36), kind=kLoop, calls=%fused_computation.51 | loop fusion | flops 131072 | bytes 790784 | tf_op jit(solution)/shard_map/neg | solution.py:44
  49.1 1.4 %collective-permute-start.13 = (bf16[1,128,512]{2,1,0:T(8,128)(2,1)S(1)}, bf16[1,128,512]{2,1,0:T(8,128)(2,1)S(1)}, u32[]{:S(2)}, u32[]{:S(2)}) collective-permute-start(bf16[1,128,512]{2,1,0:T(8,128)(2,1)S(1)} %get-tuple-element.16.refs_0_), channel_id=1, source_target_pairs={{0,4},{2,6},{4,0},{6,2},{8,12},{10,14},{12,8},{14,10},{16,20},{18,... | collective-permute-start | bytes 393224 | tf_op jit(solution)/shard_map/ppermute | solution.py:129
  51.4 2.1 %collective-permute-done.10.refs_2_ = bf16[1,128,512]{2,1,0:T(8,128)(2,1)S(1)} collective-permute-done((bf16[1,128,512]{2,1,0:T(8,128)(2,1)S(1)}, bf16[1,128,512]{2,1,0:T(8,128)(2,1)S(1)}, u32[]{:S(2)}, u32[]{:S(2)}) %collective-permute-start.10) | collective-permute-done | bytes 131104 | tf_op jit(solution)/shard_map/ppermute | solution.py:129
  54.5 1.1 %collective-permute-start.14 = (bf16[1,128,512]{2,1,0:T(8,128)(2,1)S(1)}, bf16[1,128,512]{2,1,0:T(8,128)(2,1)}, u32[]{:S(2)}, u32[]{:S(2)}) collective-permute-start(bf16[1,128,512]{2,1,0:T(8,128)(2,1)S(1)} %collective-permute-done.9.refs_1_), channel_id=1, source_target_pairs={{0,4},{2,6},{4,0},{6,2},{8,12},{10,14},{12,8},{14,10},{16,20},{18,... | collective-permute-start | bytes 393224 | tf_op jit(solution)/shard_map/ppermute | solution.py:129
  56.4 2.3 %turn.2 = bf16[512,512]{1,0:T(8,128)(2,1)} custom-call(bf16[512,512]{1,0:T(8,128)(2,1)} %bitcast.83, f32[512,128]{1,0:T(8,128)} %pad_maximum_fusion.2.cosine_ref, f32[512,128]{1,0:T(8,128)} %pad_maximum_fusion.3.sine_ref), custom_call_target="tpu_custom_call" | custom-call | tf_op jit(solution)/shard_map/turn/pallas_call | solution.py:60
  61.3 1.8 %pad_maximum_fusion.1 = bf16[4,128,512]{2,1,0:T(8,128)(2,1)} fusion(bf16[1,128,512]{2,1,0:T(8,128)(2,1)S(1)} %collective-permute-done.16.refs_8_, bf16[1,128,512]{2,1,0:T(8,128)(2,1)S(1)} %collective-permute-done.15.refs_7_, bf16[1,128,512]{2,1,0:T(8,128)(2,1)} %collective-permute-done.14.refs_6_, bf16[1,128,512]{2,1,0:T(8,128)(2,1)S(1)} %collective-permute-done.13.refs_5_), kind=kLoop, calls=%fused_computation.16 | loop fusion | flops 786432 | bytes 1048576 | tf_op jit(solution)/shard_map/concatenate | solution.py:191
  65.0 1.9 %pad_maximum_fusion.4.cosine_ref = f32[512,128]{1,0:T(8,128)} fusion(f32[512,64]{1,0:T(8,128)} %get-tuple-element.27), kind=kLoop, calls=%fused_computation.23 | loop fusion | flops 65536 | bytes 393216 | tf_op jit(solution)/shard_map/concatenate | solution.py:44
  66.9 1.9 %pad_maximum_fusion.5.sine_ref = f32[512,128]{1,0:T(8,128)} fusion(f32[512,64]{1,0:T(8,128)} %get-tuple-element.28, f32[512,64]{1,0:T(8,128)} %get-tuple-element.26), kind=kLoop, calls=%fused_computation.24 | loop fusion | flops 65536 | bytes 524288 | tf_op jit(solution)/shard_map/concatenate | solution.py:44
  68.8 4.9 %fusion.1 = f32[2048,512]{1,0:T(8,128)} fusion(bf16[512,512]{1,0:T(8,128)(2,1)} %turn.2, bf16[1,512,4096]{2,1,0:T(8,128)(2,1)} %param.6, s32[]{:T(128)S(6)} %select_n.240), kind=kOutput, calls=%fused_computation.3 | convolution fusion | flops 1073741824 | bytes 6815748 | tf_op jit(solution)/shard_map/dot_general | solution.py:205
  73.7 2.3 %turn.3 = bf16[512,512]{1,0:T(8,128)(2,1)} custom-call(bf16[512,512]{1,0:T(8,128)(2,1)} %collective-permute-done.20.value_ref, f32[512,128]{1,0:T(8,128)} %pad_maximum_fusion.4.cosine_ref, f32[512,128]{1,0:T(8,128)} %pad_maximum_fusion.5.sine_ref), custom_call_target="tpu_custom_call" | custom-call | tf_op jit(solution)/shard_map/turn/pallas_call | solution.py:60
  79.7 2.4 %project.1 = (bf16[512,512]{1,0:T(8,128)(2,1)S(1)}, bf16[2048,512]{1,0:T(8,128)(2,1)S(1)}) custom-call(s32[16]{0:T(128)S(1)} %stack.67.place_ref, bf16[512,2048]{1,0:T(8,128)(2,1)S(1)} %collective-permute-done.8.part_ref, bf16[1,128,512]{2,1,0:T(8,128)(2,1)S(1)} %get-tuple-element.16.refs_0_, bf16[1,128,512]{2,1,0:T(8,128)(2,1)S(1)} %copy-done.1, ...), custom_call_target="tpu_custom_call" | custom-call | tf_op jit(solution)/shard_map/project/pallas_call | solution.py:101
  82.1 1.6 %collective-permute-start.18 = (bf16[512,512]{1,0:T(8,128)(2,1)S(1)}, bf16[512,512]{1,0:T(8,128)(2,1)S(1)}, u32[]{:S(2)}, u32[]{:S(2)}) collective-permute-start(bf16[512,512]{1,0:T(8,128)(2,1)S(1)} %get-tuple-element.11), channel_id=1, source_target_pairs={{0,1},{1,0},{2,3},{3,2},{4,5},{5,4},{6,7},{7,6},{8,9},{9,8},{10,11... | collective-permute-start | bytes 1572872 | tf_op jit(solution)/shard_map/ppermute | solution.py:132
  83.7 2.3 %fusion.3.own_ref = f32[512,512]{1,0:T(8,128)} fusion(bf16[2048,512]{1,0:T(8,128)(2,1)S(1)} %get-tuple-element.10, bf16[1,512,4096]{2,1,0:T(8,128)(2,1)S(1)} %copy-done.9, s32[]{:T(128)S(6)} %select_n.240), kind=kOutput, calls=%fused_computation.5 | convolution fusion | flops 1073741824 | bytes 5242884 | tf_op jit(solution)/shard_map/dot_general | solution.py:217
  86.0 2.7 %fusion = bf16[1,2048,512]{2,1,0:T(8,128)(2,1)} fusion(f32[2048,512]{1,0:T(8,128)S(1)} %copy-done.8, bf16[512,2048]{1,0:T(8,128)(2,1)S(1)} %collective-permute-done.8.part_ref, bf16[512,512]{1,0:T(8,128)(2,1)S(1)} %copy-done.10), kind=kOutput, calls=%fused_computation.1 | convolution fusion | flops 1075838976 | bytes 8912896 | tf_op jit(solution)/shard_map/dot_general | solution.py:205
  88.7 7.8 %collective-permute-done.18.other_ref = bf16[512,512]{1,0:T(8,128)(2,1)S(1)} collective-permute-done((bf16[512,512]{1,0:T(8,128)(2,1)S(1)}, bf16[512,512]{1,0:T(8,128)(2,1)S(1)}, u32[]{:S(2)}, u32[]{:S(2)}) %collective-permute-start.18) | collective-permute-done | bytes 524320 | tf_op jit(solution)/shard_map/ppermute | solution.py:132
  97.3 2.6 %finish.1 = bf16[512,512]{1,0:T(8,128)(2,1)} custom-call(f32[512,512]{1,0:T(8,128)} %fusion.3.own_ref, bf16[512,512]{1,0:T(8,128)(2,1)} %copy-done.11, f32[512,128]{1,0:T(8,128)} %pad_maximum_fusion.2.cosine_ref, f32[512,128]{1,0:T(8,128)} %pad_maximum_fusion.3.sine_ref), custom_call_target="tpu_custom_call" | custom-call | tf_op jit(solution)/shard_map/finish/pallas_call | solution.py:76
  (63 shorter events, 15.8 us)
Async XLA Ops:
  0.6 6.4 %copy-start.14 = (s32[1,512]{1,0:T(1,128)S(1)}, s32[1,512]{1,0:T(1,128)}, u32[]{:S(2)}) copy-start(s32[1,512]{1,0:T(1,128)} %param.8) | copy-start | bytes 6148
  3.4 36.4 %copy-start.12 = (f32[1,128,512]{2,1,0:T(8,128)S(1)}, f32[1,128,512]{2,1,0:T(8,128)}, u32[]{:S(2)}) copy-start(f32[1,128,512]{2,1,0:T(8,128)} %param.10) | copy-start | bytes 786436
  6.6 3.2 %collective-permute-start = (bf16[1,4,2,128,512]{4,3,2,1,0:T(8,128)(2,1)}, bf16[1,4,2,128,512]{4,3,2,1,0:T(8,128)(2,1)S(1)}, u32[]{:S(2)}, u32[]{:S(2)}) collective-permute-start(bf16[1,4,2,128,512]{4,3,2,1,0:T(8,128)(2,1)} %fusion.7), channel_id=1, source_target_pairs={{0,2},{2,0},{4,6},{6,4},{8,10},{10,8},{12,14},{14,12},{16,18},{18,... | collective-permute-start | bytes 3145736 | tf_op jit(solution)/shard_map/ppermute | solution.py:129
  7.1 8.8 %collective-permute-start.19 = (s32[512]{0:T(512)S(1)}, s32[512]{0:T(512)S(1)}, u32[]{:S(2)}, u32[]{:S(2)}) collective-permute-start(s32[512]{0:T(512)S(1)} %bitcast.86), channel_id=1, source_target_pairs={{0,1},{1,0},{2,3},{3,2},{4,5},{5,4},{6,7},{7,6},{8,9},{9,8},{10,11... | collective-permute-start | bytes 6152 | tf_op jit(solution)/shard_map/ppermute | solution.py:132
  9.6 66.5 %collective-permute-start.8 = (bf16[512,2048]{1,0:T(8,128)(2,1)}, bf16[512,2048]{1,0:T(8,128)(2,1)S(1)}, u32[]{:S(2)}, u32[]{:S(2)}) collective-permute-start(bf16[512,2048]{1,0:T(8,128)(2,1)} %dynamic-slice_bitcast_fusion), channel_id=1, source_target_pairs={{0,1},{1,0},{2,3},{3,2},{4,5},{5,4},{6,7},{7,6},{8,9},{9,8},{10,11... | collective-permute-start | bytes 6291464 | tf_op jit(solution)/shard_map/ppermute | solution.py:132
  9.7 30.1 %copy-start.13 = (f32[1,128,512]{2,1,0:T(8,128)S(1)}, f32[1,128,512]{2,1,0:T(8,128)}, u32[]{:S(2)}) copy-start(f32[1,128,512]{2,1,0:T(8,128)} %param.11) | copy-start | bytes 786436
  11.2 6.9 %collective-permute-start.6 = (bf16[1,128,512]{2,1,0:T(8,128)(2,1)S(1)}, bf16[1,128,512]{2,1,0:T(8,128)(2,1)S(1)}, u32[]{:S(2)}, u32[]{:S(2)}) collective-permute-start(bf16[1,128,512]{2,1,0:T(8,128)(2,1)S(1)} %get-tuple-element.20), channel_id=1, source_target_pairs={{0,4},{2,6},{4,0},{6,2},{8,12},{10,14},{12,8},{14,10},{16,20},{18,... | collective-permute-start | bytes 393224 | tf_op jit(solution)/shard_map/ppermute | solution.py:129
  13.8 7.1 %collective-permute-start.4 = (bf16[1,128,512]{2,1,0:T(8,128)(2,1)S(1)}, bf16[1,128,512]{2,1,0:T(8,128)(2,1)S(1)}, u32[]{:S(2)}, u32[]{:S(2)}) collective-permute-start(bf16[1,128,512]{2,1,0:T(8,128)(2,1)S(1)} %get-tuple-element.21), channel_id=1, source_target_pairs={{0,4},{2,6},{4,0},{6,2},{8,12},{10,14},{12,8},{14,10},{16,20},{18,... | collective-permute-start | bytes 393224 | tf_op jit(solution)/shard_map/ppermute | solution.py:129
  13.9 9.8 %collective-permute-start.2 = (bf16[1,128,512]{2,1,0:T(8,128)(2,1)S(1)}, bf16[1,128,512]{2,1,0:T(8,128)(2,1)S(1)}, u32[]{:S(2)}, u32[]{:S(2)}) collective-permute-start(bf16[1,128,512]{2,1,0:T(8,128)(2,1)S(1)} %get-tuple-element.22), channel_id=1, source_target_pairs={{0,4},{2,6},{4,0},{6,2},{8,12},{10,14},{12,8},{14,10},{16,20},{18,... | collective-permute-start | bytes 393224 | tf_op jit(solution)/shard_map/ppermute | solution.py:129
  16.4 13.8 %collective-permute-start.1 = (bf16[1,128,512]{2,1,0:T(8,128)(2,1)S(1)}, bf16[1,128,512]{2,1,0:T(8,128)(2,1)S(1)}, u32[]{:S(2)}, u32[]{:S(2)}) collective-permute-start(bf16[1,128,512]{2,1,0:T(8,128)(2,1)S(1)} %get-tuple-element.19), channel_id=1, source_target_pairs={{0,4},{2,6},{4,0},{6,2},{8,12},{10,14},{12,8},{14,10},{16,20},{18,... | collective-permute-start | bytes 393224 | tf_op jit(solution)/shard_map/ppermute | solution.py:129
  25.0 8.6 %collective-permute-start.3 = (bf16[1,128,512]{2,1,0:T(8,128)(2,1)S(1)}, bf16[1,128,512]{2,1,0:T(8,128)(2,1)S(1)}, u32[]{:S(2)}, u32[]{:S(2)}) collective-permute-start(bf16[1,128,512]{2,1,0:T(8,128)(2,1)S(1)} %get-tuple-element.23), channel_id=1, source_target_pairs={{0,8},{2,10},{4,12},{6,14},{8,16},{10,18},{12,20},{14,22},{16,24},... | collective-permute-start | bytes 393224 | tf_op jit(solution)/shard_map/ppermute | solution.py:129
  27.2 6.5 %collective-permute-start.7 = (bf16[1,128,512]{2,1,0:T(8,128)(2,1)S(1)}, bf16[1,128,512]{2,1,0:T(8,128)(2,1)S(1)}, u32[]{:S(2)}, u32[]{:S(2)}) collective-permute-start(bf16[1,128,512]{2,1,0:T(8,128)(2,1)S(1)} %get-tuple-element.24), channel_id=1, source_target_pairs={{0,24},{2,26},{4,28},{6,30},{8,0},{10,2},{12,4},{14,6},{16,8},{18,... | collective-permute-start | bytes 393224 | tf_op jit(solution)/shard_map/ppermute | solution.py:129
  29.3 10.5 %collective-permute-start.5 = (bf16[1,128,512]{2,1,0:T(8,128)(2,1)S(1)}, bf16[1,128,512]{2,1,0:T(8,128)(2,1)S(1)}, u32[]{:S(2)}, u32[]{:S(2)}) collective-permute-start(bf16[1,128,512]{2,1,0:T(8,128)(2,1)S(1)} %get-tuple-element.25), channel_id=1, source_target_pairs={{0,16},{2,18},{4,20},{6,22},{8,24},{10,26},{12,28},{14,30},{16,0},... | collective-permute-start | bytes 393224 | tf_op jit(solution)/shard_map/ppermute | solution.py:129
  41.7 8.9 %collective-permute-start.11 = (bf16[1,128,512]{2,1,0:T(8,128)(2,1)S(1)}, bf16[1,128,512]{2,1,0:T(8,128)(2,1)S(1)}, u32[]{:S(2)}, u32[]{:S(2)}) collective-permute-start(bf16[1,128,512]{2,1,0:T(8,128)(2,1)S(1)} %get-tuple-element.16.refs_0_), channel_id=1, source_target_pairs={{0,8},{2,10},{4,12},{6,14},{8,16},{10,18},{12,20},{14,22},{16,24},... | collective-permute-start | bytes 393224 | tf_op jit(solution)/shard_map/ppermute | solution.py:129
  41.7 11.8 %collective-permute-start.10 = (bf16[1,128,512]{2,1,0:T(8,128)(2,1)S(1)}, bf16[1,128,512]{2,1,0:T(8,128)(2,1)S(1)}, u32[]{:S(2)}, u32[]{:S(2)}) collective-permute-start(bf16[1,128,512]{2,1,0:T(8,128)(2,1)S(1)} %get-tuple-element.16.refs_0_), channel_id=1, source_target_pairs={{0,16},{2,18},{4,20},{6,22},{8,24},{10,26},{12,28},{14,30},{16,0},... | collective-permute-start | bytes 393224 | tf_op jit(solution)/shard_map/ppermute | solution.py:129
  44.6 9.9 %collective-permute-start.9 = (bf16[1,128,512]{2,1,0:T(8,128)(2,1)S(1)}, bf16[1,128,512]{2,1,0:T(8,128)(2,1)S(1)}, u32[]{:S(2)}, u32[]{:S(2)}) collective-permute-start(bf16[1,128,512]{2,1,0:T(8,128)(2,1)S(1)} %get-tuple-element.16.refs_0_), channel_id=1, source_target_pairs={{0,24},{2,26},{4,28},{6,30},{8,0},{10,2},{12,4},{14,6},{16,8},{18,... | collective-permute-start | bytes 393224 | tf_op jit(solution)/shard_map/ppermute | solution.py:129
  49.1 10.5 %collective-permute-start.13 = (bf16[1,128,512]{2,1,0:T(8,128)(2,1)S(1)}, bf16[1,128,512]{2,1,0:T(8,128)(2,1)S(1)}, u32[]{:S(2)}, u32[]{:S(2)}) collective-permute-start(bf16[1,128,512]{2,1,0:T(8,128)(2,1)S(1)} %get-tuple-element.16.refs_0_), channel_id=1, source_target_pairs={{0,4},{2,6},{4,0},{6,2},{8,12},{10,14},{12,8},{14,10},{16,20},{18,... | collective-permute-start | bytes 393224 | tf_op jit(solution)/shard_map/ppermute | solution.py:129
  50.6 10.1 %collective-permute-start.16 = (bf16[1,128,512]{2,1,0:T(8,128)(2,1)S(1)}, bf16[1,128,512]{2,1,0:T(8,128)(2,1)S(1)}, u32[]{:S(2)}, u32[]{:S(2)}) collective-permute-start(bf16[1,128,512]{2,1,0:T(8,128)(2,1)S(1)} %collective-permute-done.11.refs_3_), channel_id=1, source_target_pairs={{0,4},{2,6},{4,0},{6,2},{8,12},{10,14},{12,8},{14,10},{16,20},{18,... | collective-permute-start | bytes 393224 | tf_op jit(solution)/shard_map/ppermute | solution.py:129
  53.5 7.1 %collective-permute-start.15 = (bf16[1,128,512]{2,1,0:T(8,128)(2,1)S(1)}, bf16[1,128,512]{2,1,0:T(8,128)(2,1)S(1)}, u32[]{:S(2)}, u32[]{:S(2)}) collective-permute-start(bf16[1,128,512]{2,1,0:T(8,128)(2,1)S(1)} %collective-permute-done.10.refs_2_), channel_id=1, source_target_pairs={{0,4},{2,6},{4,0},{6,2},{8,12},{10,14},{12,8},{14,10},{16,20},{18,... | collective-permute-start | bytes 393224 | tf_op jit(solution)/shard_map/ppermute | solution.py:129
  54.5 6.8 %copy-start = (bf16[1,128,512]{2,1,0:T(8,128)(2,1)}, bf16[1,128,512]{2,1,0:T(8,128)(2,1)S(1)}, u32[]{:S(2)}) copy-start(bf16[1,128,512]{2,1,0:T(8,128)(2,1)S(1)} %collective-permute-done.9.refs_1_) | copy-start | bytes 393220
  54.5 6.8 %collective-permute-start.14 = (bf16[1,128,512]{2,1,0:T(8,128)(2,1)S(1)}, bf16[1,128,512]{2,1,0:T(8,128)(2,1)}, u32[]{:S(2)}, u32[]{:S(2)}) collective-permute-start(bf16[1,128,512]{2,1,0:T(8,128)(2,1)S(1)} %collective-permute-done.9.refs_1_), channel_id=1, source_target_pairs={{0,4},{2,6},{4,0},{6,2},{8,12},{10,14},{12,8},{14,10},{16,20},{18,... | collective-permute-start | bytes 393224 | tf_op jit(solution)/shard_map/ppermute | solution.py:129
  59.6 14.1 %collective-permute-start.20 = (bf16[512,512]{1,0:T(8,128)(2,1)}, bf16[512,512]{1,0:T(8,128)(2,1)}, u32[]{:S(2)}, u32[]{:S(2)}) collective-permute-start(bf16[512,512]{1,0:T(8,128)(2,1)} %bitcast.84), channel_id=1, source_target_pairs={{0,1},{1,0},{2,3},{3,2},{4,5},{5,4},{6,7},{7,6},{8,9},{9,8},{10,11... | collective-permute-start | bytes 1572872 | tf_op jit(solution)/shard_map/ppermute | solution.py:132
  60.7 15.4 %collective-permute-start.12 = (bf16[4,128,512]{2,1,0:T(8,128)(2,1)}, bf16[4,128,512]{2,1,0:T(8,128)(2,1)S(1)}, u32[]{:S(2)}, u32[]{:S(2)}) collective-permute-start(bf16[4,128,512]{2,1,0:T(8,128)(2,1)} %pad_maximum_fusion), channel_id=1, source_target_pairs={{0,2},{2,0},{4,6},{6,4},{8,10},{10,8},{12,14},{14,12},{16,18},{18,... | collective-permute-start | bytes 1572872 | tf_op jit(solution)/shard_map/ppermute | solution.py:129
  65.0 11.0 %collective-permute-start.17 = (bf16[4,128,512]{2,1,0:T(8,128)(2,1)}, bf16[4,128,512]{2,1,0:T(8,128)(2,1)S(1)}, u32[]{:S(2)}, u32[]{:S(2)}) collective-permute-start(bf16[4,128,512]{2,1,0:T(8,128)(2,1)} %pad_maximum_fusion.1), channel_id=1, source_target_pairs={{0,2},{2,0},{4,6},{6,4},{8,10},{10,8},{12,14},{14,12},{16,18},{18,... | collective-permute-start | bytes 1572872 | tf_op jit(solution)/shard_map/ppermute | solution.py:129
  76.0 0.9 copy-start.1
  77.0 0.9 copy-start.3
  77.9 0.9 copy-start.5
  78.8 0.9 copy-start.7
  79.7 4.0 %copy-start.9 = (bf16[1,512,4096]{2,1,0:T(8,128)(2,1)S(1)}, bf16[1,512,4096]{2,1,0:T(8,128)(2,1)}, u32[]{:S(2)}) copy-start(bf16[1,512,4096]{2,1,0:T(8,128)(2,1)} %param.6) | copy-start | bytes 12582916
  82.1 3.9 %copy-start.8 = (f32[2048,512]{1,0:T(8,128)S(1)}, f32[2048,512]{1,0:T(8,128)}, u32[]{:S(2)}) copy-start(f32[2048,512]{1,0:T(8,128)} %fusion.1) | copy-start | bytes 12582916
  82.1 3.9 %copy-start.10 = (bf16[512,512]{1,0:T(8,128)(2,1)S(1)}, bf16[512,512]{1,0:T(8,128)(2,1)}, u32[]{:S(2)}) copy-start(bf16[512,512]{1,0:T(8,128)(2,1)} %turn.3) | copy-start | bytes 1572868
  82.1 14.4 %collective-permute-start.18 = (bf16[512,512]{1,0:T(8,128)(2,1)S(1)}, bf16[512,512]{1,0:T(8,128)(2,1)S(1)}, u32[]{:S(2)}, u32[]{:S(2)}) collective-permute-start(bf16[512,512]{1,0:T(8,128)(2,1)S(1)} %get-tuple-element.11), channel_id=1, source_target_pairs={{0,1},{1,0},{2,3},{3,2},{4,5},{5,4},{6,7},{7,6},{8,9},{9,8},{10,11... | collective-permute-start | bytes 1572872 | tf_op jit(solution)/shard_map/ppermute | solution.py:132
  (4 other events, 2.7 us)

commit v3 on v2

v3 whole, which is shorter than its diff:
```python
import functools
import math

import jax
import jax.numpy as jnp
from jax import lax
from jax.experimental import pallas as pl
from jax.experimental.pallas import tpu as pltpu
from jax.sharding import PartitionSpec as P

HEAD = 128
LINK = jnp.bfloat16


def factors_of(count):
    parts = []
    for size in (2, 2, 4):
        size = math.gcd(size, count)
        parts.append(size)
        count //= size
    return parts + [count]


def shift_pairs(count, stride, size, step):
    pairs = []
    for source in range(count):
        part = source // stride % size
        pairs.append((source, source + ((part + step) % size - part) * stride))
    return pairs


def picked(value, index, axis):
    return lax.dynamic_index_in_dim(value, index, axis, keepdims=False)


def total(terms):
    return sum(t.astype(jnp.float32) for t in terms)


def tables(positions):
    freqs = 500000.0 ** (-(jnp.arange(HEAD) % (HEAD // 2)).astype(jnp.float32) / (HEAD // 2))
    angles = positions.astype(jnp.float32)[:, None] * freqs[None, :]
    sign = jnp.where(jnp.arange(HEAD) < HEAD // 2, -1.0, 1.0)
    return jnp.cos(angles), jnp.sin(angles) * sign[None, :]


def after(value, *before):
    return lax.optimization_barrier((value, before))[0]


VMEM = pl.BlockSpec(memory_space=pltpu.VMEM)
PLAIN = pl.BlockSpec(memory_space=pltpu.HBM)


CHEAP = pl.CostEstimate(flops=0, bytes_accessed=0, transcendentals=0)
PARAMS = pltpu.CompilerParams(vmem_limit_bytes=24 * 1024 * 1024)


def turned(block, cosine, sine):
    return block * cosine + pltpu.roll(block, HEAD // 2, 1) * sine


def pack_kernel(
    parts, place_ref, features_ref, documents_ref, sums_ref, out_ref, core_ref, held_ref, wide_ref, half_ref, sems
):
    count, depth = features_ref.shape[0], out_ref.shape[1]
    fast, band = sums_ref.shape[1], sums_ref.shape[2]
    blocks = sums_ref.shape[0]
    at = pl.ds(pl.multiple_of(place_ref[0] * depth, depth), depth)
    ins, outs, wide, half = [], [], [], []
    for i in range(blocks):
        wide.append(
            pltpu.make_async_copy(sums_ref.at[i, place_ref[1]], wide_ref.at[i], sems.at[2, i])
        )
        half.append(pltpu.make_async_copy(half_ref.at[i], core_ref.at[i], sems.at[3, i]))
        wide[-1].start()
    for i in range(parts):
        rows = pl.ds(i * (count // parts), count // parts)
        ins.append(
            pltpu.make_async_copy(features_ref.at[rows, at], held_ref.at[rows, :], sems.at[0, i])
        )
        outs.append(pltpu.make_async_copy(held_ref.at[rows, :], out_ref.at[rows, :], sems.at[1, i]))
        ins[-1].start()
    rows = pl.ds(count, out_ref.shape[0] - count)
    held_ref[rows, :] = jnp.zeros((rows.size, depth), out_ref.dtype)
    held_ref[rows, pl.ds(0, count)] = jnp.broadcast_to(
        documents_ref[...].astype(jnp.float32).astype(out_ref.dtype), (rows.size, count)
    )
    outs.append(pltpu.make_async_copy(held_ref.at[rows, :], out_ref.at[rows, :], sems.at[1, parts]))
    outs[-1].start()
    for i in range(blocks):
        wide[i].wait()
        half_ref[i] = wide_ref[i].astype(half_ref.dtype)
        half[i].start()
    for i in range(parts):
        ins[i].wait()
        outs[i].start()
    for copy in half + outs:
        copy.wait()


def pack(place, features, documents, sums, depth, parts=8, note=16):
    shape = (features.shape[0] + note, depth)
    blocks, _, band, columns = sums.shape
    plain = pl.BlockSpec(memory_space=pltpu.HBM)
    return pl.pallas_call(
        functools.partial(pack_kernel, parts),
        in_specs=[pl.BlockSpec(memory_space=pltpu.SMEM), plain, VMEM, plain],
        out_specs=[plain, plain],
        out_shape=[
            jax.ShapeDtypeStruct(shape, features.dtype),
            jax.ShapeDtypeStruct((blocks, band, columns), LINK),
        ],
        scratch_shapes=[
            pltpu.VMEM(shape, features.dtype),
            pltpu.VMEM((blocks, band, columns), sums.dtype),
            pltpu.VMEM((blocks, band, columns), LINK),
            pltpu.SemaphoreType.DMA((4, max(parts + 1, blocks))),
        ],
        compiler_params=pltpu.CompilerParams(vmem_limit_bytes=60 * 1024 * 1024),
        cost_estimate=CHEAP,
        name="pack",
    )(place, features, documents, sums)


def turn_into(out_ref, start, value, cosine, sine):
    for head in range(value.shape[1] // HEAD):
        block = value[:, head * HEAD : (head + 1) * HEAD].astype(jnp.float32)
        block = turned(block, cosine, -sine).astype(out_ref.dtype)
        out_ref[pl.ds(start, value.shape[0]), pl.ds(head * HEAD, HEAD)] = block


def gradient_kernel(side_ref, own_ref, value_ref, cosine_ref, sine_ref, *refs):
    out_ref, rotated_ref = refs[-2:]
    others = [refs[i : i + 4] for i in range(0, len(refs) - 2, 4)]
    count, columns = value_ref.shape

    @pl.when(pl.program_id(0) == 0)
    def _():
        turn_into(rotated_ref, 0, value_ref[...], cosine_ref[...], sine_ref[...])
        for i, (_, value, cosine, sine) in enumerate(others):
            turn_into(rotated_ref, (i + 1) * count, value[...], cosine[...], sine[...])

    tiles = [own_ref[...]] + [ref[...] for other in others for ref in other[:1]]
    out_ref[...] = lax.dot_general(
        jnp.concatenate(tiles, axis=0),
        rotated_ref[...],
        (((0,), (0,)), ((), ())),
        preferred_element_type=jnp.float32,
    ).astype(out_ref.dtype)


def gradient(side, features, value, tables_, others, depth, tile=256):
    count, columns = value.shape
    tiles = depth // tile
    table = pl.BlockSpec((count, HEAD), lambda i, side: (0, 0))
    specs, operands = [], []
    for other in others:
        specs += [
            pl.BlockSpec((count, tile), lambda i, side: (0, i)),
            pl.BlockSpec((count, columns), lambda i, side: (0, 0)),
            table,
            table,
        ]
        operands += other
    return pl.pallas_call(
        gradient_kernel,
        grid_spec=pltpu.PrefetchScalarGridSpec(
            num_scalar_prefetch=1,
            grid=(tiles,),
            in_specs=[
                pl.BlockSpec((count, tile), lambda i, side: (0, side[0] * tiles + i)),
                pl.BlockSpec((count, columns), lambda i, side: (0, 0)),
                table,
                table,
            ]
            + specs,
            out_specs=pl.BlockSpec((tile, columns), lambda i, side: (i, 0)),
            scratch_shapes=[pltpu.VMEM(((len(others) + 1) * count, columns), jnp.bfloat16)],
        ),
        out_shape=jax.ShapeDtypeStruct((depth, columns), jnp.bfloat16),
        compiler_params=PARAMS,
        cost_estimate=CHEAP,
        name="gradient",
    )(side, features, value, *tables_, *operands)


def rotated_into(out_ref, product, cosine_ref, sine_ref):
    cosine, sine = cosine_ref[...], sine_ref[...]
    for head in range(product.shape[1] // HEAD):
        block = product[:, head * HEAD : (head + 1) * HEAD]
        out_ref[:, pl.ds(head * HEAD, HEAD)] = turned(block, cosine, sine).astype(out_ref.dtype)


def product_kernel(side_ref, part_ref, weights_ref, cosine_ref, sine_ref, out_ref, sum_ref):
    at = pl.program_id(0)
    tile = jnp.dot(part_ref[...], weights_ref[...], preferred_element_type=jnp.float32)

    @pl.when(at == 0)
    def _():
        sum_ref[...] = tile

    @pl.when(at > 0)
    def _():
        sum_ref[...] += tile

    @pl.when(at == pl.num_programs(0) - 1)
    def _():
        rotated_into(out_ref, sum_ref[...], cosine_ref, sine_ref)


def product(side, part, weights, cosine, sine, kind, tile=512):
    depth, columns = weights.shape
    tiles, count = depth // tile, cosine.shape[0]
    table = pl.BlockSpec((count, HEAD), lambda i, side: (0, 0))
    return pl.pallas_call(
        product_kernel,
        grid_spec=pltpu.PrefetchScalarGridSpec(
            num_scalar_prefetch=1,
            grid=(tiles,),
            in_specs=[
                pl.BlockSpec((count, tile), lambda i, side: (0, side[0] * tiles + i)),
                pl.BlockSpec((tile, columns), lambda i, side: (i, 0)),
                table,
                table,
            ],
            out_specs=pl.BlockSpec((count, columns), lambda i, side: (0, 0)),
            scratch_shapes=[pltpu.VMEM((count, columns), jnp.float32)],
        ),
        out_shape=jax.ShapeDtypeStruct((count, columns), kind),
        compiler_params=PARAMS,
        cost_estimate=CHEAP,
        name="product",
    )(side, part, weights, cosine, sine)


def project_kernel(count, place_ref, part_ref, cosine_ref, sine_ref, *refs):
    bands, (out_ref, weights_ref, held_ref, sems, part_sems) = refs[:count], refs[count:]
    copies = []
    for ref in bands:
        for i in range(ref.shape[0]):
            rows, at = ref.shape[1], len(copies)
            start = pl.multiple_of(place_ref[at] * rows, rows)
            to = weights_ref.at[pl.ds(start, rows), :]
            copies.append(pltpu.make_async_copy(ref.at[i], to, sems.at[at]))
            copies[-1].start()
    tiles = part_sems.shape[0]
    tile = part_ref.shape[1] // tiles
    parts = []
    rows = pl.ds(0, held_ref.shape[0])
    for i in range(tiles):
        at = pl.ds(i * tile, tile)
        parts.append(
            pltpu.make_async_copy(part_ref.at[rows, at], held_ref.at[:, at], part_sems.at[i])
        )
        parts[-1].start()
    for copy in copies:
        copy.wait()
    product = jnp.zeros(out_ref.shape, jnp.float32)
    for i in range(tiles):
        parts[i].wait()
        at = pl.ds(i * tile, tile)
        product += jnp.dot(
            held_ref[:, at], weights_ref[at, :], preferred_element_type=jnp.float32
        )
    rotated_into(out_ref, product, cosine_ref, sine_ref)


def project(places, part, cosine, sine, bands, tiles=4):
    rows = sum(b.shape[0] * b.shape[1] for b in bands)
    columns = bands[0].shape[2]
    return pl.pallas_call(
        functools.partial(project_kernel, len(bands)),
        in_specs=[pl.BlockSpec(memory_space=pltpu.SMEM), PLAIN, VMEM, VMEM] + [PLAIN] * len(bands),
        out_specs=[VMEM, VMEM],
        out_shape=[
            jax.ShapeDtypeStruct((cosine.shape[0], columns), LINK),
            jax.ShapeDtypeStruct((rows, columns), LINK),
        ],
        scratch_shapes=[
            pltpu.VMEM((cosine.shape[0], rows), part.dtype),
            pltpu.SemaphoreType.DMA((places.shape[0],)),
            pltpu.SemaphoreType.DMA((tiles,)),
        ],
        compiler_params=PARAMS,
        cost_estimate=CHEAP,
        name="project",
    )(places, part, cosine, sine, *bands)


def local(tokens, cotangent, doc_ids, pseudo_grads, master, momentum):
    reps = lax.axis_size("rep")
    pair = lax.axis_size("fsdp")
    rep = lax.axis_index("rep")
    side = lax.axis_index("fsdp")
    parts = factors_of(reps)
    strides = [math.prod(parts[:i]) for i in range(len(parts))]
    place = [rep // stride % size for stride, size in zip(strides, parts)]
    band, columns = master.shape[1:]
    features = tokens[0]
    count, width = features.shape
    depth = width // pair

    def moved(value, level, step):
        pairs = shift_pairs(reps, strides[level], parts[level], step)
        return lax.ppermute(value, "rep", pairs)

    def across(value, step):
        return lax.ppermute(value, "fsdp", shift_pairs(pair, 1, pair, step))

    def half_of(step):
        return lax.dynamic_slice_in_dim(features, (side + step) % pair * depth, depth, 1)

    fast, middle, slow, rest = parts
    mine = pseudo_grads[0].reshape(rest, slow, middle, fast, band, columns)
    order = sorted(range(slow), key=lambda k: -min(k, slow - k))

    documents = doc_ids[0]
    which = side.astype(jnp.int32).reshape(1)
    bands = pseudo_grads[0].reshape(-1, fast, band, columns)
    sent, out = [], []
    for step in range(1, max(pair, fast)):
        goes = jnp.stack([(side + step) % pair, (place[0] + step) % fast]).astype(jnp.int32)
        one, two = pack(goes, features, doc_ids, bands, depth)
        sent += [one] if step < pair else []
        out += [two.reshape(rest, slow, middle, band, columns)] if step < fast else []
    parted = [None] + [across(t, i + 1) for i, t in enumerate(sent)][::-1]

    cores = [moved(t, 0, i + 1) for i, t in enumerate(out)]

    def piece(k, step):
        terms = [picked(mine, place[0], 3)] + cores
        terms = [picked(t, (place[2] + k) % slow, 1) for t in terms]
        return [picked(t, (place[1] + step) % middle, 1) for t in terms]

    out = {k: [total(piece(k, i)).astype(LINK) for i in range(1, middle)] for k in order}
    sums = {k: [moved(t, 1, i + 1) for i, t in enumerate(out[k])] for k in order}
    last = out
    received = []
    for k in order:
        if k:
            out = total(piece(k, 0) + after(sums[k], last)).astype(LINK)
            last = out
            received.append(moved(out, 2, k))
        else:
            received = piece(k, 0) + sums[k] + received
    here = [picked(t, place[3], 0) for t in received]
    for step in range(1, rest):
        chosen = total([picked(t, (place[3] + step) % rest, 0) for t in received])
        here.append(moved(chosen.astype(LINK), 3, step))
    upstream = after(cotangent[0], last)
    upstream = [None] + [across(upstream, pair - step) for step in range(1, pair)]

    def updated(delta):
        new_momentum = 0.9 * momentum[0] + delta
        return master[0] - 0.7 * (delta + 0.9 * new_momentum), new_momentum

    outer_delta = total(here) / reps

    held = updated(outer_delta)[0].astype(LINK)[None]
    held = jnp.concatenate([held] + [moved(held, 3, rest - k) for k in range(1, rest)])
    outer = [(place[3] + k) % rest * strides[3] for k in range(rest)]
    order = sorted(range(slow), key=lambda k: min(k, slow - k))
    slows = {k: held if k == 0 else moved(held, 2, slow - k) for k in order}
    crossed = {
        (k, shift): moved(slows[k], 1, middle - shift) for shift in range(1, middle) for k in order
    }
    near = [key for key in crossed if key[0] != order[-1]]
    last = [key for key in crossed if key[0] == order[-1]]
    groups = [[(k, 0) for k in order], near + last]
    crossed.update({(k, 0): slows[k] for k in order})
    bands, places = [], []
    for keys in groups:
        if not keys:
            continue
        group = [crossed[key] for key in keys]
        base = [
            o + (place[2] + k) % slow * strides[2] + (place[1] + shift) % middle * strides[1]
            for k, shift in keys
            for o in outer
        ]
        joined = group[0] if len(group) == 1 else jnp.concatenate(group)
        bands += group
        places += [spot + place[0] for spot in base]
        for step in range(1, fast):
            bands.append(moved(joined, 0, fast - step))
            places += [spot + (place[0] + step) % fast for spot in base]
    places = jnp.stack(places)

    early = [documents] + [
        part[count, :count].astype(jnp.int32) for part in parted[1:]
    ]
    turns = []
    for step, docs in enumerate(early):
        at = (side + step) % pair * count + jnp.arange(count, dtype=jnp.int32)
        for others in early:
            at = at - jnp.sum((others[None, :] < docs[:, None]).astype(jnp.int32), axis=1)
        turns.append(tables(at))

    weights = None
    other = []
    none = jnp.zeros((1,), jnp.int32)
    for step in range(1, pair):
        if weights is None:
            out, weights = project(places, parted[step], *turns[step], bands)
        else:
            out = product(none, parted[step], weights, *turns[step], LINK)
        other.append(across(out, pair - step))
    features = after(features, weights)
    grads = gradient(
        which,
        features,
        cotangent[0],
        turns[0],
        [(parted[step], upstream[step], *turns[step]) for step in range(1, pair)],
        depth,
    )
    keys = total([product(which, features, weights, *turns[0], jnp.float32)] + other)
    keys = keys.astype(jnp.bfloat16)
    new_master, new_momentum = updated(after(outer_delta, weights))
    return (
        new_master[None],
        new_momentum[None],
        keys[None],
        grads[None],
    )


def solution(mesh):
    return jax.shard_map(
        local,
        mesh=mesh,
        in_specs=(
            P("rep", "fsdp", None),
            P("rep", "fsdp", None),
            P("rep", "fsdp"),
            P("rep", "fsdp", None),
            P("fsdp", "rep", None),
            P("fsdp", "rep", None),
        ),
        out_specs=(
            P("fsdp", "rep", None),
            P("fsdp", "rep", None),
            P("rep", "fsdp", None),
            P("rep", "fsdp", None),
        ),
        check_vma=False,
    )
```

time: 100 us -> 80.3 us (0.80)
  local copies, waits for them, and re-layouts: 12.4 us -> 0.16 us
  waiting for transfers between devices: 27.3 us -> 16.7 us
  matrix products: 9.94 us -> 0 us
  Pallas kernels: 9.71 us -> 18.8 us
  starting transfers between devices: 23.9 us -> 30.4 us
  other arithmetic: 16 us -> 12.9 us
    dot_general x3 -> x0, matrix products: 9.94 us -> none  [the longest x2 7.66 us: local(): lax.dot_general(part, rotated, (((0,), (0,)), ((), ())), preferred_elemen...]
    concatenate x6 -> x2, other arithmetic: 8.1 us -> 0.14 us  [local(): joined = group[0] if len(group) == 1 else jnp.concatenate(group)]
    unnamed x30 -> x24, local copies, waits for them, and re-layouts: 6.37 us -> 0.07 us
    ppermute x17, waiting for transfers between devices: 19.5 us -> 13.4 us  [moved(): return lax.ppermute(value, 'rep', pairs)]
    pallas_call x3, Pallas kernels: 7.27 us -> 13.2 us  [the longest x1 6.14 us: gradient(): pl.pallas_call(gradient_kernel, grid_spec=pltpu.PrefetchScalarGridSpec(nu...]
    ppermute x17, starting transfers between devices: 18.6 us -> 24.2 us  [moved(): return lax.ppermute(value, 'rep', pairs)]
    ppermute x4 -> x3, waiting for transfers between devices: 7.83 us -> 3.29 us  [across(): return lax.ppermute(value, 'fsdp', shift_pairs(pair, 1, pair, step))]
    pallas_call x1, Pallas kernels: 2.44 us -> 5.64 us  [project(): pl.pallas_call(functools.partial(project_kernel, len(bands)), in_specs=[p...]
  transfers between devices with their start and end apart: 21 -> 20, of which waited for: 9 -> 10; matrix products, arithmetic and copies ran while one was open for 26% -> 14% of each run, Pallas kernels for 5% -> 18%
where the time goes in v3:
time: 80.3 us; the launch traced here: 80 us
  starting transfers between devices  30.4 us (38%)
  Pallas kernels  18.8 us (23%)
  waiting for transfers between devices  16.7 us (21%)
  other arithmetic  12.9 us (16%)
  between operations  0.93 us (1%)
    ppermute x17, starting transfers between devices, moved(): return lax.ppermute(value, 'rep', pairs)  24.2 us
    ppermute x17, waiting for transfers between devices, moved(): return lax.ppermute(value, 'rep', pairs)  13.4 us
    ppermute x3, starting transfers between devices, across(): return lax.ppermute(value, 'fsdp', shift_pairs(pair, 1, pair, step))  6.2 us
    pallas_call x1, Pallas kernels, gradient(): pl.pallas_call(gradient_kernel, grid_spec=pltpu.PrefetchScalarGridSpec(nu...  6.14 us
    pallas_call x1, Pallas kernels, project(): pl.pallas_call(functools.partial(project_kernel, len(bands)), in_specs=[p...  5.64 us
    pallas_call x1, Pallas kernels, pack(): pl.pallas_call(functools.partial(pack_kernel, parts), in_specs=[pl.BlockS...  4.32 us
    ppermute x3, waiting for transfers between devices, across(): return lax.ppermute(value, 'fsdp', shift_pairs(pair, 1, pair, step))  3.29 us
    convert_element_type x3, other arithmetic, local(): out = total(piece(k, 0) + after(sums[k], last)).astype(LINK)  3.06 us
  transfers between devices with their start and end apart: 20, of which 10 were waited for; matrix products, arithmetic and copies ran while one was open for 14% of the time, Pallas kernels for 18%

profile of v3, /device:TPU:0, one launch (start us, length us, event | category | flops | bytes accessed | tf_op | source)
XLA Modules:
  0.0 80.0 jit_solution(10837941956606464075)
XLA Ops:
  1.2 4.3 %pack.1 = (bf16[528,2048]{1,0:T(8,128)(2,1)}, bf16[8,128,512]{2,1,0:T(8,128)(2,1)}) custom-call(s32[2]{0:T(128)} %pad_add_fusion.place_ref, bf16[512,4096]{1,0:T(8,128)(2,1)} %bitcast.130, s32[1,512]{1,0:T(1,128)} %documents_ref.1, f32[8,2,128,512]{3,2,1,0:T(8,128)} %bitcast.135), custom_call_target="tpu_custom_call" | custom-call | tf_op jit(solution)/shard_map/pack/pallas_call | solution.py:106
  6.1 2.6 %collective-permute-start.8 = (bf16[528,2048]{1,0:T(8,128)(2,1)}, bf16[528,2048]{1,0:T(8,128)(2,1)S(1)}, u32[]{:S(2)}, u32[]{:S(2)}) collective-permute-start(bf16[528,2048]{1,0:T(8,128)(2,1)} %get-tuple-element.18), channel_id=1, source_target_pairs={{0,1},{1,0},{2,3},{3,2},{4,5},{5,4},{6,7},{7,6},{8,9},{9,8},{10,11... | collective-permute-start | bytes 6488072 | tf_op jit(solution)/shard_map/ppermute | solution.py:309
  8.7 2.4 %fusion.15 = (bf16[1,128,512]{2,1,0:T(8,128)(2,1)}, bf16[1,128,512]{2,1,0:T(8,128)(2,1)}, bf16[1,128,512]{2,1,0:T(8,128)(2,1)}, bf16[1,128,512]{2,1,0:T(8,128)(2,1)S(1)}) fusion(f32[1,4,2,2,128,512]{5,4,3,2,1,0:T(8,128)} %bitcast.136, s32[]{:T(128)S(6)} %select_n.298, s32[]{:T(128)S(6)} %select_n.289, s32[]{:T(128)S(6)} %select_n.284, ...), kind=kLoop, calls=%fused_computation.39 | loop fusion | flops 786432 | bytes 2097176 | tf_op jit(solution)/shard_map/convert_element_type | solution.py:336
  11.1 2.8 %collective-permute-start.2 = (bf16[1,128,512]{2,1,0:T(8,128)(2,1)}, bf16[1,128,512]{2,1,0:T(8,128)(2,1)}, u32[]{:S(2)}, u32[]{:S(2)}) collective-permute-start(bf16[1,128,512]{2,1,0:T(8,128)(2,1)} %get-tuple-element.30), channel_id=1, source_target_pairs={{0,4},{2,6},{4,0},{6,2},{8,12},{10,14},{12,8},{14,10},{16,20},{18,... | collective-permute-start | bytes 393224 | tf_op jit(solution)/shard_map/ppermute | solution.py:306
  13.9 2.0 %collective-permute-start.4 = (bf16[1,128,512]{2,1,0:T(8,128)(2,1)}, bf16[1,128,512]{2,1,0:T(8,128)(2,1)S(1)}, u32[]{:S(2)}, u32[]{:S(2)}) collective-permute-start(bf16[1,128,512]{2,1,0:T(8,128)(2,1)} %get-tuple-element.29), channel_id=1, source_target_pairs={{0,4},{2,6},{4,0},{6,2},{8,12},{10,14},{12,8},{14,10},{16,20},{18,... | collective-permute-start | bytes 393224 | tf_op jit(solution)/shard_map/ppermute | solution.py:306
  15.9 2.5 %collective-permute-done.2 = bf16[1,128,512]{2,1,0:T(8,128)(2,1)} collective-permute-done((bf16[1,128,512]{2,1,0:T(8,128)(2,1)}, bf16[1,128,512]{2,1,0:T(8,128)(2,1)}, u32[]{:S(2)}, u32[]{:S(2)}) %collective-permute-start.2) | collective-permute-done | bytes 131104 | tf_op jit(solution)/shard_map/ppermute | solution.py:306
  18.5 1.1 %fusion.19 = bf16[1,128,512]{2,1,0:T(8,128)(2,1)S(1)} fusion(bf16[1,128,512]{2,1,0:T(8,128)(2,1)} %collective-permute-done.2, f32[1,4,2,2,128,512]{5,4,3,2,1,0:T(8,128)} %bitcast.137, s32[]{:T(128)S(6)} %select_n.292, s32[]{:T(128)S(6)} %select_n.281, s32[]{:T(128)S(6)} %select_n.284, bf16[1,4,2,128,512]{4,3,2,1,0:T(8,128)(2,1)S(1)} %collective-permute-done), kind=kLoop, calls=%fused_computation.46 | loop fusion | flops 327680 | bytes 655372 | tf_op jit(solution)/shard_map/convert_element_type | solution.py:342
  19.5 3.2 %collective-permute-start.3 = (bf16[1,128,512]{2,1,0:T(8,128)(2,1)S(1)}, bf16[1,128,512]{2,1,0:T(8,128)(2,1)S(1)}, u32[]{:S(2)}, u32[]{:S(2)}) collective-permute-start(bf16[1,128,512]{2,1,0:T(8,128)(2,1)S(1)} %fusion.19), channel_id=1, source_target_pairs={{0,16},{2,18},{4,20},{6,22},{8,24},{10,26},{12,28},{14,30},{16,0},... | collective-permute-start | bytes 393224 | tf_op jit(solution)/shard_map/ppermute | solution.py:306
  22.8 1.2 %collective-permute-done.4 = bf16[1,128,512]{2,1,0:T(8,128)(2,1)S(1)} collective-permute-done((bf16[1,128,512]{2,1,0:T(8,128)(2,1)}, bf16[1,128,512]{2,1,0:T(8,128)(2,1)S(1)}, u32[]{:S(2)}, u32[]{:S(2)}) %collective-permute-start.4) | collective-permute-done | bytes 131104 | tf_op jit(solution)/shard_map/ppermute | solution.py:306
  25.0 2.2 %collective-permute-start.5 = (bf16[1,128,512]{2,1,0:T(8,128)(2,1)S(1)}, bf16[1,128,512]{2,1,0:T(8,128)(2,1)S(1)}, u32[]{:S(2)}, u32[]{:S(2)}) collective-permute-start(bf16[1,128,512]{2,1,0:T(8,128)(2,1)S(1)} %fusion.14), channel_id=1, source_target_pairs={{0,8},{2,10},{4,12},{6,14},{8,16},{10,18},{12,20},{14,22},{16,24},... | collective-permute-start | bytes 393224 | tf_op jit(solution)/shard_map/ppermute | solution.py:306
  28.2 3.0 %collective-permute-start.7 = (bf16[1,128,512]{2,1,0:T(8,128)(2,1)S(1)}, bf16[1,128,512]{2,1,0:T(8,128)(2,1)S(1)}, u32[]{:S(2)}, u32[]{:S(2)}) collective-permute-start(bf16[1,128,512]{2,1,0:T(8,128)(2,1)S(1)} %fusion.12), channel_id=1, source_target_pairs={{0,24},{2,26},{4,28},{6,30},{8,0},{10,2},{12,4},{14,6},{16,8},{18,... | collective-permute-start | bytes 393224 | tf_op jit(solution)/shard_map/ppermute | solution.py:306
  31.2 1.6 %collective-permute-done.5 = bf16[1,128,512]{2,1,0:T(8,128)(2,1)S(1)} collective-permute-done((bf16[1,128,512]{2,1,0:T(8,128)(2,1)S(1)}, bf16[1,128,512]{2,1,0:T(8,128)(2,1)S(1)}, u32[]{:S(2)}, u32[]{:S(2)}) %collective-permute-start.5) | collective-permute-done | bytes 131104 | tf_op jit(solution)/shard_map/ppermute | solution.py:306
  32.8 1.4 %collective-permute-done.7 = bf16[1,128,512]{2,1,0:T(8,128)(2,1)S(1)} collective-permute-done((bf16[1,128,512]{2,1,0:T(8,128)(2,1)S(1)}, bf16[1,128,512]{2,1,0:T(8,128)(2,1)S(1)}, u32[]{:S(2)}, u32[]{:S(2)}) %collective-permute-start.7) | collective-permute-done | bytes 131104 | tf_op jit(solution)/shard_map/ppermute | solution.py:306
  34.2 1.3 %subtract_convert_fusion.refs_0_ = bf16[1,128,512]{2,1,0:T(8,128)(2,1)S(1)} fusion(f32[1,128,512]{2,1,0:T(8,128)} %param.10, bf16[1,128,512]{2,1,0:T(8,128)(2,1)S(1)} %collective-permute-done.7, bf16[1,128,512]{2,1,0:T(8,128)(2,1)S(1)} %collective-permute-done.5, bf16[1,128,512]{2,1,0:T(8,128)(2,1)S(1)} %collective-permute-done.3, ...), kind=kLoop, calls=%fused_computation.52 | loop fusion | flops 1179648 | bytes 1572876 | tf_op jit(solution)/shard_map/convert_element_type | solution.py:360
  35.5 3.8 %collective-permute-start.9 = (bf16[1,128,512]{2,1,0:T(8,128)(2,1)S(1)}, bf16[1,128,512]{2,1,0:T(8,128)(2,1)S(1)}, u32[]{:S(2)}, u32[]{:S(2)}) collective-permute-start(bf16[1,128,512]{2,1,0:T(8,128)(2,1)S(1)} %subtract_convert_fusion.refs_0_), channel_id=1, source_target_pairs={{0,24},{2,26},{4,28},{6,30},{8,0},{10,2},{12,4},{14,6},{16,8},{18,... | collective-permute-start | bytes 393224 | tf_op jit(solution)/shard_map/ppermute | solution.py:306
  40.0 1.5 %collective-permute-start.13 = (bf16[1,128,512]{2,1,0:T(8,128)(2,1)S(1)}, bf16[1,128,512]{2,1,0:T(8,128)(2,1)S(1)}, u32[]{:S(2)}, u32[]{:S(2)}) collective-permute-start(bf16[1,128,512]{2,1,0:T(8,128)(2,1)S(1)} %subtract_convert_fusion.refs_0_), channel_id=1, source_target_pairs={{0,4},{2,6},{4,0},{6,2},{8,12},{10,14},{12,8},{14,10},{16,20},{18,... | collective-permute-start | bytes 393224 | tf_op jit(solution)/shard_map/ppermute | solution.py:306
  41.5 1.8 %collective-permute-done.9.refs_1_ = bf16[1,128,512]{2,1,0:T(8,128)(2,1)S(1)} collective-permute-done((bf16[1,128,512]{2,1,0:T(8,128)(2,1)S(1)}, bf16[1,128,512]{2,1,0:T(8,128)(2,1)S(1)}, u32[]{:S(2)}, u32[]{:S(2)}) %collective-permute-start.9) | collective-permute-done | bytes 131104 | tf_op jit(solution)/shard_map/ppermute | solution.py:306
  43.3 1.4 %collective-permute-start.14 = (bf16[1,128,512]{2,1,0:T(8,128)(2,1)S(1)}, bf16[1,128,512]{2,1,0:T(8,128)(2,1)S(1)}, u32[]{:S(2)}, u32[]{:S(2)}) collective-permute-start(bf16[1,128,512]{2,1,0:T(8,128)(2,1)S(1)} %collective-permute-done.9.refs_1_), channel_id=1, source_target_pairs={{0,4},{2,6},{4,0},{6,2},{8,12},{10,14},{12,8},{14,10},{16,20},{18,... | collective-permute-start | bytes 393224 | tf_op jit(solution)/shard_map/ppermute | solution.py:306
  44.7 1.8 %collective-permute-done.10.refs_2_ = bf16[1,128,512]{2,1,0:T(8,128)(2,1)S(1)} collective-permute-done((bf16[1,128,512]{2,1,0:T(8,128)(2,1)S(1)}, bf16[1,128,512]{2,1,0:T(8,128)(2,1)S(1)}, u32[]{:S(2)}, u32[]{:S(2)}) %collective-permute-start.10) | collective-permute-done | bytes 131104 | tf_op jit(solution)/shard_map/ppermute | solution.py:306
  46.5 1.5 %collective-permute-start.15 = (bf16[1,128,512]{2,1,0:T(8,128)(2,1)S(1)}, bf16[1,128,512]{2,1,0:T(8,128)(2,1)S(1)}, u32[]{:S(2)}, u32[]{:S(2)}) collective-permute-start(bf16[1,128,512]{2,1,0:T(8,128)(2,1)S(1)} %collective-permute-done.10.refs_2_), channel_id=1, source_target_pairs={{0,4},{2,6},{4,0},{6,2},{8,12},{10,14},{12,8},{14,10},{16,20},{18,... | collective-permute-start | bytes 393224 | tf_op jit(solution)/shard_map/ppermute | solution.py:306
  48.0 1.5 %collective-permute-done.11.refs_3_ = bf16[1,128,512]{2,1,0:T(8,128)(2,1)S(1)} collective-permute-done((bf16[1,128,512]{2,1,0:T(8,128)(2,1)S(1)}, bf16[1,128,512]{2,1,0:T(8,128)(2,1)S(1)}, u32[]{:S(2)}, u32[]{:S(2)}) %collective-permute-start.11) | collective-permute-done | bytes 131104 | tf_op jit(solution)/shard_map/ppermute | solution.py:306
  49.5 1.5 %collective-permute-start.16 = (bf16[1,128,512]{2,1,0:T(8,128)(2,1)S(1)}, bf16[1,128,512]{2,1,0:T(8,128)(2,1)S(1)}, u32[]{:S(2)}, u32[]{:S(2)}) collective-permute-start(bf16[1,128,512]{2,1,0:T(8,128)(2,1)S(1)} %collective-permute-done.11.refs_3_), channel_id=1, source_target_pairs={{0,4},{2,6},{4,0},{6,2},{8,12},{10,14},{12,8},{14,10},{16,20},{18,... | collective-permute-start | bytes 393224 | tf_op jit(solution)/shard_map/ppermute | solution.py:306
  51.3 1.6 %collective-permute-start.19 = (bf16[512,512]{1,0:T(8,128)(2,1)}, bf16[512,512]{1,0:T(8,128)(2,1)S(1)}, u32[]{:S(2)}, u32[]{:S(2)}) collective-permute-start(bf16[512,512]{1,0:T(8,128)(2,1)} %bitcast.133), channel_id=1, source_target_pairs={{0,1},{1,0},{2,3},{3,2},{4,5},{5,4},{6,7},{7,6},{8,9},{9,8},{10,11... | collective-permute-start | bytes 1572872 | tf_op jit(solution)/shard_map/ppermute | solution.py:309
  52.9 1.6 %collective-permute-done.16.refs_8_ = bf16[1,128,512]{2,1,0:T(8,128)(2,1)S(1)} collective-permute-done((bf16[1,128,512]{2,1,0:T(8,128)(2,1)S(1)}, bf16[1,128,512]{2,1,0:T(8,128)(2,1)S(1)}, u32[]{:S(2)}, u32[]{:S(2)}) %collective-permute-start.16) | collective-permute-done | bytes 131104 | tf_op jit(solution)/shard_map/ppermute | solution.py:306
  54.6 2.2 %collective-permute-done.8.part_ref.refs_0_ = bf16[528,2048]{1,0:T(8,128)(2,1)S(1)} collective-permute-done((bf16[528,2048]{1,0:T(8,128)(2,1)}, bf16[528,2048]{1,0:T(8,128)(2,1)S(1)}, u32[]{:S(2)}, u32[]{:S(2)}) %collective-permute-start.8) | collective-permute-done | bytes 2162720 | tf_op jit(solution)/shard_map/ppermute | solution.py:309
  57.4 1.9 %fusion.10 = (f32[512,128]{1,0:T(8,128)S(1)}, f32[512,128]{1,0:T(8,128)S(1)}, f32[512,128]{1,0:T(8,128)S(1)}, f32[512,128]{1,0:T(8,128)S(1)}) fusion(f32[512]{0:T(512)S(1)} %get-tuple-element.40, f32[128]{0:T(128)S(1)} %get-tuple-element.42, f32[128]{0:T(128)S(1)} %get-tuple-element.43, f32[512]{0:T(512)S(1)} %get-tuple-element.41), kind=kLoop, calls=%fused_computation.31 | loop fusion | flops 262144 | bytes 1053696 | tf_op jit(solution)/shard_map/mul | solution.py:44
  59.3 5.6 %project.1 = (bf16[512,512]{1,0:T(8,128)(2,1)S(1)}, bf16[2048,512]{1,0:T(8,128)(2,1)S(1)}) custom-call(s32[16]{0:T(128)S(1)} %stack.79.place_ref, bf16[528,2048]{1,0:T(8,128)(2,1)S(1)} %collective-permute-done.8.part_ref.refs_0_, f32[512,128]{1,0:T(8,128)S(1)} %get-tuple-element.38.cosine_ref.refs_2_, f32[512,128]{1,0:T(8,128)S(1)} %get-tuple-element.39.sine_ref.refs_3_, ...), custom_call_target="tpu_custom_call" | custom-call | tf_op jit(solution)/shard_map/project/pallas_call | solution.py:272
  65.0 2.0 %collective-permute-start.18 = (bf16[512,512]{1,0:T(8,128)(2,1)S(1)}, bf16[512,512]{1,0:T(8,128)(2,1)S(1)}, u32[]{:S(2)}, u32[]{:S(2)}) collective-permute-start(bf16[512,512]{1,0:T(8,128)(2,1)S(1)} %get-tuple-element.22), channel_id=1, source_target_pairs={{0,1},{1,0},{2,3},{3,2},{4,5},{5,4},{6,7},{7,6},{8,9},{9,8},{10,11... | collective-permute-start | bytes 1572872 | tf_op jit(solution)/shard_map/ppermute | solution.py:309
  67.0 1.1 %fusion.6 = f32[128,512]{1,0:T(8,128)S(1)} fusion(bf16[1,128,512]{2,1,0:T(8,128)(2,1)S(1)} %collective-permute-done.1, bf16[1,128,512]{2,1,0:T(8,128)(2,1)S(1)} %copy-done.6, bf16[1,128,512]{2,1,0:T(8,128)(2,1)S(1)} %copy-done.8, bf16[1,128,512]{2,1,0:T(8,128)(2,1)S(1)} %copy-done.10, f32[1,4,2,2,128,512]{5,4,3,2,1,0:T(8,128)} %bitcast.141, ...), kind=kLoop, calls=%fused_computation.27 | loop fusion | flops 720896 | bytes 1179660 | tf_op jit(solution)/shard_map/div | solution.py:358
  68.1 2.7 %product.1 = f32[512,512]{1,0:T(8,128)S(1)} custom-call(s32[1]{0:T(128)} %bitcast.50.side_ref, bf16[512,4096]{1,0:T(8,128)(2,1)S(1)} %bitcast.131, bf16[2048,512]{1,0:T(8,128)(2,1)S(1)} %get-tuple-element.19.weights_ref, f32[512,128]{1,0:T(8,128)S(1)} %get-tuple-element.35.cosine_ref, f32[512,128]{1,0:T(8,128)S(1)} %get-tuple-element.34.sine_ref), custom_call_target="tpu_custom_call" | custom-call | tf_op jit(solution)/shard_map/product/pallas_call | solution.py:216
  70.9 6.1 %gradient.1 = bf16[2048,512]{1,0:T(8,128)(2,1)} custom-call(s32[1]{0:T(128)} %bitcast.50.side_ref, bf16[512,4096]{1,0:T(8,128)(2,1)S(1)} %bitcast.132, bf16[512,512]{1,0:T(8,128)(2,1)S(1)} %bitcast.134, f32[512,128]{1,0:T(8,128)S(1)} %get-tuple-element.35.cosine_ref, f32[512,128]{1,0:T(8,128)S(1)} %get-tuple-element.34.sine_ref, ...), custom_call_target="tpu_custom_call" | custom-call | tf_op jit(solution)/shard_map/gradient/pallas_call | solution.py:166
  77.9 1.1 %collective-permute-done.18 = bf16[512,512]{1,0:T(8,128)(2,1)S(1)} collective-permute-done((bf16[512,512]{1,0:T(8,128)(2,1)S(1)}, bf16[512,512]{1,0:T(8,128)(2,1)S(1)}, u32[]{:S(2)}, u32[]{:S(2)}) %collective-permute-start.18) | collective-permute-done | bytes 524320 | tf_op jit(solution)/shard_map/ppermute | solution.py:309
  (53 shorter events, 6.6 us)
Async XLA Ops:
  5.6 51.2 %copy-start.11 = (s32[1,512]{1,0:T(1,128)S(1)}, s32[1,512]{1,0:T(1,128)}, u32[]{:S(2)}) copy-start(s32[1,512]{1,0:T(1,128)} %documents_ref.1) | copy-start | bytes 6148
  5.6 3.1 %collective-permute-start = (bf16[1,4,2,128,512]{4,3,2,1,0:T(8,128)(2,1)}, bf16[1,4,2,128,512]{4,3,2,1,0:T(8,128)(2,1)S(1)}, u32[]{:S(2)}, u32[]{:S(2)}) collective-permute-start(bf16[1,4,2,128,512]{4,3,2,1,0:T(8,128)(2,1)} %bitcast.145), channel_id=1, source_target_pairs={{0,2},{2,0},{4,6},{6,4},{8,10},{10,8},{12,14},{14,12},{16,18},{18,... | collective-permute-start | bytes 3145736 | tf_op jit(solution)/shard_map/ppermute | solution.py:306
  6.1 50.7 %collective-permute-start.8 = (bf16[528,2048]{1,0:T(8,128)(2,1)}, bf16[528,2048]{1,0:T(8,128)(2,1)S(1)}, u32[]{:S(2)}, u32[]{:S(2)}) collective-permute-start(bf16[528,2048]{1,0:T(8,128)(2,1)} %get-tuple-element.18), channel_id=1, source_target_pairs={{0,1},{1,0},{2,3},{3,2},{4,5},{5,4},{6,7},{7,6},{8,9},{9,8},{10,11... | collective-permute-start | bytes 6488072 | tf_op jit(solution)/shard_map/ppermute | solution.py:309
  8.7 25.5 %copy-start.2 = (bf16[1,4,2,128,512]{4,3,2,1,0:T(8,128)(2,1)}, bf16[1,4,2,128,512]{4,3,2,1,0:T(8,128)(2,1)S(1)}, u32[]{:S(2)}) copy-start(bf16[1,4,2,128,512]{4,3,2,1,0:T(8,128)(2,1)S(1)} %collective-permute-done) | copy-start | bytes 3145732
  11.1 7.4 %collective-permute-start.2 = (bf16[1,128,512]{2,1,0:T(8,128)(2,1)}, bf16[1,128,512]{2,1,0:T(8,128)(2,1)}, u32[]{:S(2)}, u32[]{:S(2)}) collective-permute-start(bf16[1,128,512]{2,1,0:T(8,128)(2,1)} %get-tuple-element.30), channel_id=1, source_target_pairs={{0,4},{2,6},{4,0},{6,2},{8,12},{10,14},{12,8},{14,10},{16,20},{18,... | collective-permute-start | bytes 393224 | tf_op jit(solution)/shard_map/ppermute | solution.py:306
  13.9 17.3 %collective-permute-start.1 = (bf16[1,128,512]{2,1,0:T(8,128)(2,1)S(1)}, bf16[1,128,512]{2,1,0:T(8,128)(2,1)S(1)}, u32[]{:S(2)}, u32[]{:S(2)}) collective-permute-start(bf16[1,128,512]{2,1,0:T(8,128)(2,1)S(1)} %get-tuple-element.31), channel_id=1, source_target_pairs={{0,4},{2,6},{4,0},{6,2},{8,12},{10,14},{12,8},{14,10},{16,20},{18,... | collective-permute-start | bytes 393224 | tf_op jit(solution)/shard_map/ppermute | solution.py:306
  13.9 10.1 %collective-permute-start.4 = (bf16[1,128,512]{2,1,0:T(8,128)(2,1)}, bf16[1,128,512]{2,1,0:T(8,128)(2,1)S(1)}, u32[]{:S(2)}, u32[]{:S(2)}) collective-permute-start(bf16[1,128,512]{2,1,0:T(8,128)(2,1)} %get-tuple-element.29), channel_id=1, source_target_pairs={{0,4},{2,6},{4,0},{6,2},{8,12},{10,14},{12,8},{14,10},{16,20},{18,... | collective-permute-start | bytes 393224 | tf_op jit(solution)/shard_map/ppermute | solution.py:306
  15.9 11.3 %collective-permute-start.6 = (bf16[1,128,512]{2,1,0:T(8,128)(2,1)}, bf16[1,128,512]{2,1,0:T(8,128)(2,1)S(1)}, u32[]{:S(2)}, u32[]{:S(2)}) collective-permute-start(bf16[1,128,512]{2,1,0:T(8,128)(2,1)} %get-tuple-element.28), channel_id=1, source_target_pairs={{0,4},{2,6},{4,0},{6,2},{8,12},{10,14},{12,8},{14,10},{16,20},{18,... | collective-permute-start | bytes 393224 | tf_op jit(solution)/shard_map/ppermute | solution.py:306
  19.5 11.7 %collective-permute-start.3 = (bf16[1,128,512]{2,1,0:T(8,128)(2,1)S(1)}, bf16[1,128,512]{2,1,0:T(8,128)(2,1)S(1)}, u32[]{:S(2)}, u32[]{:S(2)}) collective-permute-start(bf16[1,128,512]{2,1,0:T(8,128)(2,1)S(1)} %fusion.19), channel_id=1, source_target_pairs={{0,16},{2,18},{4,20},{6,22},{8,24},{10,26},{12,28},{14,30},{16,0},... | collective-permute-start | bytes 393224 | tf_op jit(solution)/shard_map/ppermute | solution.py:306
  25.0 7.8 %collective-permute-start.5 = (bf16[1,128,512]{2,1,0:T(8,128)(2,1)S(1)}, bf16[1,128,512]{2,1,0:T(8,128)(2,1)S(1)}, u32[]{:S(2)}, u32[]{:S(2)}) collective-permute-start(bf16[1,128,512]{2,1,0:T(8,128)(2,1)S(1)} %fusion.14), channel_id=1, source_target_pairs={{0,8},{2,10},{4,12},{6,14},{8,16},{10,18},{12,20},{14,22},{16,24},... | collective-permute-start | bytes 393224 | tf_op jit(solution)/shard_map/ppermute | solution.py:306
  28.2 6.0 %collective-permute-start.7 = (bf16[1,128,512]{2,1,0:T(8,128)(2,1)S(1)}, bf16[1,128,512]{2,1,0:T(8,128)(2,1)S(1)}, u32[]{:S(2)}, u32[]{:S(2)}) collective-permute-start(bf16[1,128,512]{2,1,0:T(8,128)(2,1)S(1)} %fusion.12), channel_id=1, source_target_pairs={{0,24},{2,26},{4,28},{6,30},{8,0},{10,2},{12,4},{14,6},{16,8},{18,... | collective-permute-start | bytes 393224 | tf_op jit(solution)/shard_map/ppermute | solution.py:306
  31.2 18.3 %copy-start.5 = (bf16[1,128,512]{2,1,0:T(8,128)(2,1)}, bf16[1,128,512]{2,1,0:T(8,128)(2,1)S(1)}, u32[]{:S(2)}) copy-start(bf16[1,128,512]{2,1,0:T(8,128)(2,1)S(1)} %collective-permute-done.3) | copy-start | bytes 393220
  32.8 18.2 %copy-start.7 = (bf16[1,128,512]{2,1,0:T(8,128)(2,1)}, bf16[1,128,512]{2,1,0:T(8,128)(2,1)S(1)}, u32[]{:S(2)}) copy-start(bf16[1,128,512]{2,1,0:T(8,128)(2,1)S(1)} %collective-permute-done.5) | copy-start | bytes 393220
  34.2 16.8 %copy-start.9 = (bf16[1,128,512]{2,1,0:T(8,128)(2,1)}, bf16[1,128,512]{2,1,0:T(8,128)(2,1)S(1)}, u32[]{:S(2)}) copy-start(bf16[1,128,512]{2,1,0:T(8,128)(2,1)S(1)} %collective-permute-done.7) | copy-start | bytes 393220
  35.5 7.8 %collective-permute-start.9 = (bf16[1,128,512]{2,1,0:T(8,128)(2,1)S(1)}, bf16[1,128,512]{2,1,0:T(8,128)(2,1)S(1)}, u32[]{:S(2)}, u32[]{:S(2)}) collective-permute-start(bf16[1,128,512]{2,1,0:T(8,128)(2,1)S(1)} %subtract_convert_fusion.refs_0_), channel_id=1, source_target_pairs={{0,24},{2,26},{4,28},{6,30},{8,0},{10,2},{12,4},{14,6},{16,8},{18,... | collective-permute-start | bytes 393224 | tf_op jit(solution)/shard_map/ppermute | solution.py:306
  39.4 7.2 %collective-permute-start.10 = (bf16[1,128,512]{2,1,0:T(8,128)(2,1)S(1)}, bf16[1,128,512]{2,1,0:T(8,128)(2,1)S(1)}, u32[]{:S(2)}, u32[]{:S(2)}) collective-permute-start(bf16[1,128,512]{2,1,0:T(8,128)(2,1)S(1)} %subtract_convert_fusion.refs_0_), channel_id=1, source_target_pairs={{0,8},{2,10},{4,12},{6,14},{8,16},{10,18},{12,20},{14,22},{16,24},... | collective-permute-start | bytes 393224 | tf_op jit(solution)/shard_map/ppermute | solution.py:306
  39.4 10.2 %collective-permute-start.11 = (bf16[1,128,512]{2,1,0:T(8,128)(2,1)S(1)}, bf16[1,128,512]{2,1,0:T(8,128)(2,1)S(1)}, u32[]{:S(2)}, u32[]{:S(2)}) collective-permute-start(bf16[1,128,512]{2,1,0:T(8,128)(2,1)S(1)} %subtract_convert_fusion.refs_0_), channel_id=1, source_target_pairs={{0,16},{2,18},{4,20},{6,22},{8,24},{10,26},{12,28},{14,30},{16,0},... | collective-permute-start | bytes 393224 | tf_op jit(solution)/shard_map/ppermute | solution.py:306
  40.0 11.3 %collective-permute-start.13 = (bf16[1,128,512]{2,1,0:T(8,128)(2,1)S(1)}, bf16[1,128,512]{2,1,0:T(8,128)(2,1)S(1)}, u32[]{:S(2)}, u32[]{:S(2)}) collective-permute-start(bf16[1,128,512]{2,1,0:T(8,128)(2,1)S(1)} %subtract_convert_fusion.refs_0_), channel_id=1, source_target_pairs={{0,4},{2,6},{4,0},{6,2},{8,12},{10,14},{12,8},{14,10},{16,20},{18,... | collective-permute-start | bytes 393224 | tf_op jit(solution)/shard_map/ppermute | solution.py:306
  43.3 9.6 %collective-permute-start.14 = (bf16[1,128,512]{2,1,0:T(8,128)(2,1)S(1)}, bf16[1,128,512]{2,1,0:T(8,128)(2,1)S(1)}, u32[]{:S(2)}, u32[]{:S(2)}) collective-permute-start(bf16[1,128,512]{2,1,0:T(8,128)(2,1)S(1)} %collective-permute-done.9.refs_1_), channel_id=1, source_target_pairs={{0,4},{2,6},{4,0},{6,2},{8,12},{10,14},{12,8},{14,10},{16,20},{18,... | collective-permute-start | bytes 393224 | tf_op jit(solution)/shard_map/ppermute | solution.py:306
  46.5 6.3 %collective-permute-start.15 = (bf16[1,128,512]{2,1,0:T(8,128)(2,1)S(1)}, bf16[1,128,512]{2,1,0:T(8,128)(2,1)S(1)}, u32[]{:S(2)}, u32[]{:S(2)}) collective-permute-start(bf16[1,128,512]{2,1,0:T(8,128)(2,1)S(1)} %collective-permute-done.10.refs_2_), channel_id=1, source_target_pairs={{0,4},{2,6},{4,0},{6,2},{8,12},{10,14},{12,8},{14,10},{16,20},{18,... | collective-permute-start | bytes 393224 | tf_op jit(solution)/shard_map/ppermute | solution.py:306
  49.5 5.0 %collective-permute-start.16 = (bf16[1,128,512]{2,1,0:T(8,128)(2,1)S(1)}, bf16[1,128,512]{2,1,0:T(8,128)(2,1)S(1)}, u32[]{:S(2)}, u32[]{:S(2)}) collective-permute-start(bf16[1,128,512]{2,1,0:T(8,128)(2,1)S(1)} %collective-permute-done.11.refs_3_), channel_id=1, source_target_pairs={{0,4},{2,6},{4,0},{6,2},{8,12},{10,14},{12,8},{14,10},{16,20},{18,... | collective-permute-start | bytes 393224 | tf_op jit(solution)/shard_map/ppermute | solution.py:306
  51.1 15.9 %copy-start.6 = (bf16[1,128,512]{2,1,0:T(8,128)(2,1)S(1)}, bf16[1,128,512]{2,1,0:T(8,128)(2,1)}, u32[]{:S(2)}) copy-start(bf16[1,128,512]{2,1,0:T(8,128)(2,1)} %copy-done.5) | copy-start | bytes 393220
  51.1 15.9 %copy-start.8 = (bf16[1,128,512]{2,1,0:T(8,128)(2,1)S(1)}, bf16[1,128,512]{2,1,0:T(8,128)(2,1)}, u32[]{:S(2)}) copy-start(bf16[1,128,512]{2,1,0:T(8,128)(2,1)} %copy-done.7) | copy-start | bytes 393220
  51.2 15.9 %copy-start.10 = (bf16[1,128,512]{2,1,0:T(8,128)(2,1)S(1)}, bf16[1,128,512]{2,1,0:T(8,128)(2,1)}, u32[]{:S(2)}) copy-start(bf16[1,128,512]{2,1,0:T(8,128)(2,1)} %copy-done.9) | copy-start | bytes 393220
  51.2 16.9 %copy-start = (bf16[1,512,4096]{2,1,0:T(8,128)(2,1)S(1)}, bf16[1,512,4096]{2,1,0:T(8,128)(2,1)}, u32[]{:S(2)}) copy-start(bf16[1,512,4096]{2,1,0:T(8,128)(2,1)} %param.6) | copy-start | bytes 12582916
  51.3 19.6 %collective-permute-start.19 = (bf16[512,512]{1,0:T(8,128)(2,1)}, bf16[512,512]{1,0:T(8,128)(2,1)S(1)}, u32[]{:S(2)}, u32[]{:S(2)}) collective-permute-start(bf16[512,512]{1,0:T(8,128)(2,1)} %bitcast.133), channel_id=1, source_target_pairs={{0,1},{1,0},{2,3},{3,2},{4,5},{5,4},{6,7},{7,6},{8,9},{9,8},{10,11... | collective-permute-start | bytes 1572872 | tf_op jit(solution)/shard_map/ppermute | solution.py:309
  52.9 6.5 %collective-permute-start.12 = (bf16[4,128,512]{2,1,0:T(8,128)(2,1)S(1)}, bf16[4,128,512]{2,1,0:T(8,128)(2,1)S(1)}, u32[]{:S(2)}, u32[]{:S(2)}) collective-permute-start(bf16[4,128,512]{2,1,0:T(8,128)(2,1)S(1)} %pad_maximum_fusion), channel_id=1, source_target_pairs={{0,2},{2,0},{4,6},{6,4},{8,10},{10,8},{12,14},{14,12},{16,18},{18,... | collective-permute-start | bytes 1572872 | tf_op jit(solution)/shard_map/ppermute | solution.py:306
  54.6 4.8 %collective-permute-start.17 = (bf16[4,128,512]{2,1,0:T(8,128)(2,1)S(1)}, bf16[4,128,512]{2,1,0:T(8,128)(2,1)S(1)}, u32[]{:S(2)}, u32[]{:S(2)}) collective-permute-start(bf16[4,128,512]{2,1,0:T(8,128)(2,1)S(1)} %pad_maximum_fusion.1), channel_id=1, source_target_pairs={{0,2},{2,0},{4,6},{6,4},{8,10},{10,8},{12,14},{14,12},{16,18},{18,... | collective-permute-start | bytes 1572872 | tf_op jit(solution)/shard_map/ppermute | solution.py:306
  65.0 14.0 %collective-permute-start.18 = (bf16[512,512]{1,0:T(8,128)(2,1)S(1)}, bf16[512,512]{1,0:T(8,128)(2,1)S(1)}, u32[]{:S(2)}, u32[]{:S(2)}) collective-permute-start(bf16[512,512]{1,0:T(8,128)(2,1)S(1)} %get-tuple-element.22), channel_id=1, source_target_pairs={{0,1},{1,0},{2,3},{3,2},{4,5},{5,4},{6,7},{7,6},{8,9},{9,8},{10,11... | collective-permute-start | bytes 1572872 | tf_op jit(solution)/shard_map/ppermute | solution.py:309
  68.1 2.8 %copy-start.1 = (bf16[1,512,512]{2,1,0:T(8,128)(2,1)S(1)}, bf16[1,512,512]{2,1,0:T(8,128)(2,1)}, u32[]{:S(2)}) copy-start(bf16[1,512,512]{2,1,0:T(8,128)(2,1)} %param.7) | copy-start | bytes 1572868
  70.8 6.2 %copy-start.3 = (f32[1,128,512]{2,1,0:T(8,128)S(1)}, f32[1,128,512]{2,1,0:T(8,128)}, u32[]{:S(2)}) copy-start(f32[1,128,512]{2,1,0:T(8,128)} %param.11) | copy-start | bytes 786436
  70.8 6.2 %copy-start.4 = (f32[1,128,512]{2,1,0:T(8,128)S(1)}, f32[1,128,512]{2,1,0:T(8,128)}, u32[]{:S(2)}) copy-start(f32[1,128,512]{2,1,0:T(8,128)} %param.10) | copy-start | bytes 786436

commit v4 on v3

--- a/solution.py
+++ b/solution.py
@@ -61,51 +61,60 @@
 
 
 def pack_kernel(
-    parts, place_ref, features_ref, documents_ref, sums_ref, out_ref, core_ref, held_ref, wide_ref, half_ref, sems
+    step, sides, features_ref, documents_ref, sums_ref, out_ref, core_ref, held_ref, wide_ref, half_ref, sems
 ):
-    count, depth = features_ref.shape[0], out_ref.shape[1]
-    fast, band = sums_ref.shape[1], sums_ref.shape[2]
-    blocks = sums_ref.shape[0]
-    at = pl.ds(pl.multiple_of(place_ref[0] * depth, depth), depth)
+    count, columns = features_ref.shape[0], out_ref.shape[1]
+    blocks, fast = sums_ref.shape[:2]
+    groups = out_ref.shape[0] // count
+    side = lax.rem(lax.axis_index("fsdp") + step, sides)
+    core = lax.rem(lax.axis_index("rep") + step, fast)
     ins, outs, wide, half = [], [], [], []
-    for i in range(blocks):
-        wide.append(
-            pltpu.make_async_copy(sums_ref.at[i, place_ref[1]], wide_ref.at[i], sems.at[2, i])
-        )
-        half.append(pltpu.make_async_copy(half_ref.at[i], core_ref.at[i], sems.at[3, i]))
-        wide[-1].start()
-    for i in range(parts):
-        rows = pl.ds(i * (count // parts), count // parts)
+    for i in range(groups):
+        at = pl.ds(pl.multiple_of((side * groups + i) * columns, columns), columns)
+        rows = pl.ds(i * count, count)
         ins.append(
-            pltpu.make_async_copy(features_ref.at[rows, at], held_ref.at[rows, :], sems.at[0, i])
+            pltpu.make_async_copy(features_ref.at[:, at], held_ref.at[rows, :], sems.at[0, i])
         )
         outs.append(pltpu.make_async_copy(held_ref.at[rows, :], out_ref.at[rows, :], sems.at[1, i]))
-        ins[-1].start()
-    rows = pl.ds(count, out_ref.shape[0] - count)
-    held_ref[rows, :] = jnp.zeros((rows.size, depth), out_ref.dtype)
+    for i in range(blocks):
+        wide.append(pltpu.make_async_copy(sums_ref.at[i, core], wide_ref.at[i], sems.at[2, i]))
+        half.append(pltpu.make_async_copy(half_ref.at[i], core_ref.at[i], sems.at[3, i]))
+    for copy in wide + ins:
+        copy.start()
+    rows = pl.ds(groups * count, out_ref.shape[0] - groups * count)
+    held_ref[rows, :] = jnp.zeros((rows.size, columns), out_ref.dtype)
     held_ref[rows, pl.ds(0, count)] = jnp.broadcast_to(
         documents_ref[...].astype(jnp.float32).astype(out_ref.dtype), (rows.size, count)
     )
-    outs.append(pltpu.make_async_copy(held_ref.at[rows, :], out_ref.at[rows, :], sems.at[1, parts]))
+    outs.append(pltpu.make_async_copy(held_ref.at[rows, :], out_ref.at[rows, :], sems.at[1, groups]))
     outs[-1].start()
-    for i in range(blocks):
-        wide[i].wait()
-        half_ref[i] = wide_ref[i].astype(half_ref.dtype)
-        half[i].start()
-    for i in range(parts):
-        ins[i].wait()
-        outs[i].start()
+
+    def move_bands():
+        for i in range(blocks):
+            wide[i].wait()
+            half_ref[i] = wide_ref[i].astype(half_ref.dtype)
+            half[i].start()
+
+    def move_tokens():
+        for i in range(groups):
+            ins[i].wait()
+            outs[i].start()
+
+    move_bands()
+    move_tokens()
     for copy in half + outs:
         copy.wait()
 
 
-def pack(place, features, documents, sums, depth, parts=8, note=16):
-    shape = (features.shape[0] + note, depth)
+def pack(step, sides, features, documents, sums, note=16):
     blocks, _, band, columns = sums.shape
+    count, width = features.shape
+    groups = width // sides // columns
+    shape = (groups * count + note, columns)
     plain = pl.BlockSpec(memory_space=pltpu.HBM)
     return pl.pallas_call(
-        functools.partial(pack_kernel, parts),
-        in_specs=[pl.BlockSpec(memory_space=pltpu.SMEM), plain, VMEM, plain],
+        functools.partial(pack_kernel, step, sides),
+        in_specs=[plain, VMEM, plain],
         out_specs=[plain, plain],
         out_shape=[
             jax.ShapeDtypeStruct(shape, features.dtype),
@@ -115,12 +124,12 @@
             pltpu.VMEM(shape, features.dtype),
             pltpu.VMEM((blocks, band, columns), sums.dtype),
             pltpu.VMEM((blocks, band, columns), LINK),
-            pltpu.SemaphoreType.DMA((4, max(parts + 1, blocks))),
+            pltpu.SemaphoreType.DMA((4, max(groups + 1, blocks))),
         ],
         compiler_params=pltpu.CompilerParams(vmem_limit_bytes=60 * 1024 * 1024),
         cost_estimate=CHEAP,
         name="pack",
-    )(place, features, documents, sums)
+    )(features, documents, sums)
 
 
 def turn_into(out_ref, start, value, cosine, sine):
@@ -152,12 +161,12 @@
 
 def gradient(side, features, value, tables_, others, depth, tile=256):
     count, columns = value.shape
-    tiles = depth // tile
+    tiles, wide = depth // tile, columns // tile
     table = pl.BlockSpec((count, HEAD), lambda i, side: (0, 0))
     specs, operands = [], []
     for other in others:
         specs += [
-            pl.BlockSpec((count, tile), lambda i, side: (0, i)),
+            pl.BlockSpec((count, tile), lambda i, side: (i // wide, i % wide)),
             pl.BlockSpec((count, columns), lambda i, side: (0, 0)),
             table,
             table,
@@ -245,13 +254,12 @@
             copies.append(pltpu.make_async_copy(ref.at[i], to, sems.at[at]))
             copies[-1].start()
     tiles = part_sems.shape[0]
-    tile = part_ref.shape[1] // tiles
+    count, tile = out_ref.shape
     parts = []
-    rows = pl.ds(0, held_ref.shape[0])
     for i in range(tiles):
-        at = pl.ds(i * tile, tile)
+        rows = pl.ds(i * count, count)
         parts.append(
-            pltpu.make_async_copy(part_ref.at[rows, at], held_ref.at[:, at], part_sems.at[i])
+            pltpu.make_async_copy(part_ref.at[rows, :], held_ref.at[rows, :], part_sems.at[i])
         )
         parts[-1].start()
     for copy in copies:
@@ -259,26 +267,28 @@
     product = jnp.zeros(out_ref.shape, jnp.float32)
     for i in range(tiles):
         parts[i].wait()
-        at = pl.ds(i * tile, tile)
         product += jnp.dot(
-            held_ref[:, at], weights_ref[at, :], preferred_element_type=jnp.float32
+            held_ref[pl.ds(i * count, count), :],
+            weights_ref[pl.ds(i * tile, tile), :],
+            preferred_element_type=jnp.float32,
         )
     rotated_into(out_ref, product, cosine_ref, sine_ref)
 
 
-def project(places, part, cosine, sine, bands, tiles=4):
+def project(places, part, cosine, sine, bands):
     rows = sum(b.shape[0] * b.shape[1] for b in bands)
-    columns = bands[0].shape[2]
+    count, columns = cosine.shape[0], bands[0].shape[2]
+    tiles = rows // columns
     return pl.pallas_call(
         functools.partial(project_kernel, len(bands)),
         in_specs=[pl.BlockSpec(memory_space=pltpu.SMEM), PLAIN, VMEM, VMEM] + [PLAIN] * len(bands),
         out_specs=[VMEM, VMEM],
         out_shape=[
-            jax.ShapeDtypeStruct((cosine.shape[0], columns), LINK),
+            jax.ShapeDtypeStruct((count, columns), LINK),
             jax.ShapeDtypeStruct((rows, columns), LINK),
         ],
         scratch_shapes=[
-            pltpu.VMEM((cosine.shape[0], rows), part.dtype),
+            pltpu.VMEM((tiles * count, columns), part.dtype),
             pltpu.SemaphoreType.DMA((places.shape[0],)),
             pltpu.SemaphoreType.DMA((tiles,)),
         ],
@@ -320,8 +330,7 @@
     bands = pseudo_grads[0].reshape(-1, fast, band, columns)
     sent, out = [], []
     for step in range(1, max(pair, fast)):
-        goes = jnp.stack([(side + step) % pair, (place[0] + step) % fast]).astype(jnp.int32)
-        one, two = pack(goes, features, doc_ids, bands, depth)
+        one, two = pack(step, pair, features, doc_ids, bands)
         sent += [one] if step < pair else []
         out += [two.reshape(rest, slow, middle, band, columns)] if step < fast else []
     parted = [None] + [across(t, i + 1) for i, t in enumerate(sent)][::-1]
@@ -388,7 +397,7 @@
     places = jnp.stack(places)
 
     early = [documents] + [
-        part[count, :count].astype(jnp.int32) for part in parted[1:]
+        part[depth // columns * count, :count].astype(jnp.int32) for part in parted[1:]
     ]
     turns = []
     for step, docs in enumerate(early):
@@ -397,14 +406,9 @@
             at = at - jnp.sum((others[None, :] < docs[:, None]).astype(jnp.int32), axis=1)
         turns.append(tables(at))
 
-    weights = None
     other = []
-    none = jnp.zeros((1,), jnp.int32)
     for step in range(1, pair):
-        if weights is None:
-            out, weights = project(places, parted[step], *turns[step], bands)
-        else:
-            out = product(none, parted[step], weights, *turns[step], LINK)
+        out, weights = project(places, parted[step], *turns[step], bands)
         other.append(across(out, pair - step))
     features = after(features, weights)
     grads = gradient(

time: 80.3 us -> 78.6 us (0.979)
  waiting for transfers between devices: 16.7 us -> 15.3 us
    ppermute x3, waiting for transfers between devices: 3.29 us -> 1.93 us  [across(): return lax.ppermute(value, 'fsdp', shift_pairs(pair, 1, pair, step))]
  transfers between devices with their start and end apart: 20 -> 20, of which waited for: 10 -> 10; matrix products, arithmetic and copies ran while one was open for 14% -> 16% of each run, Pallas kernels for 18% -> 18%
where the time goes in v4:
time: 78.6 us; the launch traced here: 78.3 us
  starting transfers between devices  30.4 us (39%)
  Pallas kernels  18.4 us (23%)
  waiting for transfers between devices  15.3 us (19%)
  other arithmetic  13 us (17%)
  between operations  0.93 us (1%)
    ppermute x17, starting transfers between devices, moved(): return lax.ppermute(value, 'rep', pairs)  24.2 us
    ppermute x17, waiting for transfers between devices, moved(): return lax.ppermute(value, 'rep', pairs)  13.4 us
    ppermute x3, starting transfers between devices, across(): return lax.ppermute(value, 'fsdp', shift_pairs(pair, 1, pair, step))  6.2 us
    pallas_call x1, Pallas kernels, gradient(): pl.pallas_call(gradient_kernel, grid_spec=pltpu.PrefetchScalarGridSpec(nu...  6.16 us
    pallas_call x1, Pallas kernels, project(): pl.pallas_call(functools.partial(project_kernel, len(bands)), in_specs=[p...  5.28 us
    pallas_call x1, Pallas kernels, pack(): pl.pallas_call(functools.partial(pack_kernel, step, sides), in_specs=[pla...  4.31 us
    convert_element_type x3, other arithmetic, local(): out = total(piece(k, 0) + after(sums[k], last)).astype(LINK)  3.06 us
    pallas_call x1, Pallas kernels, product(): pl.pallas_call(product_kernel, grid_spec=pltpu.PrefetchScalarGridSpec(num...  2.69 us
  transfers between devices with their start and end apart: 20, of which 10 were waited for; matrix products, arithmetic and copies ran while one was open for 16% of the time, Pallas kernels for 18%

profile of v4, /device:TPU:0, one launch (start us, length us, event | category | flops | bytes accessed | tf_op | source)
XLA Modules:
  0.0 78.3 jit_solution(16896670313384179938)
XLA Ops:
  0.6 4.3 %pack.1 = (bf16[2064,512]{1,0:T(8,128)(2,1)}, bf16[8,128,512]{2,1,0:T(8,128)(2,1)}) custom-call(bf16[512,4096]{1,0:T(8,128)(2,1)} %bitcast.128, s32[1,512]{1,0:T(1,128)} %documents_ref.1, f32[8,2,128,512]{3,2,1,0:T(8,128)} %bitcast.133), custom_call_target="tpu_custom_call" | custom-call | tf_op jit(solution)/shard_map/pack/pallas_call | solution.py:115
  5.5 2.6 %collective-permute-start.8 = (bf16[2064,512]{1,0:T(8,128)(2,1)}, bf16[2064,512]{1,0:T(8,128)(2,1)S(1)}, u32[]{:S(2)}, u32[]{:S(2)}) collective-permute-start(bf16[2064,512]{1,0:T(8,128)(2,1)} %get-tuple-element.18), channel_id=1, source_target_pairs={{0,1},{1,0},{2,3},{3,2},{4,5},{5,4},{6,7},{7,6},{8,9},{9,8},{10,11... | collective-permute-start | bytes 6340616 | tf_op jit(solution)/shard_map/ppermute | solution.py:319
  8.1 2.4 %fusion.15 = (bf16[1,128,512]{2,1,0:T(8,128)(2,1)}, bf16[1,128,512]{2,1,0:T(8,128)(2,1)}, bf16[1,128,512]{2,1,0:T(8,128)(2,1)}, bf16[1,128,512]{2,1,0:T(8,128)(2,1)S(1)}) fusion(f32[1,4,2,2,128,512]{5,4,3,2,1,0:T(8,128)} %bitcast.134, s32[]{:T(128)S(6)} %select_n.292, s32[]{:T(128)S(6)} %select_n.283, s32[]{:T(128)S(6)} %select_n.280, ...), kind=kLoop, calls=%fused_computation.39 | loop fusion | flops 786432 | bytes 2097176 | tf_op jit(solution)/shard_map/convert_element_type | solution.py:345
  10.5 2.8 %collective-permute-start.2 = (bf16[1,128,512]{2,1,0:T(8,128)(2,1)}, bf16[1,128,512]{2,1,0:T(8,128)(2,1)}, u32[]{:S(2)}, u32[]{:S(2)}) collective-permute-start(bf16[1,128,512]{2,1,0:T(8,128)(2,1)} %get-tuple-element.30), channel_id=1, source_target_pairs={{0,4},{2,6},{4,0},{6,2},{8,12},{10,14},{12,8},{14,10},{16,20},{18,... | collective-permute-start | bytes 393224 | tf_op jit(solution)/shard_map/ppermute | solution.py:316
  13.3 2.0 %collective-permute-start.4 = (bf16[1,128,512]{2,1,0:T(8,128)(2,1)}, bf16[1,128,512]{2,1,0:T(8,128)(2,1)S(1)}, u32[]{:S(2)}, u32[]{:S(2)}) collective-permute-start(bf16[1,128,512]{2,1,0:T(8,128)(2,1)} %get-tuple-element.29), channel_id=1, source_target_pairs={{0,4},{2,6},{4,0},{6,2},{8,12},{10,14},{12,8},{14,10},{16,20},{18,... | collective-permute-start | bytes 393224 | tf_op jit(solution)/shard_map/ppermute | solution.py:316
  15.3 2.5 %collective-permute-done.2 = bf16[1,128,512]{2,1,0:T(8,128)(2,1)} collective-permute-done((bf16[1,128,512]{2,1,0:T(8,128)(2,1)}, bf16[1,128,512]{2,1,0:T(8,128)(2,1)}, u32[]{:S(2)}, u32[]{:S(2)}) %collective-permute-start.2) | collective-permute-done | bytes 131104 | tf_op jit(solution)/shard_map/ppermute | solution.py:316
  17.8 1.1 %fusion.19 = bf16[1,128,512]{2,1,0:T(8,128)(2,1)S(1)} fusion(bf16[1,128,512]{2,1,0:T(8,128)(2,1)} %collective-permute-done.2, f32[1,4,2,2,128,512]{5,4,3,2,1,0:T(8,128)} %bitcast.135, s32[]{:T(128)S(6)} %select_n.286, s32[]{:T(128)S(6)} %select_n.277, s32[]{:T(128)S(6)} %select_n.280, bf16[1,4,2,128,512]{4,3,2,1,0:T(8,128)(2,1)S(1)} %collective-permute-done), kind=kLoop, calls=%fused_computation.46 | loop fusion | flops 327680 | bytes 655372 | tf_op jit(solution)/shard_map/convert_element_type | solution.py:351
  18.9 3.2 %collective-permute-start.3 = (bf16[1,128,512]{2,1,0:T(8,128)(2,1)S(1)}, bf16[1,128,512]{2,1,0:T(8,128)(2,1)S(1)}, u32[]{:S(2)}, u32[]{:S(2)}) collective-permute-start(bf16[1,128,512]{2,1,0:T(8,128)(2,1)S(1)} %fusion.19), channel_id=1, source_target_pairs={{0,16},{2,18},{4,20},{6,22},{8,24},{10,26},{12,28},{14,30},{16,0},... | collective-permute-start | bytes 393224 | tf_op jit(solution)/shard_map/ppermute | solution.py:316
  22.1 1.2 %collective-permute-done.4 = bf16[1,128,512]{2,1,0:T(8,128)(2,1)S(1)} collective-permute-done((bf16[1,128,512]{2,1,0:T(8,128)(2,1)}, bf16[1,128,512]{2,1,0:T(8,128)(2,1)S(1)}, u32[]{:S(2)}, u32[]{:S(2)}) %collective-permute-start.4) | collective-permute-done | bytes 131104 | tf_op jit(solution)/shard_map/ppermute | solution.py:316
  24.3 2.2 %collective-permute-start.5 = (bf16[1,128,512]{2,1,0:T(8,128)(2,1)S(1)}, bf16[1,128,512]{2,1,0:T(8,128)(2,1)S(1)}, u32[]{:S(2)}, u32[]{:S(2)}) collective-permute-start(bf16[1,128,512]{2,1,0:T(8,128)(2,1)S(1)} %fusion.14), channel_id=1, source_target_pairs={{0,8},{2,10},{4,12},{6,14},{8,16},{10,18},{12,20},{14,22},{16,24},... | collective-permute-start | bytes 393224 | tf_op jit(solution)/shard_map/ppermute | solution.py:316
  27.6 3.0 %collective-permute-start.7 = (bf16[1,128,512]{2,1,0:T(8,128)(2,1)S(1)}, bf16[1,128,512]{2,1,0:T(8,128)(2,1)S(1)}, u32[]{:S(2)}, u32[]{:S(2)}) collective-permute-start(bf16[1,128,512]{2,1,0:T(8,128)(2,1)S(1)} %fusion.12), channel_id=1, source_target_pairs={{0,24},{2,26},{4,28},{6,30},{8,0},{10,2},{12,4},{14,6},{16,8},{18,... | collective-permute-start | bytes 393224 | tf_op jit(solution)/shard_map/ppermute | solution.py:316
  30.6 1.6 %collective-permute-done.5 = bf16[1,128,512]{2,1,0:T(8,128)(2,1)S(1)} collective-permute-done((bf16[1,128,512]{2,1,0:T(8,128)(2,1)S(1)}, bf16[1,128,512]{2,1,0:T(8,128)(2,1)S(1)}, u32[]{:S(2)}, u32[]{:S(2)}) %collective-permute-start.5) | collective-permute-done | bytes 131104 | tf_op jit(solution)/shard_map/ppermute | solution.py:316
  32.2 1.4 %collective-permute-done.7 = bf16[1,128,512]{2,1,0:T(8,128)(2,1)S(1)} collective-permute-done((bf16[1,128,512]{2,1,0:T(8,128)(2,1)S(1)}, bf16[1,128,512]{2,1,0:T(8,128)(2,1)S(1)}, u32[]{:S(2)}, u32[]{:S(2)}) %collective-permute-start.7) | collective-permute-done | bytes 131104 | tf_op jit(solution)/shard_map/ppermute | solution.py:316
  33.6 1.2 %subtract_convert_fusion.refs_0_ = bf16[1,128,512]{2,1,0:T(8,128)(2,1)S(1)} fusion(f32[1,128,512]{2,1,0:T(8,128)} %param.10, bf16[1,128,512]{2,1,0:T(8,128)(2,1)S(1)} %collective-permute-done.7, bf16[1,128,512]{2,1,0:T(8,128)(2,1)S(1)} %collective-permute-done.5, bf16[1,128,512]{2,1,0:T(8,128)(2,1)S(1)} %collective-permute-done.3, ...), kind=kLoop, calls=%fused_computation.52 | loop fusion | flops 1179648 | bytes 1572876 | tf_op jit(solution)/shard_map/convert_element_type | solution.py:369
  34.8 3.8 %collective-permute-start.9 = (bf16[1,128,512]{2,1,0:T(8,128)(2,1)S(1)}, bf16[1,128,512]{2,1,0:T(8,128)(2,1)S(1)}, u32[]{:S(2)}, u32[]{:S(2)}) collective-permute-start(bf16[1,128,512]{2,1,0:T(8,128)(2,1)S(1)} %subtract_convert_fusion.refs_0_), channel_id=1, source_target_pairs={{0,24},{2,26},{4,28},{6,30},{8,0},{10,2},{12,4},{14,6},{16,8},{18,... | collective-permute-start | bytes 393224 | tf_op jit(solution)/shard_map/ppermute | solution.py:316
  39.3 1.5 %collective-permute-start.13 = (bf16[1,128,512]{2,1,0:T(8,128)(2,1)S(1)}, bf16[1,128,512]{2,1,0:T(8,128)(2,1)S(1)}, u32[]{:S(2)}, u32[]{:S(2)}) collective-permute-start(bf16[1,128,512]{2,1,0:T(8,128)(2,1)S(1)} %subtract_convert_fusion.refs_0_), channel_id=1, source_target_pairs={{0,4},{2,6},{4,0},{6,2},{8,12},{10,14},{12,8},{14,10},{16,20},{18,... | collective-permute-start | bytes 393224 | tf_op jit(solution)/shard_map/ppermute | solution.py:316
  40.8 1.8 %collective-permute-done.9.refs_1_ = bf16[1,128,512]{2,1,0:T(8,128)(2,1)S(1)} collective-permute-done((bf16[1,128,512]{2,1,0:T(8,128)(2,1)S(1)}, bf16[1,128,512]{2,1,0:T(8,128)(2,1)S(1)}, u32[]{:S(2)}, u32[]{:S(2)}) %collective-permute-start.9) | collective-permute-done | bytes 131104 | tf_op jit(solution)/shard_map/ppermute | solution.py:316
  42.6 1.4 %collective-permute-start.14 = (bf16[1,128,512]{2,1,0:T(8,128)(2,1)S(1)}, bf16[1,128,512]{2,1,0:T(8,128)(2,1)S(1)}, u32[]{:S(2)}, u32[]{:S(2)}) collective-permute-start(bf16[1,128,512]{2,1,0:T(8,128)(2,1)S(1)} %collective-permute-done.9.refs_1_), channel_id=1, source_target_pairs={{0,4},{2,6},{4,0},{6,2},{8,12},{10,14},{12,8},{14,10},{16,20},{18,... | collective-permute-start | bytes 393224 | tf_op jit(solution)/shard_map/ppermute | solution.py:316
  44.0 1.8 %collective-permute-done.10.refs_2_ = bf16[1,128,512]{2,1,0:T(8,128)(2,1)S(1)} collective-permute-done((bf16[1,128,512]{2,1,0:T(8,128)(2,1)S(1)}, bf16[1,128,512]{2,1,0:T(8,128)(2,1)S(1)}, u32[]{:S(2)}, u32[]{:S(2)}) %collective-permute-start.10) | collective-permute-done | bytes 131104 | tf_op jit(solution)/shard_map/ppermute | solution.py:316
  45.8 1.5 %collective-permute-start.15 = (bf16[1,128,512]{2,1,0:T(8,128)(2,1)S(1)}, bf16[1,128,512]{2,1,0:T(8,128)(2,1)S(1)}, u32[]{:S(2)}, u32[]{:S(2)}) collective-permute-start(bf16[1,128,512]{2,1,0:T(8,128)(2,1)S(1)} %collective-permute-done.10.refs_2_), channel_id=1, source_target_pairs={{0,4},{2,6},{4,0},{6,2},{8,12},{10,14},{12,8},{14,10},{16,20},{18,... | collective-permute-start | bytes 393224 | tf_op jit(solution)/shard_map/ppermute | solution.py:316
  47.3 1.5 %collective-permute-done.11.refs_3_ = bf16[1,128,512]{2,1,0:T(8,128)(2,1)S(1)} collective-permute-done((bf16[1,128,512]{2,1,0:T(8,128)(2,1)S(1)}, bf16[1,128,512]{2,1,0:T(8,128)(2,1)S(1)}, u32[]{:S(2)}, u32[]{:S(2)}) %collective-permute-start.11) | collective-permute-done | bytes 131104 | tf_op jit(solution)/shard_map/ppermute | solution.py:316
  48.8 1.5 %collective-permute-start.16 = (bf16[1,128,512]{2,1,0:T(8,128)(2,1)S(1)}, bf16[1,128,512]{2,1,0:T(8,128)(2,1)S(1)}, u32[]{:S(2)}, u32[]{:S(2)}) collective-permute-start(bf16[1,128,512]{2,1,0:T(8,128)(2,1)S(1)} %collective-permute-done.11.refs_3_), channel_id=1, source_target_pairs={{0,4},{2,6},{4,0},{6,2},{8,12},{10,14},{12,8},{14,10},{16,20},{18,... | collective-permute-start | bytes 393224 | tf_op jit(solution)/shard_map/ppermute | solution.py:316
  50.6 1.6 %collective-permute-start.19 = (bf16[512,512]{1,0:T(8,128)(2,1)}, bf16[512,512]{1,0:T(8,128)(2,1)S(1)}, u32[]{:S(2)}, u32[]{:S(2)}) collective-permute-start(bf16[512,512]{1,0:T(8,128)(2,1)} %bitcast.131), channel_id=1, source_target_pairs={{0,1},{1,0},{2,3},{3,2},{4,5},{5,4},{6,7},{7,6},{8,9},{9,8},{10,11... | collective-permute-start | bytes 1572872 | tf_op jit(solution)/shard_map/ppermute | solution.py:319
  52.2 1.6 %collective-permute-done.16.refs_8_ = bf16[1,128,512]{2,1,0:T(8,128)(2,1)S(1)} collective-permute-done((bf16[1,128,512]{2,1,0:T(8,128)(2,1)S(1)}, bf16[1,128,512]{2,1,0:T(8,128)(2,1)S(1)}, u32[]{:S(2)}, u32[]{:S(2)}) %collective-permute-start.16) | collective-permute-done | bytes 131104 | tf_op jit(solution)/shard_map/ppermute | solution.py:316
  53.9 1.2 %collective-permute-done.8.part_ref.refs_0_ = bf16[2064,512]{1,0:T(8,128)(2,1)S(1)} collective-permute-done((bf16[2064,512]{1,0:T(8,128)(2,1)}, bf16[2064,512]{1,0:T(8,128)(2,1)S(1)}, u32[]{:S(2)}, u32[]{:S(2)}) %collective-permute-start.8) | collective-permute-done | bytes 2113568 | tf_op jit(solution)/shard_map/ppermute | solution.py:319
  55.1 1.3 %convert_reduce_fusion = (s32[512]{0:T(512)S(1)}, s32[512]{0:T(512)S(1)}, s32[512]{0:T(512)S(1)}, s32[512]{0:T(512)S(1)}) fusion(s32[512]{0:T(512)S(1)} %bitcast.142, s32[512]{0:T(512)} %bitcast.141), kind=kLoop, calls=%fused_computation.1 | loop fusion | flops 3143680 | bytes 12288 | tf_op jit(solution)/shard_map/reduce_sum | solution.py:406
  56.5 1.9 %fusion.10 = (f32[512,128]{1,0:T(8,128)S(1)}, f32[512,128]{1,0:T(8,128)S(1)}, f32[512,128]{1,0:T(8,128)S(1)}, f32[512,128]{1,0:T(8,128)S(1)}) fusion(f32[512]{0:T(512)S(1)} %get-tuple-element.40, f32[128]{0:T(128)S(1)} %get-tuple-element.42, f32[128]{0:T(128)S(1)} %get-tuple-element.43, f32[512]{0:T(512)S(1)} %get-tuple-element.41), kind=kLoop, calls=%fused_computation.31 | loop fusion | flops 262144 | bytes 1053696 | tf_op jit(solution)/shard_map/mul | solution.py:44
  58.4 5.3 %project.1 = (bf16[512,512]{1,0:T(8,128)(2,1)S(1)}, bf16[2048,512]{1,0:T(8,128)(2,1)S(1)}) custom-call(s32[16]{0:T(128)S(1)} %stack.67.place_ref, bf16[2064,512]{1,0:T(8,128)(2,1)S(1)} %collective-permute-done.8.part_ref.refs_0_, f32[512,128]{1,0:T(8,128)S(1)} %get-tuple-element.38.cosine_ref.refs_2_, f32[512,128]{1,0:T(8,128)S(1)} %get-tuple-element.39.sine_ref.refs_3_, ...), custom_call_target="tpu_custom_call" | custom-call | tf_op jit(solution)/shard_map/project/pallas_call | solution.py:282
  63.7 2.0 %collective-permute-start.18 = (bf16[512,512]{1,0:T(8,128)(2,1)S(1)}, bf16[512,512]{1,0:T(8,128)(2,1)S(1)}, u32[]{:S(2)}, u32[]{:S(2)}) collective-permute-start(bf16[512,512]{1,0:T(8,128)(2,1)S(1)} %get-tuple-element.22), channel_id=1, source_target_pairs={{0,1},{1,0},{2,3},{3,2},{4,5},{5,4},{6,7},{7,6},{8,9},{9,8},{10,11... | collective-permute-start | bytes 1572872 | tf_op jit(solution)/shard_map/ppermute | solution.py:319
  65.7 1.1 %fusion.6 = f32[128,512]{1,0:T(8,128)S(1)} fusion(bf16[1,128,512]{2,1,0:T(8,128)(2,1)S(1)} %copy-done.6, bf16[1,128,512]{2,1,0:T(8,128)(2,1)S(1)} %copy-done.8, bf16[1,128,512]{2,1,0:T(8,128)(2,1)S(1)} %copy-done.10, bf16[1,128,512]{2,1,0:T(8,128)(2,1)S(1)} %copy-done.12, f32[1,4,2,2,128,512]{5,4,3,2,1,0:T(8,128)} %bitcast.139, s32[]{:T(128)S(6)} %select_n.272, ...), kind=kLoop, calls=%fused_computation.27 | loop fusion | flops 720896 | bytes 1179660 | tf_op jit(solution)/shard_map/div | solution.py:367
  66.8 2.7 %product.1 = f32[512,512]{1,0:T(8,128)S(1)} custom-call(s32[1]{0:T(128)} %bitcast.48.side_ref, bf16[512,4096]{1,0:T(8,128)(2,1)S(1)} %bitcast.129, bf16[2048,512]{1,0:T(8,128)(2,1)S(1)} %get-tuple-element.19.weights_ref, f32[512,128]{1,0:T(8,128)S(1)} %get-tuple-element.35.cosine_ref, f32[512,128]{1,0:T(8,128)S(1)} %get-tuple-element.34.sine_ref), custom_call_target="tpu_custom_call" | custom-call | tf_op jit(solution)/shard_map/product/pallas_call | solution.py:225
  69.6 6.2 %gradient.1 = bf16[2048,512]{1,0:T(8,128)(2,1)} custom-call(s32[1]{0:T(128)} %bitcast.48.side_ref, bf16[512,4096]{1,0:T(8,128)(2,1)S(1)} %bitcast.130, bf16[512,512]{1,0:T(8,128)(2,1)S(1)} %bitcast.132, f32[512,128]{1,0:T(8,128)S(1)} %get-tuple-element.35.cosine_ref, f32[512,128]{1,0:T(8,128)S(1)} %get-tuple-element.34.sine_ref, ...), custom_call_target="tpu_custom_call" | custom-call | tf_op jit(solution)/shard_map/gradient/pallas_call | solution.py:175
  (54 shorter events, 6.2 us)
Async XLA Ops:
  5.0 28.6 %copy-start.3 = (f32[1,128,512]{2,1,0:T(8,128)S(1)}, f32[1,128,512]{2,1,0:T(8,128)}, u32[]{:S(2)}) copy-start(f32[1,128,512]{2,1,0:T(8,128)} %param.11) | copy-start | bytes 786436
  5.0 3.1 %collective-permute-start = (bf16[1,4,2,128,512]{4,3,2,1,0:T(8,128)(2,1)}, bf16[1,4,2,128,512]{4,3,2,1,0:T(8,128)(2,1)S(1)}, u32[]{:S(2)}, u32[]{:S(2)}) collective-permute-start(bf16[1,4,2,128,512]{4,3,2,1,0:T(8,128)(2,1)} %bitcast.143), channel_id=1, source_target_pairs={{0,2},{2,0},{4,6},{6,4},{8,10},{10,8},{12,14},{14,12},{16,18},{18,... | collective-permute-start | bytes 3145736 | tf_op jit(solution)/shard_map/ppermute | solution.py:316
  5.5 49.6 %collective-permute-start.8 = (bf16[2064,512]{1,0:T(8,128)(2,1)}, bf16[2064,512]{1,0:T(8,128)(2,1)S(1)}, u32[]{:S(2)}, u32[]{:S(2)}) collective-permute-start(bf16[2064,512]{1,0:T(8,128)(2,1)} %get-tuple-element.18), channel_id=1, source_target_pairs={{0,1},{1,0},{2,3},{3,2},{4,5},{5,4},{6,7},{7,6},{8,9},{9,8},{10,11... | collective-permute-start | bytes 6340616 | tf_op jit(solution)/shard_map/ppermute | solution.py:319
  8.1 25.5 %copy-start.2 = (bf16[1,4,2,128,512]{4,3,2,1,0:T(8,128)(2,1)}, bf16[1,4,2,128,512]{4,3,2,1,0:T(8,128)(2,1)S(1)}, u32[]{:S(2)}) copy-start(bf16[1,4,2,128,512]{4,3,2,1,0:T(8,128)(2,1)S(1)} %collective-permute-done) | copy-start | bytes 3145732
  10.5 7.4 %collective-permute-start.2 = (bf16[1,128,512]{2,1,0:T(8,128)(2,1)}, bf16[1,128,512]{2,1,0:T(8,128)(2,1)}, u32[]{:S(2)}, u32[]{:S(2)}) collective-permute-start(bf16[1,128,512]{2,1,0:T(8,128)(2,1)} %get-tuple-element.30), channel_id=1, source_target_pairs={{0,4},{2,6},{4,0},{6,2},{8,12},{10,14},{12,8},{14,10},{16,20},{18,... | collective-permute-start | bytes 393224 | tf_op jit(solution)/shard_map/ppermute | solution.py:316
  13.2 17.3 %collective-permute-start.1 = (bf16[1,128,512]{2,1,0:T(8,128)(2,1)S(1)}, bf16[1,128,512]{2,1,0:T(8,128)(2,1)S(1)}, u32[]{:S(2)}, u32[]{:S(2)}) collective-permute-start(bf16[1,128,512]{2,1,0:T(8,128)(2,1)S(1)} %get-tuple-element.31), channel_id=1, source_target_pairs={{0,4},{2,6},{4,0},{6,2},{8,12},{10,14},{12,8},{14,10},{16,20},{18,... | collective-permute-start | bytes 393224 | tf_op jit(solution)/shard_map/ppermute | solution.py:316
  13.3 10.1 %collective-permute-start.4 = (bf16[1,128,512]{2,1,0:T(8,128)(2,1)}, bf16[1,128,512]{2,1,0:T(8,128)(2,1)S(1)}, u32[]{:S(2)}, u32[]{:S(2)}) collective-permute-start(bf16[1,128,512]{2,1,0:T(8,128)(2,1)} %get-tuple-element.29), channel_id=1, source_target_pairs={{0,4},{2,6},{4,0},{6,2},{8,12},{10,14},{12,8},{14,10},{16,20},{18,... | collective-permute-start | bytes 393224 | tf_op jit(solution)/shard_map/ppermute | solution.py:316
  15.3 11.3 %collective-permute-start.6 = (bf16[1,128,512]{2,1,0:T(8,128)(2,1)}, bf16[1,128,512]{2,1,0:T(8,128)(2,1)S(1)}, u32[]{:S(2)}, u32[]{:S(2)}) collective-permute-start(bf16[1,128,512]{2,1,0:T(8,128)(2,1)} %get-tuple-element.28), channel_id=1, source_target_pairs={{0,4},{2,6},{4,0},{6,2},{8,12},{10,14},{12,8},{14,10},{16,20},{18,... | collective-permute-start | bytes 393224 | tf_op jit(solution)/shard_map/ppermute | solution.py:316
  18.9 11.7 %collective-permute-start.3 = (bf16[1,128,512]{2,1,0:T(8,128)(2,1)S(1)}, bf16[1,128,512]{2,1,0:T(8,128)(2,1)S(1)}, u32[]{:S(2)}, u32[]{:S(2)}) collective-permute-start(bf16[1,128,512]{2,1,0:T(8,128)(2,1)S(1)} %fusion.19), channel_id=1, source_target_pairs={{0,16},{2,18},{4,20},{6,22},{8,24},{10,26},{12,28},{14,30},{16,0},... | collective-permute-start | bytes 393224 | tf_op jit(solution)/shard_map/ppermute | solution.py:316
  24.3 7.8 %collective-permute-start.5 = (bf16[1,128,512]{2,1,0:T(8,128)(2,1)S(1)}, bf16[1,128,512]{2,1,0:T(8,128)(2,1)S(1)}, u32[]{:S(2)}, u32[]{:S(2)}) collective-permute-start(bf16[1,128,512]{2,1,0:T(8,128)(2,1)S(1)} %fusion.14), channel_id=1, source_target_pairs={{0,8},{2,10},{4,12},{6,14},{8,16},{10,18},{12,20},{14,22},{16,24},... | collective-permute-start | bytes 393224 | tf_op jit(solution)/shard_map/ppermute | solution.py:316
  27.6 6.0 %collective-permute-start.7 = (bf16[1,128,512]{2,1,0:T(8,128)(2,1)S(1)}, bf16[1,128,512]{2,1,0:T(8,128)(2,1)S(1)}, u32[]{:S(2)}, u32[]{:S(2)}) collective-permute-start(bf16[1,128,512]{2,1,0:T(8,128)(2,1)S(1)} %fusion.12), channel_id=1, source_target_pairs={{0,24},{2,26},{4,28},{6,30},{8,0},{10,2},{12,4},{14,6},{16,8},{18,... | collective-permute-start | bytes 393224 | tf_op jit(solution)/shard_map/ppermute | solution.py:316
  30.6 18.2 %copy-start.5 = (bf16[1,128,512]{2,1,0:T(8,128)(2,1)}, bf16[1,128,512]{2,1,0:T(8,128)(2,1)S(1)}, u32[]{:S(2)}) copy-start(bf16[1,128,512]{2,1,0:T(8,128)(2,1)S(1)} %collective-permute-done.1) | copy-start | bytes 393220
  30.6 19.7 %copy-start.7 = (bf16[1,128,512]{2,1,0:T(8,128)(2,1)}, bf16[1,128,512]{2,1,0:T(8,128)(2,1)S(1)}, u32[]{:S(2)}) copy-start(bf16[1,128,512]{2,1,0:T(8,128)(2,1)S(1)} %collective-permute-done.3) | copy-start | bytes 393220
  32.2 18.1 %copy-start.9 = (bf16[1,128,512]{2,1,0:T(8,128)(2,1)}, bf16[1,128,512]{2,1,0:T(8,128)(2,1)S(1)}, u32[]{:S(2)}) copy-start(bf16[1,128,512]{2,1,0:T(8,128)(2,1)S(1)} %collective-permute-done.5) | copy-start | bytes 393220
  33.6 16.7 %copy-start.11 = (bf16[1,128,512]{2,1,0:T(8,128)(2,1)}, bf16[1,128,512]{2,1,0:T(8,128)(2,1)S(1)}, u32[]{:S(2)}) copy-start(bf16[1,128,512]{2,1,0:T(8,128)(2,1)S(1)} %collective-permute-done.7) | copy-start | bytes 393220
  34.8 7.8 %collective-permute-start.9 = (bf16[1,128,512]{2,1,0:T(8,128)(2,1)S(1)}, bf16[1,128,512]{2,1,0:T(8,128)(2,1)S(1)}, u32[]{:S(2)}, u32[]{:S(2)}) collective-permute-start(bf16[1,128,512]{2,1,0:T(8,128)(2,1)S(1)} %subtract_convert_fusion.refs_0_), channel_id=1, source_target_pairs={{0,24},{2,26},{4,28},{6,30},{8,0},{10,2},{12,4},{14,6},{16,8},{18,... | collective-permute-start | bytes 393224 | tf_op jit(solution)/shard_map/ppermute | solution.py:316
  38.7 7.2 %collective-permute-start.10 = (bf16[1,128,512]{2,1,0:T(8,128)(2,1)S(1)}, bf16[1,128,512]{2,1,0:T(8,128)(2,1)S(1)}, u32[]{:S(2)}, u32[]{:S(2)}) collective-permute-start(bf16[1,128,512]{2,1,0:T(8,128)(2,1)S(1)} %subtract_convert_fusion.refs_0_), channel_id=1, source_target_pairs={{0,8},{2,10},{4,12},{6,14},{8,16},{10,18},{12,20},{14,22},{16,24},... | collective-permute-start | bytes 393224 | tf_op jit(solution)/shard_map/ppermute | solution.py:316
  38.7 10.2 %collective-permute-start.11 = (bf16[1,128,512]{2,1,0:T(8,128)(2,1)S(1)}, bf16[1,128,512]{2,1,0:T(8,128)(2,1)S(1)}, u32[]{:S(2)}, u32[]{:S(2)}) collective-permute-start(bf16[1,128,512]{2,1,0:T(8,128)(2,1)S(1)} %subtract_convert_fusion.refs_0_), channel_id=1, source_target_pairs={{0,16},{2,18},{4,20},{6,22},{8,24},{10,26},{12,28},{14,30},{16,0},... | collective-permute-start | bytes 393224 | tf_op jit(solution)/shard_map/ppermute | solution.py:316
  39.3 11.3 %collective-permute-start.13 = (bf16[1,128,512]{2,1,0:T(8,128)(2,1)S(1)}, bf16[1,128,512]{2,1,0:T(8,128)(2,1)S(1)}, u32[]{:S(2)}, u32[]{:S(2)}) collective-permute-start(bf16[1,128,512]{2,1,0:T(8,128)(2,1)S(1)} %subtract_convert_fusion.refs_0_), channel_id=1, source_target_pairs={{0,4},{2,6},{4,0},{6,2},{8,12},{10,14},{12,8},{14,10},{16,20},{18,... | collective-permute-start | bytes 393224 | tf_op jit(solution)/shard_map/ppermute | solution.py:316
  42.6 9.6 %collective-permute-start.14 = (bf16[1,128,512]{2,1,0:T(8,128)(2,1)S(1)}, bf16[1,128,512]{2,1,0:T(8,128)(2,1)S(1)}, u32[]{:S(2)}, u32[]{:S(2)}) collective-permute-start(bf16[1,128,512]{2,1,0:T(8,128)(2,1)S(1)} %collective-permute-done.9.refs_1_), channel_id=1, source_target_pairs={{0,4},{2,6},{4,0},{6,2},{8,12},{10,14},{12,8},{14,10},{16,20},{18,... | collective-permute-start | bytes 393224 | tf_op jit(solution)/shard_map/ppermute | solution.py:316
  45.8 6.4 %collective-permute-start.15 = (bf16[1,128,512]{2,1,0:T(8,128)(2,1)S(1)}, bf16[1,128,512]{2,1,0:T(8,128)(2,1)S(1)}, u32[]{:S(2)}, u32[]{:S(2)}) collective-permute-start(bf16[1,128,512]{2,1,0:T(8,128)(2,1)S(1)} %collective-permute-done.10.refs_2_), channel_id=1, source_target_pairs={{0,4},{2,6},{4,0},{6,2},{8,12},{10,14},{12,8},{14,10},{16,20},{18,... | collective-permute-start | bytes 393224 | tf_op jit(solution)/shard_map/ppermute | solution.py:316
  48.8 5.0 %collective-permute-start.16 = (bf16[1,128,512]{2,1,0:T(8,128)(2,1)S(1)}, bf16[1,128,512]{2,1,0:T(8,128)(2,1)S(1)}, u32[]{:S(2)}, u32[]{:S(2)}) collective-permute-start(bf16[1,128,512]{2,1,0:T(8,128)(2,1)S(1)} %collective-permute-done.11.refs_3_), channel_id=1, source_target_pairs={{0,4},{2,6},{4,0},{6,2},{8,12},{10,14},{12,8},{14,10},{16,20},{18,... | collective-permute-start | bytes 393224 | tf_op jit(solution)/shard_map/ppermute | solution.py:316
  50.5 15.2 %copy-start.6 = (bf16[1,128,512]{2,1,0:T(8,128)(2,1)S(1)}, bf16[1,128,512]{2,1,0:T(8,128)(2,1)}, u32[]{:S(2)}) copy-start(bf16[1,128,512]{2,1,0:T(8,128)(2,1)} %copy-done.5) | copy-start | bytes 393220
  50.5 15.2 %copy-start.8 = (bf16[1,128,512]{2,1,0:T(8,128)(2,1)S(1)}, bf16[1,128,512]{2,1,0:T(8,128)(2,1)}, u32[]{:S(2)}) copy-start(bf16[1,128,512]{2,1,0:T(8,128)(2,1)} %copy-done.7) | copy-start | bytes 393220
  50.5 15.2 %copy-start.10 = (bf16[1,128,512]{2,1,0:T(8,128)(2,1)S(1)}, bf16[1,128,512]{2,1,0:T(8,128)(2,1)}, u32[]{:S(2)}) copy-start(bf16[1,128,512]{2,1,0:T(8,128)(2,1)} %copy-done.9) | copy-start | bytes 393220
  50.5 15.2 %copy-start.12 = (bf16[1,128,512]{2,1,0:T(8,128)(2,1)S(1)}, bf16[1,128,512]{2,1,0:T(8,128)(2,1)}, u32[]{:S(2)}) copy-start(bf16[1,128,512]{2,1,0:T(8,128)(2,1)} %copy-done.11) | copy-start | bytes 393220
  50.6 16.2 %copy-start = (bf16[1,512,4096]{2,1,0:T(8,128)(2,1)S(1)}, bf16[1,512,4096]{2,1,0:T(8,128)(2,1)}, u32[]{:S(2)}) copy-start(bf16[1,512,4096]{2,1,0:T(8,128)(2,1)} %param.6) | copy-start | bytes 12582916
  50.6 18.9 %collective-permute-start.19 = (bf16[512,512]{1,0:T(8,128)(2,1)}, bf16[512,512]{1,0:T(8,128)(2,1)S(1)}, u32[]{:S(2)}, u32[]{:S(2)}) collective-permute-start(bf16[512,512]{1,0:T(8,128)(2,1)} %bitcast.131), channel_id=1, source_target_pairs={{0,1},{1,0},{2,3},{3,2},{4,5},{5,4},{6,7},{7,6},{8,9},{9,8},{10,11... | collective-permute-start | bytes 1572872 | tf_op jit(solution)/shard_map/ppermute | solution.py:319
  52.2 6.2 %collective-permute-start.12 = (bf16[4,128,512]{2,1,0:T(8,128)(2,1)S(1)}, bf16[4,128,512]{2,1,0:T(8,128)(2,1)S(1)}, u32[]{:S(2)}, u32[]{:S(2)}) collective-permute-start(bf16[4,128,512]{2,1,0:T(8,128)(2,1)S(1)} %pad_maximum_fusion), channel_id=1, source_target_pairs={{0,2},{2,0},{4,6},{6,4},{8,10},{10,8},{12,14},{14,12},{16,18},{18,... | collective-permute-start | bytes 1572872 | tf_op jit(solution)/shard_map/ppermute | solution.py:316
  53.9 4.5 %collective-permute-start.17 = (bf16[4,128,512]{2,1,0:T(8,128)(2,1)S(1)}, bf16[4,128,512]{2,1,0:T(8,128)(2,1)S(1)}, u32[]{:S(2)}, u32[]{:S(2)}) collective-permute-start(bf16[4,128,512]{2,1,0:T(8,128)(2,1)S(1)} %pad_maximum_fusion.1), channel_id=1, source_target_pairs={{0,2},{2,0},{4,6},{6,4},{8,10},{10,8},{12,14},{14,12},{16,18},{18,... | collective-permute-start | bytes 1572872 | tf_op jit(solution)/shard_map/ppermute | solution.py:316
  63.7 13.7 %collective-permute-start.18 = (bf16[512,512]{1,0:T(8,128)(2,1)S(1)}, bf16[512,512]{1,0:T(8,128)(2,1)S(1)}, u32[]{:S(2)}, u32[]{:S(2)}) collective-permute-start(bf16[512,512]{1,0:T(8,128)(2,1)S(1)} %get-tuple-element.22), channel_id=1, source_target_pairs={{0,1},{1,0},{2,3},{3,2},{4,5},{5,4},{6,7},{7,6},{8,9},{9,8},{10,11... | collective-permute-start | bytes 1572872 | tf_op jit(solution)/shard_map/ppermute | solution.py:319
  69.5 6.2 %copy-start.4 = (f32[1,128,512]{2,1,0:T(8,128)S(1)}, f32[1,128,512]{2,1,0:T(8,128)}, u32[]{:S(2)}) copy-start(f32[1,128,512]{2,1,0:T(8,128)} %param.10) | copy-start | bytes 786436
  (1 other events, 2.7 us)

commit v5 on v4

--- a/solution.py
+++ b/solution.py
@@ -10,6 +10,7 @@
 
 HEAD = 128
 LINK = jnp.bfloat16
+SHARES = 2
 
 
 def factors_of(count):
@@ -76,9 +77,10 @@
             pltpu.make_async_copy(features_ref.at[:, at], held_ref.at[rows, :], sems.at[0, i])
         )
         outs.append(pltpu.make_async_copy(held_ref.at[rows, :], out_ref.at[rows, :], sems.at[1, i]))
-    for i in range(blocks):
-        wide.append(pltpu.make_async_copy(sums_ref.at[i, core], wide_ref.at[i], sems.at[2, i]))
-        half.append(pltpu.make_async_copy(half_ref.at[i], core_ref.at[i], sems.at[3, i]))
+    chunks = [pl.ds(i * blocks // SHARES, blocks // SHARES) for i in range(SHARES)]
+    for i, at in enumerate(chunks):
+        wide.append(pltpu.make_async_copy(sums_ref.at[at, core], wide_ref.at[at], sems.at[2, i]))
+        half.append(pltpu.make_async_copy(half_ref.at[at], core_ref.at[at], sems.at[3, i]))
     for copy in wide + ins:
         copy.start()
     rows = pl.ds(groups * count, out_ref.shape[0] - groups * count)
@@ -90,9 +92,9 @@
     outs[-1].start()
 
     def move_bands():
-        for i in range(blocks):
+        for i, at in enumerate(chunks):
             wide[i].wait()
-            half_ref[i] = wide_ref[i].astype(half_ref.dtype)
+            half_ref[at] = wide_ref[at].astype(half_ref.dtype)
             half[i].start()
 
     def move_tokens():
@@ -124,7 +126,7 @@
             pltpu.VMEM(shape, features.dtype),
             pltpu.VMEM((blocks, band, columns), sums.dtype),
             pltpu.VMEM((blocks, band, columns), LINK),
-            pltpu.SemaphoreType.DMA((4, max(groups + 1, blocks))),
+            pltpu.SemaphoreType.DMA((4, max(groups + 1, SHARES))),
         ],
         compiler_params=pltpu.CompilerParams(vmem_limit_bytes=60 * 1024 * 1024),
         cost_estimate=CHEAP,

time: 78.6 us -> 78.3 us (level)
  no operation moved by 1% of the time
where the time goes in v5:
time: 78.3 us; the launch traced here: 77.9 us
  starting transfers between devices  30.4 us (39%)
  Pallas kernels  18.1 us (23%)
  waiting for transfers between devices  15.3 us (20%)
  other arithmetic  13 us (17%)
  between operations  0.93 us (1%)
    ppermute x17, starting transfers between devices, moved(): return lax.ppermute(value, 'rep', pairs)  24.2 us
    ppermute x17, waiting for transfers between devices, moved(): return lax.ppermute(value, 'rep', pairs)  13.4 us
    ppermute x3, starting transfers between devices, across(): return lax.ppermute(value, 'fsdp', shift_pairs(pair, 1, pair, step))  6.19 us
    pallas_call x1, Pallas kernels, gradient(): pl.pallas_call(gradient_kernel, grid_spec=pltpu.PrefetchScalarGridSpec(nu...  6.17 us
    pallas_call x1, Pallas kernels, project(): pl.pallas_call(functools.partial(project_kernel, len(bands)), in_specs=[p...  5.28 us
    pallas_call x1, Pallas kernels, pack(): pl.pallas_call(functools.partial(pack_kernel, step, sides), in_specs=[pla...  3.95 us
    convert_element_type x3, other arithmetic, local(): out = total(piece(k, 0) + after(sums[k], last)).astype(LINK)  3.06 us
    pallas_call x1, Pallas kernels, product(): pl.pallas_call(product_kernel, grid_spec=pltpu.PrefetchScalarGridSpec(num...  2.69 us
  transfers between devices with their start and end apart: 20, of which 10 were waited for; matrix products, arithmetic and copies ran while one was open for 16% of the time, Pallas kernels for 18%

profile of v5, /device:TPU:0, one launch (start us, length us, event | category | flops | bytes accessed | tf_op | source)
XLA Modules:
  0.0 77.9 jit_solution(1606093884820225976)
XLA Ops:
  0.6 4.0 %pack.1 = (bf16[2064,512]{1,0:T(8,128)(2,1)}, bf16[8,128,512]{2,1,0:T(8,128)(2,1)}) custom-call(bf16[512,4096]{1,0:T(8,128)(2,1)} %bitcast.128, s32[1,512]{1,0:T(1,128)} %documents_ref.1, f32[8,2,128,512]{3,2,1,0:T(8,128)} %bitcast.133), custom_call_target="tpu_custom_call" | custom-call | tf_op jit(solution)/shard_map/pack/pallas_call | solution.py:117
  5.1 2.6 %collective-permute-start.8 = (bf16[2064,512]{1,0:T(8,128)(2,1)}, bf16[2064,512]{1,0:T(8,128)(2,1)S(1)}, u32[]{:S(2)}, u32[]{:S(2)}) collective-permute-start(bf16[2064,512]{1,0:T(8,128)(2,1)} %get-tuple-element.18), channel_id=1, source_target_pairs={{0,1},{1,0},{2,3},{3,2},{4,5},{5,4},{6,7},{7,6},{8,9},{9,8},{10,11... | collective-permute-start | bytes 6340616 | tf_op jit(solution)/shard_map/ppermute | solution.py:321
  7.7 2.4 %fusion.15 = (bf16[1,128,512]{2,1,0:T(8,128)(2,1)}, bf16[1,128,512]{2,1,0:T(8,128)(2,1)}, bf16[1,128,512]{2,1,0:T(8,128)(2,1)}, bf16[1,128,512]{2,1,0:T(8,128)(2,1)S(1)}) fusion(f32[1,4,2,2,128,512]{5,4,3,2,1,0:T(8,128)} %bitcast.134, s32[]{:T(128)S(6)} %select_n.292, s32[]{:T(128)S(6)} %select_n.283, s32[]{:T(128)S(6)} %select_n.280, ...), kind=kLoop, calls=%fused_computation.39 | loop fusion | flops 786432 | bytes 2097176 | tf_op jit(solution)/shard_map/convert_element_type | solution.py:347
  10.1 2.8 %collective-permute-start.2 = (bf16[1,128,512]{2,1,0:T(8,128)(2,1)}, bf16[1,128,512]{2,1,0:T(8,128)(2,1)}, u32[]{:S(2)}, u32[]{:S(2)}) collective-permute-start(bf16[1,128,512]{2,1,0:T(8,128)(2,1)} %get-tuple-element.30), channel_id=1, source_target_pairs={{0,4},{2,6},{4,0},{6,2},{8,12},{10,14},{12,8},{14,10},{16,20},{18,... | collective-permute-start | bytes 393224 | tf_op jit(solution)/shard_map/ppermute | solution.py:318
  12.9 2.0 %collective-permute-start.4 = (bf16[1,128,512]{2,1,0:T(8,128)(2,1)}, bf16[1,128,512]{2,1,0:T(8,128)(2,1)S(1)}, u32[]{:S(2)}, u32[]{:S(2)}) collective-permute-start(bf16[1,128,512]{2,1,0:T(8,128)(2,1)} %get-tuple-element.29), channel_id=1, source_target_pairs={{0,4},{2,6},{4,0},{6,2},{8,12},{10,14},{12,8},{14,10},{16,20},{18,... | collective-permute-start | bytes 393224 | tf_op jit(solution)/shard_map/ppermute | solution.py:318
  15.0 2.5 %collective-permute-done.2 = bf16[1,128,512]{2,1,0:T(8,128)(2,1)} collective-permute-done((bf16[1,128,512]{2,1,0:T(8,128)(2,1)}, bf16[1,128,512]{2,1,0:T(8,128)(2,1)}, u32[]{:S(2)}, u32[]{:S(2)}) %collective-permute-start.2) | collective-permute-done | bytes 131104 | tf_op jit(solution)/shard_map/ppermute | solution.py:318
  17.5 1.1 %fusion.19 = bf16[1,128,512]{2,1,0:T(8,128)(2,1)S(1)} fusion(bf16[1,128,512]{2,1,0:T(8,128)(2,1)} %collective-permute-done.2, f32[1,4,2,2,128,512]{5,4,3,2,1,0:T(8,128)} %bitcast.135, s32[]{:T(128)S(6)} %select_n.286, s32[]{:T(128)S(6)} %select_n.277, s32[]{:T(128)S(6)} %select_n.280, bf16[1,4,2,128,512]{4,3,2,1,0:T(8,128)(2,1)S(1)} %collective-permute-done), kind=kLoop, calls=%fused_computation.46 | loop fusion | flops 327680 | bytes 655372 | tf_op jit(solution)/shard_map/convert_element_type | solution.py:353
  18.5 3.2 %collective-permute-start.3 = (bf16[1,128,512]{2,1,0:T(8,128)(2,1)S(1)}, bf16[1,128,512]{2,1,0:T(8,128)(2,1)S(1)}, u32[]{:S(2)}, u32[]{:S(2)}) collective-permute-start(bf16[1,128,512]{2,1,0:T(8,128)(2,1)S(1)} %fusion.19), channel_id=1, source_target_pairs={{0,16},{2,18},{4,20},{6,22},{8,24},{10,26},{12,28},{14,30},{16,0},... | collective-permute-start | bytes 393224 | tf_op jit(solution)/shard_map/ppermute | solution.py:318
  21.8 1.2 %collective-permute-done.4 = bf16[1,128,512]{2,1,0:T(8,128)(2,1)S(1)} collective-permute-done((bf16[1,128,512]{2,1,0:T(8,128)(2,1)}, bf16[1,128,512]{2,1,0:T(8,128)(2,1)S(1)}, u32[]{:S(2)}, u32[]{:S(2)}) %collective-permute-start.4) | collective-permute-done | bytes 131104 | tf_op jit(solution)/shard_map/ppermute | solution.py:318
  24.0 2.2 %collective-permute-start.5 = (bf16[1,128,512]{2,1,0:T(8,128)(2,1)S(1)}, bf16[1,128,512]{2,1,0:T(8,128)(2,1)S(1)}, u32[]{:S(2)}, u32[]{:S(2)}) collective-permute-start(bf16[1,128,512]{2,1,0:T(8,128)(2,1)S(1)} %fusion.14), channel_id=1, source_target_pairs={{0,8},{2,10},{4,12},{6,14},{8,16},{10,18},{12,20},{14,22},{16,24},... | collective-permute-start | bytes 393224 | tf_op jit(solution)/shard_map/ppermute | solution.py:318
  27.2 3.0 %collective-permute-start.7 = (bf16[1,128,512]{2,1,0:T(8,128)(2,1)S(1)}, bf16[1,128,512]{2,1,0:T(8,128)(2,1)S(1)}, u32[]{:S(2)}, u32[]{:S(2)}) collective-permute-start(bf16[1,128,512]{2,1,0:T(8,128)(2,1)S(1)} %fusion.12), channel_id=1, source_target_pairs={{0,24},{2,26},{4,28},{6,30},{8,0},{10,2},{12,4},{14,6},{16,8},{18,... | collective-permute-start | bytes 393224 | tf_op jit(solution)/shard_map/ppermute | solution.py:318
  30.2 1.6 %collective-permute-done.5 = bf16[1,128,512]{2,1,0:T(8,128)(2,1)S(1)} collective-permute-done((bf16[1,128,512]{2,1,0:T(8,128)(2,1)S(1)}, bf16[1,128,512]{2,1,0:T(8,128)(2,1)S(1)}, u32[]{:S(2)}, u32[]{:S(2)}) %collective-permute-start.5) | collective-permute-done | bytes 131104 | tf_op jit(solution)/shard_map/ppermute | solution.py:318
  31.8 1.4 %collective-permute-done.7 = bf16[1,128,512]{2,1,0:T(8,128)(2,1)S(1)} collective-permute-done((bf16[1,128,512]{2,1,0:T(8,128)(2,1)S(1)}, bf16[1,128,512]{2,1,0:T(8,128)(2,1)S(1)}, u32[]{:S(2)}, u32[]{:S(2)}) %collective-permute-start.7) | collective-permute-done | bytes 131104 | tf_op jit(solution)/shard_map/ppermute | solution.py:318
  33.2 1.2 %subtract_convert_fusion.refs_0_ = bf16[1,128,512]{2,1,0:T(8,128)(2,1)S(1)} fusion(f32[1,128,512]{2,1,0:T(8,128)} %param.10, bf16[1,128,512]{2,1,0:T(8,128)(2,1)S(1)} %collective-permute-done.7, bf16[1,128,512]{2,1,0:T(8,128)(2,1)S(1)} %collective-permute-done.5, bf16[1,128,512]{2,1,0:T(8,128)(2,1)S(1)} %collective-permute-done.3, ...), kind=kLoop, calls=%fused_computation.52 | loop fusion | flops 1179648 | bytes 1572876 | tf_op jit(solution)/shard_map/convert_element_type | solution.py:371
  34.5 3.8 %collective-permute-start.9 = (bf16[1,128,512]{2,1,0:T(8,128)(2,1)S(1)}, bf16[1,128,512]{2,1,0:T(8,128)(2,1)S(1)}, u32[]{:S(2)}, u32[]{:S(2)}) collective-permute-start(bf16[1,128,512]{2,1,0:T(8,128)(2,1)S(1)} %subtract_convert_fusion.refs_0_), channel_id=1, source_target_pairs={{0,24},{2,26},{4,28},{6,30},{8,0},{10,2},{12,4},{14,6},{16,8},{18,... | collective-permute-start | bytes 393224 | tf_op jit(solution)/shard_map/ppermute | solution.py:318
  38.9 1.5 %collective-permute-start.13 = (bf16[1,128,512]{2,1,0:T(8,128)(2,1)S(1)}, bf16[1,128,512]{2,1,0:T(8,128)(2,1)S(1)}, u32[]{:S(2)}, u32[]{:S(2)}) collective-permute-start(bf16[1,128,512]{2,1,0:T(8,128)(2,1)S(1)} %subtract_convert_fusion.refs_0_), channel_id=1, source_target_pairs={{0,4},{2,6},{4,0},{6,2},{8,12},{10,14},{12,8},{14,10},{16,20},{18,... | collective-permute-start | bytes 393224 | tf_op jit(solution)/shard_map/ppermute | solution.py:318
  40.4 1.8 %collective-permute-done.9.refs_1_ = bf16[1,128,512]{2,1,0:T(8,128)(2,1)S(1)} collective-permute-done((bf16[1,128,512]{2,1,0:T(8,128)(2,1)S(1)}, bf16[1,128,512]{2,1,0:T(8,128)(2,1)S(1)}, u32[]{:S(2)}, u32[]{:S(2)}) %collective-permute-start.9) | collective-permute-done | bytes 131104 | tf_op jit(solution)/shard_map/ppermute | solution.py:318
  42.2 1.4 %collective-permute-start.14 = (bf16[1,128,512]{2,1,0:T(8,128)(2,1)S(1)}, bf16[1,128,512]{2,1,0:T(8,128)(2,1)S(1)}, u32[]{:S(2)}, u32[]{:S(2)}) collective-permute-start(bf16[1,128,512]{2,1,0:T(8,128)(2,1)S(1)} %collective-permute-done.9.refs_1_), channel_id=1, source_target_pairs={{0,4},{2,6},{4,0},{6,2},{8,12},{10,14},{12,8},{14,10},{16,20},{18,... | collective-permute-start | bytes 393224 | tf_op jit(solution)/shard_map/ppermute | solution.py:318
  43.7 1.8 %collective-permute-done.10.refs_2_ = bf16[1,128,512]{2,1,0:T(8,128)(2,1)S(1)} collective-permute-done((bf16[1,128,512]{2,1,0:T(8,128)(2,1)S(1)}, bf16[1,128,512]{2,1,0:T(8,128)(2,1)S(1)}, u32[]{:S(2)}, u32[]{:S(2)}) %collective-permute-start.10) | collective-permute-done | bytes 131104 | tf_op jit(solution)/shard_map/ppermute | solution.py:318
  45.5 1.5 %collective-permute-start.15 = (bf16[1,128,512]{2,1,0:T(8,128)(2,1)S(1)}, bf16[1,128,512]{2,1,0:T(8,128)(2,1)S(1)}, u32[]{:S(2)}, u32[]{:S(2)}) collective-permute-start(bf16[1,128,512]{2,1,0:T(8,128)(2,1)S(1)} %collective-permute-done.10.refs_2_), channel_id=1, source_target_pairs={{0,4},{2,6},{4,0},{6,2},{8,12},{10,14},{12,8},{14,10},{16,20},{18,... | collective-permute-start | bytes 393224 | tf_op jit(solution)/shard_map/ppermute | solution.py:318
  47.0 1.5 %collective-permute-done.11.refs_3_ = bf16[1,128,512]{2,1,0:T(8,128)(2,1)S(1)} collective-permute-done((bf16[1,128,512]{2,1,0:T(8,128)(2,1)S(1)}, bf16[1,128,512]{2,1,0:T(8,128)(2,1)S(1)}, u32[]{:S(2)}, u32[]{:S(2)}) %collective-permute-start.11) | collective-permute-done | bytes 131104 | tf_op jit(solution)/shard_map/ppermute | solution.py:318
  48.5 1.5 %collective-permute-start.16 = (bf16[1,128,512]{2,1,0:T(8,128)(2,1)S(1)}, bf16[1,128,512]{2,1,0:T(8,128)(2,1)S(1)}, u32[]{:S(2)}, u32[]{:S(2)}) collective-permute-start(bf16[1,128,512]{2,1,0:T(8,128)(2,1)S(1)} %collective-permute-done.11.refs_3_), channel_id=1, source_target_pairs={{0,4},{2,6},{4,0},{6,2},{8,12},{10,14},{12,8},{14,10},{16,20},{18,... | collective-permute-start | bytes 393224 | tf_op jit(solution)/shard_map/ppermute | solution.py:318
  50.2 1.6 %collective-permute-start.19 = (bf16[512,512]{1,0:T(8,128)(2,1)}, bf16[512,512]{1,0:T(8,128)(2,1)S(1)}, u32[]{:S(2)}, u32[]{:S(2)}) collective-permute-start(bf16[512,512]{1,0:T(8,128)(2,1)} %bitcast.131), channel_id=1, source_target_pairs={{0,1},{1,0},{2,3},{3,2},{4,5},{5,4},{6,7},{7,6},{8,9},{9,8},{10,11... | collective-permute-start | bytes 1572872 | tf_op jit(solution)/shard_map/ppermute | solution.py:321
  51.8 1.6 %collective-permute-done.16.refs_8_ = bf16[1,128,512]{2,1,0:T(8,128)(2,1)S(1)} collective-permute-done((bf16[1,128,512]{2,1,0:T(8,128)(2,1)S(1)}, bf16[1,128,512]{2,1,0:T(8,128)(2,1)S(1)}, u32[]{:S(2)}, u32[]{:S(2)}) %collective-permute-start.16) | collective-permute-done | bytes 131104 | tf_op jit(solution)/shard_map/ppermute | solution.py:318
  53.6 1.2 %collective-permute-done.8.part_ref.refs_0_ = bf16[2064,512]{1,0:T(8,128)(2,1)S(1)} collective-permute-done((bf16[2064,512]{1,0:T(8,128)(2,1)}, bf16[2064,512]{1,0:T(8,128)(2,1)S(1)}, u32[]{:S(2)}, u32[]{:S(2)}) %collective-permute-start.8) | collective-permute-done | bytes 2113568 | tf_op jit(solution)/shard_map/ppermute | solution.py:321
  54.8 1.3 %convert_reduce_fusion = (s32[512]{0:T(512)S(1)}, s32[512]{0:T(512)S(1)}, s32[512]{0:T(512)S(1)}, s32[512]{0:T(512)S(1)}) fusion(s32[512]{0:T(512)S(1)} %bitcast.142, s32[512]{0:T(512)} %bitcast.141), kind=kLoop, calls=%fused_computation.1 | loop fusion | flops 3143680 | bytes 12288 | tf_op jit(solution)/shard_map/reduce_sum | solution.py:408
  56.1 1.9 %fusion.10 = (f32[512,128]{1,0:T(8,128)S(1)}, f32[512,128]{1,0:T(8,128)S(1)}, f32[512,128]{1,0:T(8,128)S(1)}, f32[512,128]{1,0:T(8,128)S(1)}) fusion(f32[512]{0:T(512)S(1)} %get-tuple-element.40, f32[128]{0:T(128)S(1)} %get-tuple-element.42, f32[128]{0:T(128)S(1)} %get-tuple-element.43, f32[512]{0:T(512)S(1)} %get-tuple-element.41), kind=kLoop, calls=%fused_computation.31 | loop fusion | flops 262144 | bytes 1053696 | tf_op jit(solution)/shard_map/mul | solution.py:45
  58.0 5.3 %project.1 = (bf16[512,512]{1,0:T(8,128)(2,1)S(1)}, bf16[2048,512]{1,0:T(8,128)(2,1)S(1)}) custom-call(s32[16]{0:T(128)S(1)} %stack.67.place_ref, bf16[2064,512]{1,0:T(8,128)(2,1)S(1)} %collective-permute-done.8.part_ref.refs_0_, f32[512,128]{1,0:T(8,128)S(1)} %get-tuple-element.38.cosine_ref.refs_2_, f32[512,128]{1,0:T(8,128)S(1)} %get-tuple-element.39.sine_ref.refs_3_, ...), custom_call_target="tpu_custom_call" | custom-call | tf_op jit(solution)/shard_map/project/pallas_call | solution.py:284
  63.3 2.0 %collective-permute-start.18 = (bf16[512,512]{1,0:T(8,128)(2,1)S(1)}, bf16[512,512]{1,0:T(8,128)(2,1)S(1)}, u32[]{:S(2)}, u32[]{:S(2)}) collective-permute-start(bf16[512,512]{1,0:T(8,128)(2,1)S(1)} %get-tuple-element.22), channel_id=1, source_target_pairs={{0,1},{1,0},{2,3},{3,2},{4,5},{5,4},{6,7},{7,6},{8,9},{9,8},{10,11... | collective-permute-start | bytes 1572872 | tf_op jit(solution)/shard_map/ppermute | solution.py:321
  65.3 1.1 %fusion.6 = f32[128,512]{1,0:T(8,128)S(1)} fusion(bf16[1,128,512]{2,1,0:T(8,128)(2,1)S(1)} %copy-done.6, bf16[1,128,512]{2,1,0:T(8,128)(2,1)S(1)} %copy-done.8, bf16[1,128,512]{2,1,0:T(8,128)(2,1)S(1)} %copy-done.10, bf16[1,128,512]{2,1,0:T(8,128)(2,1)S(1)} %copy-done.12, f32[1,4,2,2,128,512]{5,4,3,2,1,0:T(8,128)} %bitcast.139, s32[]{:T(128)S(6)} %select_n.272, ...), kind=kLoop, calls=%fused_computation.27 | loop fusion | flops 720896 | bytes 1179660 | tf_op jit(solution)/shard_map/div | solution.py:369
  66.5 2.7 %product.1 = f32[512,512]{1,0:T(8,128)S(1)} custom-call(s32[1]{0:T(128)} %bitcast.48.side_ref, bf16[512,4096]{1,0:T(8,128)(2,1)S(1)} %bitcast.129, bf16[2048,512]{1,0:T(8,128)(2,1)S(1)} %get-tuple-element.19.weights_ref, f32[512,128]{1,0:T(8,128)S(1)} %get-tuple-element.35.cosine_ref, f32[512,128]{1,0:T(8,128)S(1)} %get-tuple-element.34.sine_ref), custom_call_target="tpu_custom_call" | custom-call | tf_op jit(solution)/shard_map/product/pallas_call | solution.py:227
  69.2 6.2 %gradient.1 = bf16[2048,512]{1,0:T(8,128)(2,1)} custom-call(s32[1]{0:T(128)} %bitcast.48.side_ref, bf16[512,4096]{1,0:T(8,128)(2,1)S(1)} %bitcast.130, bf16[512,512]{1,0:T(8,128)(2,1)S(1)} %bitcast.132, f32[512,128]{1,0:T(8,128)S(1)} %get-tuple-element.35.cosine_ref, f32[512,128]{1,0:T(8,128)S(1)} %get-tuple-element.34.sine_ref, ...), custom_call_target="tpu_custom_call" | custom-call | tf_op jit(solution)/shard_map/gradient/pallas_call | solution.py:177
  (54 shorter events, 6.2 us)
Async XLA Ops:
  4.6 28.6 %copy-start.3 = (f32[1,128,512]{2,1,0:T(8,128)S(1)}, f32[1,128,512]{2,1,0:T(8,128)}, u32[]{:S(2)}) copy-start(f32[1,128,512]{2,1,0:T(8,128)} %param.11) | copy-start | bytes 786436
  4.6 3.1 %collective-permute-start = (bf16[1,4,2,128,512]{4,3,2,1,0:T(8,128)(2,1)}, bf16[1,4,2,128,512]{4,3,2,1,0:T(8,128)(2,1)S(1)}, u32[]{:S(2)}, u32[]{:S(2)}) collective-permute-start(bf16[1,4,2,128,512]{4,3,2,1,0:T(8,128)(2,1)} %bitcast.143), channel_id=1, source_target_pairs={{0,2},{2,0},{4,6},{6,4},{8,10},{10,8},{12,14},{14,12},{16,18},{18,... | collective-permute-start | bytes 3145736 | tf_op jit(solution)/shard_map/ppermute | solution.py:318
  5.1 49.6 %collective-permute-start.8 = (bf16[2064,512]{1,0:T(8,128)(2,1)}, bf16[2064,512]{1,0:T(8,128)(2,1)S(1)}, u32[]{:S(2)}, u32[]{:S(2)}) collective-permute-start(bf16[2064,512]{1,0:T(8,128)(2,1)} %get-tuple-element.18), channel_id=1, source_target_pairs={{0,1},{1,0},{2,3},{3,2},{4,5},{5,4},{6,7},{7,6},{8,9},{9,8},{10,11... | collective-permute-start | bytes 6340616 | tf_op jit(solution)/shard_map/ppermute | solution.py:321
  7.7 25.5 %copy-start.2 = (bf16[1,4,2,128,512]{4,3,2,1,0:T(8,128)(2,1)}, bf16[1,4,2,128,512]{4,3,2,1,0:T(8,128)(2,1)S(1)}, u32[]{:S(2)}) copy-start(bf16[1,4,2,128,512]{4,3,2,1,0:T(8,128)(2,1)S(1)} %collective-permute-done) | copy-start | bytes 3145732
  10.1 7.4 %collective-permute-start.2 = (bf16[1,128,512]{2,1,0:T(8,128)(2,1)}, bf16[1,128,512]{2,1,0:T(8,128)(2,1)}, u32[]{:S(2)}, u32[]{:S(2)}) collective-permute-start(bf16[1,128,512]{2,1,0:T(8,128)(2,1)} %get-tuple-element.30), channel_id=1, source_target_pairs={{0,4},{2,6},{4,0},{6,2},{8,12},{10,14},{12,8},{14,10},{16,20},{18,... | collective-permute-start | bytes 393224 | tf_op jit(solution)/shard_map/ppermute | solution.py:318
  12.9 17.3 %collective-permute-start.1 = (bf16[1,128,512]{2,1,0:T(8,128)(2,1)S(1)}, bf16[1,128,512]{2,1,0:T(8,128)(2,1)S(1)}, u32[]{:S(2)}, u32[]{:S(2)}) collective-permute-start(bf16[1,128,512]{2,1,0:T(8,128)(2,1)S(1)} %get-tuple-element.31), channel_id=1, source_target_pairs={{0,4},{2,6},{4,0},{6,2},{8,12},{10,14},{12,8},{14,10},{16,20},{18,... | collective-permute-start | bytes 393224 | tf_op jit(solution)/shard_map/ppermute | solution.py:318
  12.9 10.1 %collective-permute-start.4 = (bf16[1,128,512]{2,1,0:T(8,128)(2,1)}, bf16[1,128,512]{2,1,0:T(8,128)(2,1)S(1)}, u32[]{:S(2)}, u32[]{:S(2)}) collective-permute-start(bf16[1,128,512]{2,1,0:T(8,128)(2,1)} %get-tuple-element.29), channel_id=1, source_target_pairs={{0,4},{2,6},{4,0},{6,2},{8,12},{10,14},{12,8},{14,10},{16,20},{18,... | collective-permute-start | bytes 393224 | tf_op jit(solution)/shard_map/ppermute | solution.py:318
  14.9 11.3 %collective-permute-start.6 = (bf16[1,128,512]{2,1,0:T(8,128)(2,1)}, bf16[1,128,512]{2,1,0:T(8,128)(2,1)S(1)}, u32[]{:S(2)}, u32[]{:S(2)}) collective-permute-start(bf16[1,128,512]{2,1,0:T(8,128)(2,1)} %get-tuple-element.28), channel_id=1, source_target_pairs={{0,4},{2,6},{4,0},{6,2},{8,12},{10,14},{12,8},{14,10},{16,20},{18,... | collective-permute-start | bytes 393224 | tf_op jit(solution)/shard_map/ppermute | solution.py:318
  18.5 11.7 %collective-permute-start.3 = (bf16[1,128,512]{2,1,0:T(8,128)(2,1)S(1)}, bf16[1,128,512]{2,1,0:T(8,128)(2,1)S(1)}, u32[]{:S(2)}, u32[]{:S(2)}) collective-permute-start(bf16[1,128,512]{2,1,0:T(8,128)(2,1)S(1)} %fusion.19), channel_id=1, source_target_pairs={{0,16},{2,18},{4,20},{6,22},{8,24},{10,26},{12,28},{14,30},{16,0},... | collective-permute-start | bytes 393224 | tf_op jit(solution)/shard_map/ppermute | solution.py:318
  24.0 7.8 %collective-permute-start.5 = (bf16[1,128,512]{2,1,0:T(8,128)(2,1)S(1)}, bf16[1,128,512]{2,1,0:T(8,128)(2,1)S(1)}, u32[]{:S(2)}, u32[]{:S(2)}) collective-permute-start(bf16[1,128,512]{2,1,0:T(8,128)(2,1)S(1)} %fusion.14), channel_id=1, source_target_pairs={{0,8},{2,10},{4,12},{6,14},{8,16},{10,18},{12,20},{14,22},{16,24},... | collective-permute-start | bytes 393224 | tf_op jit(solution)/shard_map/ppermute | solution.py:318
  27.2 6.0 %collective-permute-start.7 = (bf16[1,128,512]{2,1,0:T(8,128)(2,1)S(1)}, bf16[1,128,512]{2,1,0:T(8,128)(2,1)S(1)}, u32[]{:S(2)}, u32[]{:S(2)}) collective-permute-start(bf16[1,128,512]{2,1,0:T(8,128)(2,1)S(1)} %fusion.12), channel_id=1, source_target_pairs={{0,24},{2,26},{4,28},{6,30},{8,0},{10,2},{12,4},{14,6},{16,8},{18,... | collective-permute-start | bytes 393224 | tf_op jit(solution)/shard_map/ppermute | solution.py:318
  30.2 18.2 %copy-start.5 = (bf16[1,128,512]{2,1,0:T(8,128)(2,1)}, bf16[1,128,512]{2,1,0:T(8,128)(2,1)S(1)}, u32[]{:S(2)}) copy-start(bf16[1,128,512]{2,1,0:T(8,128)(2,1)S(1)} %collective-permute-done.1) | copy-start | bytes 393220
  30.2 19.7 %copy-start.7 = (bf16[1,128,512]{2,1,0:T(8,128)(2,1)}, bf16[1,128,512]{2,1,0:T(8,128)(2,1)S(1)}, u32[]{:S(2)}) copy-start(bf16[1,128,512]{2,1,0:T(8,128)(2,1)S(1)} %collective-permute-done.3) | copy-start | bytes 393220
  31.8 18.1 %copy-start.9 = (bf16[1,128,512]{2,1,0:T(8,128)(2,1)}, bf16[1,128,512]{2,1,0:T(8,128)(2,1)S(1)}, u32[]{:S(2)}) copy-start(bf16[1,128,512]{2,1,0:T(8,128)(2,1)S(1)} %collective-permute-done.5) | copy-start | bytes 393220
  33.2 16.7 %copy-start.11 = (bf16[1,128,512]{2,1,0:T(8,128)(2,1)}, bf16[1,128,512]{2,1,0:T(8,128)(2,1)S(1)}, u32[]{:S(2)}) copy-start(bf16[1,128,512]{2,1,0:T(8,128)(2,1)S(1)} %collective-permute-done.7) | copy-start | bytes 393220
  34.5 7.8 %collective-permute-start.9 = (bf16[1,128,512]{2,1,0:T(8,128)(2,1)S(1)}, bf16[1,128,512]{2,1,0:T(8,128)(2,1)S(1)}, u32[]{:S(2)}, u32[]{:S(2)}) collective-permute-start(bf16[1,128,512]{2,1,0:T(8,128)(2,1)S(1)} %subtract_convert_fusion.refs_0_), channel_id=1, source_target_pairs={{0,24},{2,26},{4,28},{6,30},{8,0},{10,2},{12,4},{14,6},{16,8},{18,... | collective-permute-start | bytes 393224 | tf_op jit(solution)/shard_map/ppermute | solution.py:318
  38.3 7.2 %collective-permute-start.10 = (bf16[1,128,512]{2,1,0:T(8,128)(2,1)S(1)}, bf16[1,128,512]{2,1,0:T(8,128)(2,1)S(1)}, u32[]{:S(2)}, u32[]{:S(2)}) collective-permute-start(bf16[1,128,512]{2,1,0:T(8,128)(2,1)S(1)} %subtract_convert_fusion.refs_0_), channel_id=1, source_target_pairs={{0,8},{2,10},{4,12},{6,14},{8,16},{10,18},{12,20},{14,22},{16,24},... | collective-permute-start | bytes 393224 | tf_op jit(solution)/shard_map/ppermute | solution.py:318
  38.3 10.2 %collective-permute-start.11 = (bf16[1,128,512]{2,1,0:T(8,128)(2,1)S(1)}, bf16[1,128,512]{2,1,0:T(8,128)(2,1)S(1)}, u32[]{:S(2)}, u32[]{:S(2)}) collective-permute-start(bf16[1,128,512]{2,1,0:T(8,128)(2,1)S(1)} %subtract_convert_fusion.refs_0_), channel_id=1, source_target_pairs={{0,16},{2,18},{4,20},{6,22},{8,24},{10,26},{12,28},{14,30},{16,0},... | collective-permute-start | bytes 393224 | tf_op jit(solution)/shard_map/ppermute | solution.py:318
  38.9 11.3 %collective-permute-start.13 = (bf16[1,128,512]{2,1,0:T(8,128)(2,1)S(1)}, bf16[1,128,512]{2,1,0:T(8,128)(2,1)S(1)}, u32[]{:S(2)}, u32[]{:S(2)}) collective-permute-start(bf16[1,128,512]{2,1,0:T(8,128)(2,1)S(1)} %subtract_convert_fusion.refs_0_), channel_id=1, source_target_pairs={{0,4},{2,6},{4,0},{6,2},{8,12},{10,14},{12,8},{14,10},{16,20},{18,... | collective-permute-start | bytes 393224 | tf_op jit(solution)/shard_map/ppermute | solution.py:318
  42.2 9.6 %collective-permute-start.14 = (bf16[1,128,512]{2,1,0:T(8,128)(2,1)S(1)}, bf16[1,128,512]{2,1,0:T(8,128)(2,1)S(1)}, u32[]{:S(2)}, u32[]{:S(2)}) collective-permute-start(bf16[1,128,512]{2,1,0:T(8,128)(2,1)S(1)} %collective-permute-done.9.refs_1_), channel_id=1, source_target_pairs={{0,4},{2,6},{4,0},{6,2},{8,12},{10,14},{12,8},{14,10},{16,20},{18,... | collective-permute-start | bytes 393224 | tf_op jit(solution)/shard_map/ppermute | solution.py:318
  45.5 6.4 %collective-permute-start.15 = (bf16[1,128,512]{2,1,0:T(8,128)(2,1)S(1)}, bf16[1,128,512]{2,1,0:T(8,128)(2,1)S(1)}, u32[]{:S(2)}, u32[]{:S(2)}) collective-permute-start(bf16[1,128,512]{2,1,0:T(8,128)(2,1)S(1)} %collective-permute-done.10.refs_2_), channel_id=1, source_target_pairs={{0,4},{2,6},{4,0},{6,2},{8,12},{10,14},{12,8},{14,10},{16,20},{18,... | collective-permute-start | bytes 393224 | tf_op jit(solution)/shard_map/ppermute | solution.py:318
  48.5 5.0 %collective-permute-start.16 = (bf16[1,128,512]{2,1,0:T(8,128)(2,1)S(1)}, bf16[1,128,512]{2,1,0:T(8,128)(2,1)S(1)}, u32[]{:S(2)}, u32[]{:S(2)}) collective-permute-start(bf16[1,128,512]{2,1,0:T(8,128)(2,1)S(1)} %collective-permute-done.11.refs_3_), channel_id=1, source_target_pairs={{0,4},{2,6},{4,0},{6,2},{8,12},{10,14},{12,8},{14,10},{16,20},{18,... | collective-permute-start | bytes 393224 | tf_op jit(solution)/shard_map/ppermute | solution.py:318
  50.1 15.2 %copy-start.6 = (bf16[1,128,512]{2,1,0:T(8,128)(2,1)S(1)}, bf16[1,128,512]{2,1,0:T(8,128)(2,1)}, u32[]{:S(2)}) copy-start(bf16[1,128,512]{2,1,0:T(8,128)(2,1)} %copy-done.5) | copy-start | bytes 393220
  50.1 15.2 %copy-start.8 = (bf16[1,128,512]{2,1,0:T(8,128)(2,1)S(1)}, bf16[1,128,512]{2,1,0:T(8,128)(2,1)}, u32[]{:S(2)}) copy-start(bf16[1,128,512]{2,1,0:T(8,128)(2,1)} %copy-done.7) | copy-start | bytes 393220
  50.1 15.2 %copy-start.10 = (bf16[1,128,512]{2,1,0:T(8,128)(2,1)S(1)}, bf16[1,128,512]{2,1,0:T(8,128)(2,1)}, u32[]{:S(2)}) copy-start(bf16[1,128,512]{2,1,0:T(8,128)(2,1)} %copy-done.9) | copy-start | bytes 393220
  50.1 15.2 %copy-start.12 = (bf16[1,128,512]{2,1,0:T(8,128)(2,1)S(1)}, bf16[1,128,512]{2,1,0:T(8,128)(2,1)}, u32[]{:S(2)}) copy-start(bf16[1,128,512]{2,1,0:T(8,128)(2,1)} %copy-done.11) | copy-start | bytes 393220
  50.2 16.2 %copy-start = (bf16[1,512,4096]{2,1,0:T(8,128)(2,1)S(1)}, bf16[1,512,4096]{2,1,0:T(8,128)(2,1)}, u32[]{:S(2)}) copy-start(bf16[1,512,4096]{2,1,0:T(8,128)(2,1)} %param.6) | copy-start | bytes 12582916
  50.2 18.9 %collective-permute-start.19 = (bf16[512,512]{1,0:T(8,128)(2,1)}, bf16[512,512]{1,0:T(8,128)(2,1)S(1)}, u32[]{:S(2)}, u32[]{:S(2)}) collective-permute-start(bf16[512,512]{1,0:T(8,128)(2,1)} %bitcast.131), channel_id=1, source_target_pairs={{0,1},{1,0},{2,3},{3,2},{4,5},{5,4},{6,7},{7,6},{8,9},{9,8},{10,11... | collective-permute-start | bytes 1572872 | tf_op jit(solution)/shard_map/ppermute | solution.py:321
  51.8 6.2 %collective-permute-start.12 = (bf16[4,128,512]{2,1,0:T(8,128)(2,1)S(1)}, bf16[4,128,512]{2,1,0:T(8,128)(2,1)S(1)}, u32[]{:S(2)}, u32[]{:S(2)}) collective-permute-start(bf16[4,128,512]{2,1,0:T(8,128)(2,1)S(1)} %pad_maximum_fusion), channel_id=1, source_target_pairs={{0,2},{2,0},{4,6},{6,4},{8,10},{10,8},{12,14},{14,12},{16,18},{18,... | collective-permute-start | bytes 1572872 | tf_op jit(solution)/shard_map/ppermute | solution.py:318
  53.5 4.5 %collective-permute-start.17 = (bf16[4,128,512]{2,1,0:T(8,128)(2,1)S(1)}, bf16[4,128,512]{2,1,0:T(8,128)(2,1)S(1)}, u32[]{:S(2)}, u32[]{:S(2)}) collective-permute-start(bf16[4,128,512]{2,1,0:T(8,128)(2,1)S(1)} %pad_maximum_fusion.1), channel_id=1, source_target_pairs={{0,2},{2,0},{4,6},{6,4},{8,10},{10,8},{12,14},{14,12},{16,18},{18,... | collective-permute-start | bytes 1572872 | tf_op jit(solution)/shard_map/ppermute | solution.py:318
  63.3 13.7 %collective-permute-start.18 = (bf16[512,512]{1,0:T(8,128)(2,1)S(1)}, bf16[512,512]{1,0:T(8,128)(2,1)S(1)}, u32[]{:S(2)}, u32[]{:S(2)}) collective-permute-start(bf16[512,512]{1,0:T(8,128)(2,1)S(1)} %get-tuple-element.22), channel_id=1, source_target_pairs={{0,1},{1,0},{2,3},{3,2},{4,5},{5,4},{6,7},{7,6},{8,9},{9,8},{10,11... | collective-permute-start | bytes 1572872 | tf_op jit(solution)/shard_map/ppermute | solution.py:321
  69.2 6.2 %copy-start.4 = (f32[1,128,512]{2,1,0:T(8,128)S(1)}, f32[1,128,512]{2,1,0:T(8,128)}, u32[]{:S(2)}) copy-start(f32[1,128,512]{2,1,0:T(8,128)} %param.10) | copy-start | bytes 786436
  (1 other events, 2.7 us)
